TPU v7x, 32 devices: a whole 2x2x4 slice. The times are simulated.
32 devices in a mesh: gx: 2 (over y), gy: 4 (over z), gz: 4 (over x, core).
Axes of the slice: x: 2, y: 2, z: 4, core: 2. Of those that a mesh axis runs over, the one named last changes fastest.
Arguments:
- adjoint: float32 [1024, 1715], P(('gx', 'gy', 'gz')), may hold values from -6 to 6
- order: int32 [1024], P(('gx', 'gy', 'gz')), may hold values from 2 to 6
- mortar_trace: float32 [3072, 245], P(('gx', 'gy', 'gz')), may hold values from -6 to 6
- mortar_sub: int32 [3072], P(('gx', 'gy', 'gz')), may hold values from 0 to 3
- mortar_dest: int32 [3072, 1], P(('gx', 'gy', 'gz')), may hold values from 0 to 7; in each aligned block of 96 rows (0 to 95, 96 to 191, ...) at most 24 rows name the same one
- mortar_elem: int32 [3072], P(('gx', 'gy', 'gz')), may hold values from 0 to 31
- mortar_face: int32 [3072], P(('gx', 'gy', 'gz')), may hold values from 0 to 5
- conf_trace: float32 [2048, 245], P(('gx', 'gy', 'gz')), may hold values from -6 to 6
- conf_elem: int32 [2048], P(('gx', 'gy', 'gz')), may hold values from 0 to 31
- conf_face: int32 [2048], P(('gx', 'gy', 'gz')), may hold values from 0 to 5
- coarse_row: int32 [1024], P(('gx', 'gy', 'gz')), may hold values from 0 to 255, as said below
Outputs:
- coarse_rows: float32 [1024, 1080], P(('gx', 'gy', 'gz'))
Inputs may be any that keep to these rules, and one draw needn't show every extreme that they name: `mortar_dest`: in each aligned block of 96 rows (one device) no value appears more than 24 times. `coarse_row`: within each gz layer the values of all its devices form a permutation; each device sends either exactly 4 or no rows to each device of its layer.
All inputs are finite; a program needn't handle non-finite values.
Results may differ from a plain program's by a relative error of at most 0.0003.
Values sent between devices are 32-bit elements; how exact they have to be, the bound alone decides.
No kernel may reach another device: no remote copies, remote signals or barrier semaphores. Data moves between devices by JAX's collectives and lax.ppermute only.
A program may use at most 192 MiB of HBM per device.

v0:
```python
import functools

import jax
import jax.numpy as jnp
import ml_dtypes
import numpy as np
from jax import lax
from jax.experimental import pallas as pl
from jax.experimental.pallas import tpu as pltpu
from jax.sharding import PartitionSpec as P

VARS = 5
NODE = 7
FACE = NODE * NODE
CELL = NODE * FACE
ROW = 216
FACES = 6
ORDERS = (2, 3, 4, 5, 6)
TRACE = VARS * FACE
LANES = 256
TAG_FACE = TRACE
TAG_ROW = TRACE + 1
CELL_PAD = 384
FACE_PAD = 64


def grid_nodes(degree):
    return -np.cos(np.pi * np.arange(degree + 1) / degree)


def lagrange_rows(degree, points):
    anchors = grid_nodes(degree)
    values = np.ones((len(points), degree + 1))
    for k in range(degree + 1):
        for other in range(degree + 1):
            if other != k:
                values[:, k] *= (points - anchors[other]) / (anchors[k] - anchors[other])
    return values


def split_table(table):
    table = np.asarray(table, np.float32)
    high = table.astype(ml_dtypes.bfloat16)
    low = (table - high.astype(np.float32)).astype(ml_dtypes.bfloat16)
    return high, low


@functools.lru_cache(maxsize=None)
def basis_tables():
    top_nodes = grid_nodes(6)
    mortar = [lagrange_rows(6, (top_nodes - 1.0) / 2.0), lagrange_rows(6, (top_nodes + 1.0) / 2.0)]
    lift = np.zeros((4, LANES, LANES))
    for sub in range(4):
        both = np.kron(mortar[sub // 2], mortar[sub % 2])
        for v in range(VARS):
            part = slice(v * FACE, (v + 1) * FACE)
            lift[sub, part, part] = both
    cell = np.zeros((len(ORDERS), CELL_PAD, ROW))
    face = np.zeros((len(ORDERS), FACES, FACE_PAD, ROW))
    for index, p in enumerate(ORDERS):
        shrink = np.zeros((6, NODE))
        shrink[:p, : p + 1] = lagrange_rows(p - 1, grid_nodes(p)).T
        reduce = np.zeros((NODE, NODE))
        reduce[: p + 1, :] = lagrange_rows(p, top_nodes).T
        cell[index, :CELL] = np.einsum("ai,bj,ck->ijkabc", shrink, shrink, shrink).reshape(CELL, ROW)
        flat = shrink @ reduce
        low, high = shrink[:, 0], shrink[:, p]
        for axis, spec in enumerate(("c,ai,bj->ijcab", "c,ai,bj->ijacb", "c,ai,bj->ijabc")):
            for side, edge in enumerate((low, high)):
                face[index, 2 * axis + side, :FACE] = np.einsum(spec, edge, flat, flat).reshape(FACE, ROW)
    return (
        split_table(lift.reshape(4 * LANES, LANES)),
        split_table(cell.reshape(-1, ROW)),
        split_table(face.reshape(-1, ROW)),
    )


def iota(shape, axis):
    return lax.broadcasted_iota(jnp.int32, shape, axis)


def halves(x):
    high = x.astype(jnp.bfloat16)
    low = (x - high.astype(jnp.float32)).astype(jnp.bfloat16)
    return high, low


def dot(a, b):
    return jnp.dot(a, b, preferred_element_type=jnp.float32)


def dot3(high, low, table_high, table_low):
    return dot(high, table_high) + dot(low, table_high) + dot(high, table_low)


def earlier(member):
    count = member.shape[1]
    before = (iota((count, count), 0) < iota((count, count), 1)).astype(jnp.float32)
    return dot(member.astype(jnp.bfloat16), before.astype(jnp.bfloat16))


def owner_of(crow, peers, elements):
    first = iota((peers, crow.shape[1]), 0) * elements
    return ((crow >= first) & (crow < first + elements)).astype(jnp.float32)


def row_places(crow, peers, elements, stride):
    member = owner_of(crow, peers, elements)
    rank = earlier(member)
    base = iota(member.shape, 0).astype(jnp.float32)
    place = jnp.sum(member * (base * stride + rank), axis=0, keepdims=True)
    slot = crow.astype(jnp.float32) - jnp.sum(member * (base * elements), axis=0, keepdims=True)
    return place, slot


def onehot_rows(place, rows):
    return (iota((rows, place.shape[1]), 0).astype(jnp.float32) == place).astype(jnp.float32)


def column(onehot, values):
    return jnp.sum(onehot * values, axis=1, keepdims=True)


def pack_kernel(
    peers,
    cap,
    elements,
    trace,
    sub,
    dest,
    elem,
    face,
    crow,
    ctrace,
    celem,
    cface,
    lift_high,
    lift_low,
    out,
    conf_out,
):
    count = trace.shape[0]
    rows = peers * cap
    member = (iota((peers, count), 0) == dest[...]).astype(jnp.float32)
    base = iota(member.shape, 0).astype(jnp.float32) * cap
    place = jnp.sum(member * (base + earlier(member)), axis=0, keepdims=True)
    put = onehot_rows(place, rows)
    code = (face[...] * elements + elem[...] + 1).astype(jnp.float32)
    code_col = column(put, code)
    row_place, row_slot = row_places(crow[...], peers, elements, cap)
    row_col = column(onehot_rows(row_place, rows), row_slot + 1.0)
    eye = (iota((count, count), 0) == iota((count, count), 1)).astype(jnp.float32)
    sub_col = column(eye, sub[...].astype(jnp.float32))
    x = jnp.concatenate([trace[...], jnp.zeros((count, LANES - TRACE), jnp.float32)], axis=1)
    wide = jnp.concatenate([jnp.where(sub_col == float(s), x, 0.0) for s in range(4)], axis=1)
    high, low = halves(wide)
    lifted = dot3(high, low, lift_high[...], lift_low[...])
    lifted_high, lifted_low = halves(lifted)
    put = put.astype(jnp.bfloat16)
    packed = dot(put, lifted_high) + dot(put, lifted_low)
    lane = iota((rows, LANES), 1)
    packed = jnp.where(lane == TAG_FACE, code_col, packed)
    packed = jnp.where(lane == TAG_ROW, row_col, packed)
    out[...] = packed.reshape(peers, cap, LANES)
    confs = ctrace.shape[0]
    eye = (iota((confs, confs), 0) == iota((confs, confs), 1)).astype(jnp.float32)
    conf_col = column(eye, (cface[...] * elements + celem[...] + 1).astype(jnp.float32))
    c = jnp.concatenate([ctrace[...], jnp.zeros((confs, LANES - TRACE), jnp.float32)], axis=1)
    conf_out[...] = jnp.where(iota((confs, LANES), 1) == TAG_FACE, conf_col, c)


def cell_kernel(peers, row_cap, adjoint, order, crow, table_high, table_low, y_out, col_out, spread):
    elements = adjoint.shape[0]
    slots = peers * row_cap
    place, _ = row_places(crow[...], peers, elements, row_cap)
    take = onehot_rows(place, slots)
    order_col = column(take, order[...].astype(jnp.float32))
    elem_col = column(take, iota((1, elements), 1).astype(jnp.float32) + 1.0)
    lane = iota((slots, 128), 1)
    col_out[...] = jnp.where(lane == 0, order_col, jnp.where(lane == 1, elem_col, 0.0))
    take = take.astype(jnp.bfloat16)
    spread[...] = jnp.zeros_like(spread)
    for half, part in enumerate(halves(adjoint[...])):
        moved = dot(take, part)
        for v in range(VARS):
            spread[half, v * slots : (v + 1) * slots, :CELL] = moved[:, v * CELL : (v + 1) * CELL]
    order_rows = jnp.concatenate([order_col] * VARS, axis=0)
    high, low = spread[0], spread[1]
    wide_high = jnp.concatenate([jnp.where(order_rows == float(p), high, 0.0).astype(jnp.bfloat16) for p in ORDERS], axis=1)
    wide_low = jnp.concatenate([jnp.where(order_rows == float(p), low, 0.0).astype(jnp.bfloat16) for p in ORDERS], axis=1)
    y_out[...] = dot3(wide_high, wide_low, table_high[...], table_low[...])


def face_kernel(peers, row_cap, elements, incoming, conf, y, cols, table_high, table_low, out, spread):
    slots = peers * row_cap
    x = jnp.concatenate([incoming[...].reshape(-1, LANES), conf[...]], axis=0)
    count = x.shape[0]
    code_col = x[:, TAG_FACE : TAG_FACE + 1]
    code_row = jnp.sum(jnp.where(iota((count, count), 0) == iota((count, count), 1), code_col, 0.0), axis=0, keepdims=True)
    order_col, elem_col = cols[:, 0:1], cols[:, 1:2]
    wanted = jnp.concatenate([jnp.where(elem_col > 0.0, elem_col + float(f * elements), -1.0) for f in range(FACES)], axis=0)
    gather = (wanted == code_row).astype(jnp.bfloat16)
    high, low = halves(x)
    face_sum = dot(gather, high) + dot(gather, low)
    spread[...] = jnp.zeros_like(spread)
    for f in range(FACES):
        for v in range(VARS):
            spread[v * slots : (v + 1) * slots, f * FACE_PAD : f * FACE_PAD + FACE] = face_sum[
                f * slots : (f + 1) * slots, v * FACE : (v + 1) * FACE
            ]
    order_rows = jnp.concatenate([order_col] * VARS, axis=0)
    z = spread[...]
    wide = jnp.concatenate([jnp.where(order_rows == float(p), z, 0.0) for p in ORDERS], axis=1)
    high, low = halves(wide)
    total = y[...] + dot3(high, low, table_high[...], table_low[...])
    for v in range(VARS):
        out[:, :, v * ROW : (v + 1) * ROW] = total[v * slots : (v + 1) * slots].reshape(peers, row_cap, ROW)


def place_kernel(peers, row_cap, arrived, tags, out):
    elements = out.shape[0]
    rows = peers * row_cap
    x = arrived[...].reshape(rows, arrived.shape[2])
    slot_col = tags[:, :row_cap, TAG_ROW : TAG_ROW + 1].reshape(rows, 1)
    slot_row = jnp.sum(jnp.where(iota((rows, rows), 0) == iota((rows, rows), 1), slot_col, 0.0), axis=0, keepdims=True)
    put = (iota((elements, rows), 0).astype(jnp.float32) + 1.0 == slot_row).astype(jnp.bfloat16)
    high, low = halves(x)
    rest = (x - high.astype(jnp.float32) - low.astype(jnp.float32)).astype(jnp.bfloat16)
    out[...] = dot(put, high) + dot(put, low) + dot(put, rest)


def call(kernel, outs, *args, scratch=(), flops=0):
    sizes = [np.prod(a.shape) * a.dtype.itemsize for a in (*args, *jax.tree.leaves(outs))]
    return pl.pallas_call(
        kernel,
        out_shape=outs,
        scratch_shapes=scratch,
        compiler_params=pltpu.CompilerParams(vmem_limit_bytes=48 * 1024 * 1024),
        cost_estimate=pl.CostEstimate(flops=flops, bytes_accessed=int(sum(sizes)), transcendentals=0),
    )(*args)


def exchange(block):
    return lax.all_to_all(block, ("gx", "gy"), split_axis=0, concat_axis=0, tiled=True)


def from_behind(block, axis, distance):
    devices = range(lax.axis_size(axis))
    route = [((i - distance) % len(devices), i) for i in devices]
    return lax.ppermute(block, axis, route)


def body(
    adjoint,
    order,
    mortar_trace,
    mortar_sub,
    mortar_dest,
    mortar_elem,
    mortar_face,
    conf_trace,
    conf_elem,
    conf_face,
    coarse_row,
):
    elements = adjoint.shape[0]
    count = mortar_trace.shape[0]
    confs = conf_trace.shape[0]
    peers = lax.axis_size("gx") * lax.axis_size("gy")
    cap = max(2, 2 * count // peers)
    row_cap = max(2, elements // peers)
    slots = peers * row_cap
    assert row_cap <= cap
    lift, cell, face = [tuple(jnp.asarray(t) for t in pair) for pair in basis_tables()]
    f32 = jnp.float32
    line = lambda a: a.reshape(1, -1)
    order, coarse_row = line(order), line(coarse_row)
    outgoing, conf = call(
        functools.partial(pack_kernel, peers, cap, elements),
        (jax.ShapeDtypeStruct((peers, cap, LANES), f32), jax.ShapeDtypeStruct((confs, LANES), f32)),
        mortar_trace,
        line(mortar_sub),
        line(mortar_dest),
        line(mortar_elem),
        line(mortar_face),
        coarse_row,
        conf_trace,
        line(conf_elem),
        line(conf_face),
        *lift,
    )
    incoming = exchange(outgoing)
    conf = from_behind(conf, "gz", 1)
    y, cols = call(
        functools.partial(cell_kernel, peers, row_cap),
        (jax.ShapeDtypeStruct((VARS * slots, ROW), f32), jax.ShapeDtypeStruct((slots, 128), f32)),
        adjoint,
        order,
        coarse_row,
        *cell,
        scratch=[pltpu.VMEM((2, VARS * slots, CELL_PAD), f32)],
    )
    rows = call(
        functools.partial(face_kernel, peers, row_cap, elements),
        jax.ShapeDtypeStruct((peers, row_cap, VARS * ROW), f32),
        incoming,
        conf,
        y,
        cols,
        *face,
        scratch=[pltpu.VMEM((VARS * slots, FACES * FACE_PAD), f32)],
    )
    arrived = exchange(rows)
    return call(
        functools.partial(place_kernel, peers, row_cap),
        jax.ShapeDtypeStruct((elements, VARS * ROW), f32),
        arrived,
        incoming,
    )


def solution(mesh):
    rows = P(("gx", "gy", "gz"))
    wide = P(("gx", "gy", "gz"), None)
    return jax.shard_map(
        body,
        mesh=mesh,
        in_specs=(wide, rows, wide, rows, wide, rows, rows, wide, rows, rows, rows),
        out_specs=wide,
        check_vma=False,
    )
```

profile of v0, /device:TPU:0, one launch (start us, length us, event | category | flops | bytes accessed | tf_op | source)
XLA Modules:
  0.0 39.1 jit_solution(3293465309182147806)
XLA Ops:
  0.0 0.0 copy-start.2
  0.0 0.0 copy-start.4
  0.0 1.1 %copy-done.4 = bf16[1024,256]{1,0:T(8,128)(2,1)S(1)} copy-done((bf16[1024,256]{1,0:T(8,128)(2,1)S(1)}, bf16[1024,256]{1,0:T(8,128)(2,1)}, u32[]{:S(2)}) %copy-start.4) | copy-done | bytes 524312
  1.1 1.0 %copy-done.5 = bf16[1024,256]{1,0:T(8,128)(2,1)S(1)} copy-done((bf16[1024,256]{1,0:T(8,128)(2,1)S(1)}, bf16[1024,256]{1,0:T(8,128)(2,1)}, u32[]{:S(2)}) %copy-start.5) | copy-done | bytes 524312
  2.2 0.9 %copy-done.7 = f32[96,245]{1,0:T(8,128)S(1)} copy-done((f32[96,245]{1,0:T(8,128)S(1)}, f32[96,245]{1,0:T(8,128)}, u32[]{:S(2)}) %copy-start.7) | copy-done | bytes 94104
  3.1 0.8 %copy-done.8 = f32[64,245]{1,0:T(8,128)S(1)} copy-done((f32[64,245]{1,0:T(8,128)S(1)}, f32[64,245]{1,0:T(8,128)}, u32[]{:S(2)}) %copy-start.8) | copy-done | bytes 62744
  3.9 0.7 %copy-done.11 = s32[32]{0:T(128)S(1)} copy-done((s32[32]{0:T(128)S(1)}, s32[32]{0:T(128)}, u32[]{:S(2)}) %copy-start.11) | copy-done | bytes 152
  4.6 0.7 %copy-done.13 = s32[96]{0:T(128)S(1)} copy-done((s32[96]{0:T(128)S(1)}, s32[96]{0:T(128)}, u32[]{:S(2)}) %copy-start.13) | copy-done | bytes 408
  5.2 0.7 %copy-done.14 = s32[96,1]{0,1:T(1,128)S(1)} copy-done((s32[96,1]{0,1:T(1,128)S(1)}, s32[96,1]{0,1:T(1,128)}, u32[]{:S(2)}) %copy-start.14) | copy-done | bytes 408
  5.9 0.7 %copy-done.15 = s32[96]{0:T(128)S(1)} copy-done((s32[96]{0:T(128)S(1)}, s32[96]{0:T(128)}, u32[]{:S(2)}) %copy-start.15) | copy-done | bytes 408
  6.5 0.7 %copy-done.16 = s32[96]{0:T(128)S(1)} copy-done((s32[96]{0:T(128)S(1)}, s32[96]{0:T(128)}, u32[]{:S(2)}) %copy-start.16) | copy-done | bytes 408
  7.2 0.7 %copy-done.17 = s32[64]{0:T(128)S(1)} copy-done((s32[64]{0:T(128)S(1)}, s32[64]{0:T(128)}, u32[]{:S(2)}) %copy-start.17) | copy-done | bytes 280
  7.8 0.7 %copy-done.18 = s32[64]{0:T(128)S(1)} copy-done((s32[64]{0:T(128)S(1)}, s32[64]{0:T(128)}, u32[]{:S(2)}) %copy-start.18) | copy-done | bytes 280
  8.5 1.4 %shard_map.163 = (f32[8,24,256]{2,1,0:T(8,128)}, f32[64,256]{1,0:T(8,128)}) custom-call(f32[96,245]{1,0:T(8,128)S(1)} %copy-done.7, s32[1,96]{1,0:T(1,128)S(1)} %bitcast.10, s32[1,96]{1,0:T(1,128)S(1)} %bitcast.11, s32[1,96]{1,0:T(1,128)S(1)} %bitcast.12, s32[1,96]{1,0:T(1,128)S(1)} %bitcast.13, s32[1,32]{1,0:T(1,128)S(1)} %bitcast.8, ...), custom_call_target="tpu_custom_call" | custom-call | bytes 1469696 | tf_op jit(solution)/shard_map/pallas_call | solution.py:234
  9.9 7.4 %all-to-all-start = ((f32[8,24,256]{2,1,0:T(8,128)}), f32[8,24,256]{2,1,0:T(8,128)S(1)}, u32[]{:S(2)}, u32[]{:S(2)}) async-start(f32[8,24,256]{2,1,0:T(8,128)} %get-tuple-element.9), calls=%async_computation | async-start | bytes 393216 | tf_op jit(solution)/shard_map/all_to_all | solution.py:244
  17.3 0.0 copy-start.19
  17.3 0.1 collective-permute-start
  17.4 0.0 copy-done.2
  17.4 0.0 copy-done.6
  17.4 0.6 %copy-done.12 = s32[32]{0:T(128)S(1)} copy-done((s32[32]{0:T(128)S(1)}, s32[32]{0:T(128)}, u32[]{:S(2)}) %copy-start.12) | copy-done | bytes 152
  18.0 0.0 copy-done.19
  18.0 1.2 %copy-done.3 = bf16[1920,216]{1,0:T(8,128)(2,1)S(1)} copy-done((bf16[1920,216]{1,0:T(8,128)(2,1)S(1)}, bf16[1920,216]{1,0:T(8,128)(2,1)}, u32[]{:S(2)}) %copy-start.3) | copy-done | bytes 829464
  19.2 1.1 %shard_map.164 = (f32[160,216]{1,0:T(8,128)S(1)}, f32[32,128]{1,0:T(8,128)S(1)}) custom-call(f32[32,1715]{1,0:T(8,128)S(1)} %copy-done.6, s32[1,32]{1,0:T(1,128)S(1)} %bitcast.16, s32[1,32]{1,0:T(1,128)S(1)} %bitcast.9, bf16[1920,216]{1,0:T(8,128)(2,1)S(1)} %copy-done.2, bf16[1920,216]{1,0:T(8,128)(2,1)S(1)} %copy-done.3), custom_call_target="tpu_custom_call" | custom-call | bytes 2033280 | tf_op jit(solution)/shard_map/pallas_call | solution.py:234
  20.3 1.0 %collective-permute-done.conf = f32[64,256]{1,0:T(8,128)S(1)} collective-permute-done((f32[64,256]{1,0:T(8,128)}, f32[64,256]{1,0:T(8,128)S(1)}, u32[]{:S(2)}, u32[]{:S(2)}) %collective-permute-start) | collective-permute-done | bytes 65568 | tf_op jit(solution)/shard_map/ppermute | solution.py:250
  21.3 0.6 %copy-done.9 = f32[64,256]{1,0:T(8,128)} copy-done((f32[64,256]{1,0:T(8,128)}, f32[64,256]{1,0:T(8,128)S(1)}, u32[]{:S(2)}) %copy-start.9) | copy-done | bytes 65560
  21.9 4.1 %all-to-all-done.incoming.tags = f32[8,24,256]{2,1,0:T(8,128)S(1)} async-done(((f32[8,24,256]{2,1,0:T(8,128)}), f32[8,24,256]{2,1,0:T(8,128)S(1)}, u32[]{:S(2)}, u32[]{:S(2)}) %all-to-all-start) | async-done | bytes 196640 | tf_op jit(solution)/shard_map/all_to_all | solution.py:244
  26.0 0.0 copy-done
  26.0 0.0 copy-done.1
  26.0 0.8 %copy-done.10 = f32[64,256]{1,0:T(8,128)S(1)} copy-done((f32[64,256]{1,0:T(8,128)S(1)}, f32[64,256]{1,0:T(8,128)}, u32[]{:S(2)}) %copy-start.10) | copy-done | bytes 65560
  26.9 1.2 %shard_map.165 = f32[8,4,1080]{2,1,0:T(4,128)S(1)} custom-call(f32[8,24,256]{2,1,0:T(8,128)S(1)} %all-to-all-done.incoming.tags, f32[64,256]{1,0:T(8,128)S(1)} %copy-done.10, f32[160,216]{1,0:T(8,128)S(1)} %get-tuple-element.11.y, f32[32,128]{1,0:T(8,128)S(1)} %get-tuple-element.12.cols, bf16[1920,216]{1,0:T(8,128)(2,1)S(1)} %copy-done, ...), custom_call_target="tpu_custom_call" | custom-call | bytes 2213888 | tf_op jit(solution)/shard_map/pallas_call | solution.py:234
  28.1 10.0 %all_to_all.10.arrived = f32[8,4,1080]{2,1,0:T(4,128)S(1)} all-to-all(f32[8,4,1080]{2,1,0:T(4,128)S(1)} %shard_map.165), channel_id=1, replica_groups=mesh['gx'=2,'gy'=4,'gz'=4] {'gx','gy'}, dimensions={0} | all-to-all | bytes 276480 | tf_op jit(solution)/shard_map/all_to_all | solution.py:244
  38.1 0.9 %shard_map.166 = f32[32,1080]{1,0:T(8,128)} custom-call(f32[8,4,1080]{2,1,0:T(4,128)S(1)} %all_to_all.10.arrived, f32[8,24,256]{2,1,0:T(8,128)S(1)} %all-to-all-done.incoming.tags), custom_call_target="tpu_custom_call" | custom-call | bytes 473088 | tf_op jit(solution)/shard_map/pallas_call | solution.py:234
  (17 shorter events, 0.0 us)
Async XLA Ops:
  0.0 17.4 %copy-start.2 = (bf16[1920,216]{1,0:T(8,128)(2,1)S(1)}, bf16[1920,216]{1,0:T(8,128)(2,1)}, u32[]{:S(2)}) copy-start(bf16[1920,216]{1,0:T(8,128)(2,1)} %constant.14.clone.table_high) | copy-start | bytes 2488324
  0.0 1.1 %copy-start.4 = (bf16[1024,256]{1,0:T(8,128)(2,1)S(1)}, bf16[1024,256]{1,0:T(8,128)(2,1)}, u32[]{:S(2)}) copy-start(bf16[1024,256]{1,0:T(8,128)(2,1)} %constant.12.clone.lift_high) | copy-start | bytes 1572868
  1.1 1.0 %copy-start.5 = (bf16[1024,256]{1,0:T(8,128)(2,1)S(1)}, bf16[1024,256]{1,0:T(8,128)(2,1)}, u32[]{:S(2)}) copy-start(bf16[1024,256]{1,0:T(8,128)(2,1)} %constant.13.clone.lift_low) | copy-start | bytes 1572868
  2.2 0.9 %copy-start.7 = (f32[96,245]{1,0:T(8,128)S(1)}, f32[96,245]{1,0:T(8,128)}, u32[]{:S(2)}) copy-start(f32[96,245]{1,0:T(8,128)} %trace.1) | copy-start | bytes 282244
  3.1 0.8 %copy-start.8 = (f32[64,245]{1,0:T(8,128)S(1)}, f32[64,245]{1,0:T(8,128)}, u32[]{:S(2)}) copy-start(f32[64,245]{1,0:T(8,128)} %ctrace.1) | copy-start | bytes 188164
  3.9 0.7 %copy-start.11 = (s32[32]{0:T(128)S(1)}, s32[32]{0:T(128)}, u32[]{:S(2)}) copy-start(s32[32]{0:T(128)} %param.27) | copy-start | bytes 388
  4.6 0.7 %copy-start.13 = (s32[96]{0:T(128)S(1)}, s32[96]{0:T(128)}, u32[]{:S(2)}) copy-start(s32[96]{0:T(128)} %param.20) | copy-start | bytes 1156
  5.2 0.7 %copy-start.14 = (s32[96,1]{0,1:T(1,128)S(1)}, s32[96,1]{0,1:T(1,128)}, u32[]{:S(2)}) copy-start(s32[96,1]{0,1:T(1,128)} %param.21) | copy-start | bytes 1156
  5.9 0.7 %copy-start.15 = (s32[96]{0:T(128)S(1)}, s32[96]{0:T(128)}, u32[]{:S(2)}) copy-start(s32[96]{0:T(128)} %param.22) | copy-start | bytes 1156
  6.5 0.7 %copy-start.16 = (s32[96]{0:T(128)S(1)}, s32[96]{0:T(128)}, u32[]{:S(2)}) copy-start(s32[96]{0:T(128)} %param.23) | copy-start | bytes 1156
  7.2 0.7 %copy-start.17 = (s32[64]{0:T(128)S(1)}, s32[64]{0:T(128)}, u32[]{:S(2)}) copy-start(s32[64]{0:T(128)} %param.25) | copy-start | bytes 772
  7.8 0.7 %copy-start.18 = (s32[64]{0:T(128)S(1)}, s32[64]{0:T(128)}, u32[]{:S(2)}) copy-start(s32[64]{0:T(128)} %param.26) | copy-start | bytes 772
  9.9 7.5 %copy-start.6 = (f32[32,1715]{1,0:T(8,128)S(1)}, f32[32,1715]{1,0:T(8,128)}, u32[]{:S(2)}) copy-start(f32[32,1715]{1,0:T(8,128)} %adjoint.1) | copy-start | bytes 658564
  9.9 16.1 %all-to-all-start = ((f32[8,24,256]{2,1,0:T(8,128)}), f32[8,24,256]{2,1,0:T(8,128)S(1)}, u32[]{:S(2)}, u32[]{:S(2)}) async-start(f32[8,24,256]{2,1,0:T(8,128)} %get-tuple-element.9), calls=%async_computation | async-start | bytes 393216 | tf_op jit(solution)/shard_map/all_to_all | solution.py:244
  17.3 0.7 %copy-start.12 = (s32[32]{0:T(128)S(1)}, s32[32]{0:T(128)}, u32[]{:S(2)}) copy-start(s32[32]{0:T(128)} %param.27) | copy-start | bytes 388
  17.3 0.7 %copy-start.19 = (s32[32]{0:T(128)S(1)}, s32[32]{0:T(128)}, u32[]{:S(2)}) copy-start(s32[32]{0:T(128)} %param.18) | copy-start | bytes 388
  17.3 4.0 %collective-permute-start = (f32[64,256]{1,0:T(8,128)}, f32[64,256]{1,0:T(8,128)S(1)}, u32[]{:S(2)}, u32[]{:S(2)}) collective-permute-start(f32[64,256]{1,0:T(8,128)} %get-tuple-element.10), channel_id=1, source_target_pairs={{3,0},{0,1},{1,2},{2,3},{7,4},{4,5},{5,6},{6,7},{11,8},{8,9},{9,10... | collective-permute-start | bytes 196616 | tf_op jit(solution)/shard_map/ppermute | solution.py:250
  18.0 1.2 %copy-start.3 = (bf16[1920,216]{1,0:T(8,128)(2,1)S(1)}, bf16[1920,216]{1,0:T(8,128)(2,1)}, u32[]{:S(2)}) copy-start(bf16[1920,216]{1,0:T(8,128)(2,1)} %constant.15.clone.table_low) | copy-start | bytes 2488324
  19.2 6.9 %copy-start = (bf16[1920,216]{1,0:T(8,128)(2,1)S(1)}, bf16[1920,216]{1,0:T(8,128)(2,1)}, u32[]{:S(2)}) copy-start(bf16[1920,216]{1,0:T(8,128)(2,1)} %constant.16.clone.table_high) | copy-start | bytes 2488324
  19.2 6.9 %copy-start.1 = (bf16[1920,216]{1,0:T(8,128)(2,1)S(1)}, bf16[1920,216]{1,0:T(8,128)(2,1)}, u32[]{:S(2)}) copy-start(bf16[1920,216]{1,0:T(8,128)(2,1)} %constant.17.clone.table_low) | copy-start | bytes 2488324
  21.3 0.6 %copy-start.9 = (f32[64,256]{1,0:T(8,128)}, f32[64,256]{1,0:T(8,128)S(1)}, u32[]{:S(2)}) copy-start(f32[64,256]{1,0:T(8,128)S(1)} %collective-permute-done.conf) | copy-start | bytes 196612
  26.0 0.8 %copy-start.10 = (f32[64,256]{1,0:T(8,128)S(1)}, f32[64,256]{1,0:T(8,128)}, u32[]{:S(2)}) copy-start(f32[64,256]{1,0:T(8,128)} %copy-done.9) | copy-start | bytes 196612
where the time goes:
time: 39.6 us; the launch traced here: 39.1 us
  local copies, waits for them, and re-layouts  11.7 us (30%)
  blocking collectives  10 us (25%)
  starting transfers between devices  7.47 us (19%)
  waiting for transfers between devices  5.14 us (13%)
  Pallas kernels  4.61 us (12%)
    unnamed x40, local copies, waits for them, and re-layouts  11.7 us
    all_to_all x1, blocking collectives, exchange(): lax.all_to_all(block, ('gx', 'gy'), split_axis=0, concat_axis=0, tiled=True)  10 us
    all_to_all x1, starting transfers between devices, exchange(): lax.all_to_all(block, ('gx', 'gy'), split_axis=0, concat_axis=0, tiled=True)  7.41 us
    pallas_call x4, Pallas kernels, call(): pl.pallas_call(kernel, out_shape=outs, scratch_shapes=scratch, compiler_p...  4.61 us
    all_to_all x1, waiting for transfers between devices, exchange(): lax.all_to_all(block, ('gx', 'gy'), split_axis=0, concat_axis=0, tiled=True)  4.13 us
    ppermute x1, waiting for transfers between devices, from_behind(): return lax.ppermute(block, axis, route)  1.01 us
  transfers between devices with their start and end apart: 2, of which 2 were waited for; matrix products, arithmetic and copies ran while one was open for 0% of the time, Pallas kernels for 3%

commit v1 on v0

--- a/solution.py
+++ b/solution.py
@@ -125,36 +125,27 @@
     peers,
     cap,
     elements,
-    trace,
-    sub,
-    dest,
-    elem,
-    face,
-    crow,
-    ctrace,
-    celem,
-    cface,
-    lift_high,
-    lift_low,
+    get,
     out,
     conf_out,
 ):
-    count = trace.shape[0]
+    dest, elem, face, sub, crow, cface, celem = [get(i) for i in range(7)]
+    count = dest.shape[1]
     rows = peers * cap
-    member = (iota((peers, count), 0) == dest[...]).astype(jnp.float32)
+    member = (iota((peers, count), 0) == dest).astype(jnp.float32)
     base = iota(member.shape, 0).astype(jnp.float32) * cap
     place = jnp.sum(member * (base + earlier(member)), axis=0, keepdims=True)
     put = onehot_rows(place, rows)
-    code = (face[...] * elements + elem[...] + 1).astype(jnp.float32)
+    code = (face * elements + elem + 1).astype(jnp.float32)
     code_col = column(put, code)
-    row_place, row_slot = row_places(crow[...], peers, elements, cap)
+    row_place, row_slot = row_places(crow, peers, elements, cap)
     row_col = column(onehot_rows(row_place, rows), row_slot + 1.0)
     eye = (iota((count, count), 0) == iota((count, count), 1)).astype(jnp.float32)
-    sub_col = column(eye, sub[...].astype(jnp.float32))
-    x = jnp.concatenate([trace[...], jnp.zeros((count, LANES - TRACE), jnp.float32)], axis=1)
+    sub_col = column(eye, sub.astype(jnp.float32))
+    x = jnp.concatenate([get(7), jnp.zeros((count, LANES - TRACE), jnp.float32)], axis=1)
     wide = jnp.concatenate([jnp.where(sub_col == float(s), x, 0.0) for s in range(4)], axis=1)
     high, low = halves(wide)
-    lifted = dot3(high, low, lift_high[...], lift_low[...])
+    lifted = dot3(high, low, get(9), get(10))
     lifted_high, lifted_low = halves(lifted)
     put = put.astype(jnp.bfloat16)
     packed = dot(put, lifted_high) + dot(put, lifted_low)
@@ -162,25 +153,26 @@
     packed = jnp.where(lane == TAG_FACE, code_col, packed)
     packed = jnp.where(lane == TAG_ROW, row_col, packed)
     out[...] = packed.reshape(peers, cap, LANES)
-    confs = ctrace.shape[0]
+    confs = cface.shape[1]
     eye = (iota((confs, confs), 0) == iota((confs, confs), 1)).astype(jnp.float32)
-    conf_col = column(eye, (cface[...] * elements + celem[...] + 1).astype(jnp.float32))
-    c = jnp.concatenate([ctrace[...], jnp.zeros((confs, LANES - TRACE), jnp.float32)], axis=1)
+    conf_col = column(eye, (cface * elements + celem + 1).astype(jnp.float32))
+    c = jnp.concatenate([get(8), jnp.zeros((confs, LANES - TRACE), jnp.float32)], axis=1)
     conf_out[...] = jnp.where(iota((confs, LANES), 1) == TAG_FACE, conf_col, c)
 
 
-def cell_kernel(peers, row_cap, adjoint, order, crow, table_high, table_low, y_out, col_out, spread):
-    elements = adjoint.shape[0]
+def cell_kernel(peers, row_cap, get, y_out, col_out, face_high, face_low, spread):
+    order, crow = get(0), get(1)
+    elements = order.shape[1]
     slots = peers * row_cap
-    place, _ = row_places(crow[...], peers, elements, row_cap)
+    place, _ = row_places(crow, peers, elements, row_cap)
     take = onehot_rows(place, slots)
-    order_col = column(take, order[...].astype(jnp.float32))
+    order_col = column(take, order.astype(jnp.float32))
     elem_col = column(take, iota((1, elements), 1).astype(jnp.float32) + 1.0)
     lane = iota((slots, 128), 1)
     col_out[...] = jnp.where(lane == 0, order_col, jnp.where(lane == 1, elem_col, 0.0))
     take = take.astype(jnp.bfloat16)
     spread[...] = jnp.zeros_like(spread)
-    for half, part in enumerate(halves(adjoint[...])):
+    for half, part in enumerate(halves(get(2))):
         moved = dot(take, part)
         for v in range(VARS):
             spread[half, v * slots : (v + 1) * slots, :CELL] = moved[:, v * CELL : (v + 1) * CELL]
@@ -188,10 +180,12 @@
     high, low = spread[0], spread[1]
     wide_high = jnp.concatenate([jnp.where(order_rows == float(p), high, 0.0).astype(jnp.bfloat16) for p in ORDERS], axis=1)
     wide_low = jnp.concatenate([jnp.where(order_rows == float(p), low, 0.0).astype(jnp.bfloat16) for p in ORDERS], axis=1)
-    y_out[...] = dot3(wide_high, wide_low, table_high[...], table_low[...])
-
-
-def face_kernel(peers, row_cap, elements, incoming, conf, y, cols, table_high, table_low, out, spread):
+    y_out[...] = dot3(wide_high, wide_low, get(3), get(4))
+    face_high[...] = get(5)
+    face_low[...] = get(6)
+
+
+def face_kernel(peers, row_cap, elements, get, incoming, conf, y, cols, table_high, table_low, out, spread):
     slots = peers * row_cap
     x = jnp.concatenate([incoming[...].reshape(-1, LANES), conf[...]], axis=0)
     count = x.shape[0]
@@ -217,7 +211,7 @@
         out[:, :, v * ROW : (v + 1) * ROW] = total[v * slots : (v + 1) * slots].reshape(peers, row_cap, ROW)
 
 
-def place_kernel(peers, row_cap, arrived, tags, out):
+def place_kernel(peers, row_cap, get, arrived, tags, out):
     elements = out.shape[0]
     rows = peers * row_cap
     x = arrived[...].reshape(rows, arrived.shape[2])
@@ -229,15 +223,34 @@
     out[...] = dot(put, high) + dot(put, low) + dot(put, rest)
 
 
-def call(kernel, outs, *args, scratch=(), flops=0):
-    sizes = [np.prod(a.shape) * a.dtype.itemsize for a in (*args, *jax.tree.leaves(outs))]
+def fetched(kernel, n_far, n_near, n_out, *refs):
+    far, near, outs = refs[:n_far], refs[n_far : n_far + n_near], refs[n_far + n_near : n_far + n_near + n_out]
+    rest = refs[n_far + n_near + n_out :]
+    held, sems, scratch = rest[:n_far], rest[n_far], rest[n_far + 1 :]
+    copies = [pltpu.make_async_copy(src, dst, sems.at[i]) for i, (src, dst) in enumerate(zip(far, held))]
+    for copy in copies:
+        copy.start()
+
+    def get(i):
+        copies[i].wait()
+        return held[i][...]
+
+    kernel(get, *near, *outs, *scratch)
+
+
+def call(kernel, outs, far, near=(), scratch=(), flops=0):
+    shapes = jax.tree.leaves(outs)
+    sizes = [np.prod(a.shape) * a.dtype.itemsize for a in (*far, *near, *shapes)]
+    in_specs = [pl.BlockSpec(memory_space=pltpu.HBM)] * len(far) + [pl.BlockSpec(memory_space=pltpu.VMEM)] * len(near)
+    scratch = [*[pltpu.VMEM(a.shape, a.dtype) for a in far], pltpu.SemaphoreType.DMA((max(1, len(far)),)), *scratch]
     return pl.pallas_call(
-        kernel,
+        functools.partial(fetched, kernel, len(far), len(near), len(shapes)),
+        in_specs=in_specs,
         out_shape=outs,
         scratch_shapes=scratch,
         compiler_params=pltpu.CompilerParams(vmem_limit_bytes=48 * 1024 * 1024),
         cost_estimate=pl.CostEstimate(flops=flops, bytes_accessed=int(sum(sizes)), transcendentals=0),
-    )(*args)
+    )(*[pltpu.with_memory_space_constraint(a, pltpu.HBM) for a in far], *near)
 
 
 def exchange(block):
@@ -278,44 +291,44 @@
     outgoing, conf = call(
         functools.partial(pack_kernel, peers, cap, elements),
         (jax.ShapeDtypeStruct((peers, cap, LANES), f32), jax.ShapeDtypeStruct((confs, LANES), f32)),
-        mortar_trace,
-        line(mortar_sub),
-        line(mortar_dest),
-        line(mortar_elem),
-        line(mortar_face),
-        coarse_row,
-        conf_trace,
-        line(conf_elem),
-        line(conf_face),
-        *lift,
+        (
+            line(mortar_dest),
+            line(mortar_elem),
+            line(mortar_face),
+            line(mortar_sub),
+            coarse_row,
+            line(conf_face),
+            line(conf_elem),
+            mortar_trace,
+            conf_trace,
+            *lift,
+        ),
     )
     incoming = exchange(outgoing)
     conf = from_behind(conf, "gz", 1)
-    y, cols = call(
+    y, cols, *face = call(
         functools.partial(cell_kernel, peers, row_cap),
-        (jax.ShapeDtypeStruct((VARS * slots, ROW), f32), jax.ShapeDtypeStruct((slots, 128), f32)),
-        adjoint,
-        order,
-        coarse_row,
-        *cell,
+        (
+            jax.ShapeDtypeStruct((VARS * slots, ROW), f32),
+            jax.ShapeDtypeStruct((slots, 128), f32),
+            *[jax.ShapeDtypeStruct(t.shape, t.dtype) for t in face],
+        ),
+        (order, coarse_row, adjoint, *cell, *face),
         scratch=[pltpu.VMEM((2, VARS * slots, CELL_PAD), f32)],
     )
     rows = call(
         functools.partial(face_kernel, peers, row_cap, elements),
         jax.ShapeDtypeStruct((peers, row_cap, VARS * ROW), f32),
-        incoming,
-        conf,
-        y,
-        cols,
-        *face,
+        (),
+        (incoming, conf, y, cols, *face),
         scratch=[pltpu.VMEM((VARS * slots, FACES * FACE_PAD), f32)],
     )
     arrived = exchange(rows)
     return call(
         functools.partial(place_kernel, peers, row_cap),
         jax.ShapeDtypeStruct((elements, VARS * ROW), f32),
-        arrived,
-        incoming,
+        (),
+        (arrived, incoming),
     )
 
 

time: 39.6 us -> 31.3 us (0.79)
  local copies, waits for them, and re-layouts: 11.7 us -> 0 us
  Pallas kernels: 4.61 us -> 7.5 us
  waiting for transfers between devices: 5.14 us -> 6.2 us
    unnamed x40 -> x0, local copies, waits for them, and re-layouts: 11.7 us -> none
    pallas_call x4, Pallas kernels: 4.61 us -> 7.5 us  [call(): pl.pallas_call(functools.partial(fetched, kernel, len(far), len(near), le...]
    all_to_all x1, waiting for transfers between devices: 4.13 us -> 5.03 us  [exchange(): lax.all_to_all(block, ('gx', 'gy'), split_axis=0, concat_axis=0, tiled=True)]
  transfers between devices with their start and end apart: 2 -> 2, of which waited for: 2 -> 2; matrix products, arithmetic and copies ran while one was open for 0% -> 0% of each run, Pallas kernels for 3% -> 8%
where the time goes in v1:
time: 31.3 us; the launch traced here: 31.1 us
  blocking collectives  10 us (32%)
  Pallas kernels  7.5 us (24%)
  starting transfers between devices  7.3 us (23%)
  waiting for transfers between devices  6.2 us (20%)
    all_to_all x1, blocking collectives, exchange(): lax.all_to_all(block, ('gx', 'gy'), split_axis=0, concat_axis=0, tiled=True)  10 us
    pallas_call x4, Pallas kernels, call(): pl.pallas_call(functools.partial(fetched, kernel, len(far), len(near), le...  7.5 us
    all_to_all x1, starting transfers between devices, exchange(): lax.all_to_all(block, ('gx', 'gy'), split_axis=0, concat_axis=0, tiled=True)  7.29 us
    all_to_all x1, waiting for transfers between devices, exchange(): lax.all_to_all(block, ('gx', 'gy'), split_axis=0, concat_axis=0, tiled=True)  5.03 us
    ppermute x1, waiting for transfers between devices, from_behind(): return lax.ppermute(block, axis, route)  1.16 us
  transfers between devices with their start and end apart: 2, of which 2 were waited for; matrix products, arithmetic and copies ran while one was open for 0% of the time, Pallas kernels for 8%

profile of v1, /device:TPU:0, one launch (start us, length us, event | category | flops | bytes accessed | tf_op | source)
XLA Modules:
  0.0 31.1 jit_solution(12300942456654452228)
XLA Ops:
  0.0 2.8 %shard_map.163 = (f32[8,24,256]{2,1,0:T(8,128)}, f32[64,256]{1,0:T(8,128)S(1)}) custom-call(s32[1,96]{1,0:T(1,128)} %bitcast.10, s32[1,96]{1,0:T(1,128)} %bitcast.11, s32[1,96]{1,0:T(1,128)} %bitcast.12, s32[1,96]{1,0:T(1,128)} %bitcast.13, s32[1,32]{1,0:T(1,128)} %bitcast.8, s32[1,64]{1,0:T(1,128)} %bitcast.14, s32[1,64]{1,0:T(1,128)} %bitcast.15, ...), custom_call_target="tpu_custom_call" | custom-call | bytes 1469696 | tf_op jit(solution)/shard_map/pallas_call | solution.py:246
  2.8 7.3 %all-to-all-start = ((f32[8,24,256]{2,1,0:T(8,128)}), f32[8,24,256]{2,1,0:T(8,128)S(1)}, u32[]{:S(2)}, u32[]{:S(2)}) async-start(f32[8,24,256]{2,1,0:T(8,128)} %get-tuple-element.11), calls=%async_computation | async-start | bytes 393216 | tf_op jit(solution)/shard_map/all_to_all | solution.py:257
  10.1 0.0 collective-permute-start
  10.1 2.5 %shard_map.164 = (f32[160,216]{1,0:T(8,128)S(1)}, f32[32,128]{1,0:T(8,128)S(1)}, bf16[1920,216]{1,0:T(8,128)(2,1)S(1)}, bf16[1920,216]{1,0:T(8,128)(2,1)S(1)}) custom-call(s32[1,32]{1,0:T(1,128)} %bitcast.16, s32[1,32]{1,0:T(1,128)} %bitcast.9, f32[32,1715]{1,0:T(8,128)} %refs_2_.1, bf16[1920,216]{1,0:T(8,128)(2,1)} %constant.14.clone.refs_3_, ...), custom_call_target="tpu_custom_call" | custom-call | bytes 5351040 | tf_op jit(solution)/shard_map/pallas_call | solution.py:246
  12.6 1.2 %collective-permute-done.refs_1_ = f32[64,256]{1,0:T(8,128)S(1)} collective-permute-done((f32[64,256]{1,0:T(8,128)S(1)}, f32[64,256]{1,0:T(8,128)S(1)}, u32[]{:S(2)}, u32[]{:S(2)}) %collective-permute-start) | collective-permute-done | bytes 65568 | tf_op jit(solution)/shard_map/ppermute | solution.py:263
  13.8 5.0 %all-to-all-done.refs_0_.refs_1_ = f32[8,24,256]{2,1,0:T(8,128)S(1)} async-done(((f32[8,24,256]{2,1,0:T(8,128)}), f32[8,24,256]{2,1,0:T(8,128)S(1)}, u32[]{:S(2)}, u32[]{:S(2)}) %all-to-all-start) | async-done | bytes 196640 | tf_op jit(solution)/shard_map/all_to_all | solution.py:257
  18.8 1.2 %shard_map.165 = f32[8,4,1080]{2,1,0:T(4,128)S(1)} custom-call(f32[8,24,256]{2,1,0:T(8,128)S(1)} %all-to-all-done.refs_0_.refs_1_, f32[64,256]{1,0:T(8,128)S(1)} %collective-permute-done.refs_1_, f32[160,216]{1,0:T(8,128)S(1)} %get-tuple-element.13.refs_2_, f32[32,128]{1,0:T(8,128)S(1)} %get-tuple-element.14.refs_3_, ...), custom_call_target="tpu_custom_call" | custom-call | bytes 2213888 | tf_op jit(solution)/shard_map/pallas_call | solution.py:246
  20.1 10.0 %all_to_all.10.refs_0_ = f32[8,4,1080]{2,1,0:T(4,128)S(1)} all-to-all(f32[8,4,1080]{2,1,0:T(4,128)S(1)} %shard_map.165), channel_id=1, replica_groups=mesh['gx'=2,'gy'=4,'gz'=4] {'gx','gy'}, dimensions={0} | all-to-all | bytes 276480 | tf_op jit(solution)/shard_map/all_to_all | solution.py:257
  30.1 0.9 %shard_map.166 = f32[32,1080]{1,0:T(8,128)} custom-call(f32[8,4,1080]{2,1,0:T(4,128)S(1)} %all_to_all.10.refs_0_, f32[8,24,256]{2,1,0:T(8,128)S(1)} %all-to-all-done.refs_0_.refs_1_), custom_call_target="tpu_custom_call" | custom-call | bytes 473088 | tf_op jit(solution)/shard_map/pallas_call | solution.py:246
Async XLA Ops:
  2.8 16.0 %all-to-all-start = ((f32[8,24,256]{2,1,0:T(8,128)}), f32[8,24,256]{2,1,0:T(8,128)S(1)}, u32[]{:S(2)}, u32[]{:S(2)}) async-start(f32[8,24,256]{2,1,0:T(8,128)} %get-tuple-element.11), calls=%async_computation | async-start | bytes 393216 | tf_op jit(solution)/shard_map/all_to_all | solution.py:257
  10.1 3.7 %collective-permute-start = (f32[64,256]{1,0:T(8,128)S(1)}, f32[64,256]{1,0:T(8,128)S(1)}, u32[]{:S(2)}, u32[]{:S(2)}) collective-permute-start(f32[64,256]{1,0:T(8,128)S(1)} %get-tuple-element.12), channel_id=1, source_target_pairs={{3,0},{0,1},{1,2},{2,3},{7,4},{4,5},{5,6},{6,7},{11,8},{8,9},{9,10... | collective-permute-start | bytes 196616 | tf_op jit(solution)/shard_map/ppermute | solution.py:263

commit v2 on v1

--- a/solution.py
+++ b/solution.py
@@ -99,17 +99,29 @@
     return dot(member.astype(jnp.bfloat16), before.astype(jnp.bfloat16))
 
 
-def owner_of(crow, peers, elements):
-    first = iota((peers, crow.shape[1]), 0) * elements
+def pairwise(peers):
+    return peers <= 8 and peers & (peers - 1) == 0
+
+
+def own_index(peers):
+    if not pairwise(peers):
+        return 0
+    return lax.axis_index("gx") * lax.axis_size("gy") + lax.axis_index("gy")
+
+
+def owner_of(crow, peers, elements, me):
+    first = (iota((peers, crow.shape[1]), 0) ^ me) * elements
     return ((crow >= first) & (crow < first + elements)).astype(jnp.float32)
 
 
 def row_places(crow, peers, elements, stride):
-    member = owner_of(crow, peers, elements)
+    me = own_index(peers)
+    member = owner_of(crow, peers, elements, me)
     rank = earlier(member)
-    base = iota(member.shape, 0).astype(jnp.float32)
-    place = jnp.sum(member * (base * stride + rank), axis=0, keepdims=True)
-    slot = crow.astype(jnp.float32) - jnp.sum(member * (base * elements), axis=0, keepdims=True)
+    block = iota(member.shape, 0)
+    place = jnp.sum(member * (block * stride + rank.astype(jnp.int32)).astype(jnp.float32), axis=0, keepdims=True)
+    owned = ((block ^ me) * elements).astype(jnp.float32)
+    slot = crow.astype(jnp.float32) - jnp.sum(member * owned, axis=0, keepdims=True)
     return place, slot
 
 
@@ -126,13 +138,13 @@
     cap,
     elements,
     get,
-    out,
     conf_out,
+    *outs,
 ):
     dest, elem, face, sub, crow, cface, celem = [get(i) for i in range(7)]
     count = dest.shape[1]
     rows = peers * cap
-    member = (iota((peers, count), 0) == dest).astype(jnp.float32)
+    member = ((iota((peers, count), 0) ^ own_index(peers)) == dest).astype(jnp.float32)
     base = iota(member.shape, 0).astype(jnp.float32) * cap
     place = jnp.sum(member * (base + earlier(member)), axis=0, keepdims=True)
     put = onehot_rows(place, rows)
@@ -152,7 +164,11 @@
     lane = iota((rows, LANES), 1)
     packed = jnp.where(lane == TAG_FACE, code_col, packed)
     packed = jnp.where(lane == TAG_ROW, row_col, packed)
-    out[...] = packed.reshape(peers, cap, LANES)
+    if len(outs) > 1:
+        for k, out in enumerate(outs):
+            out[...] = packed[k * cap : (k + 1) * cap]
+    else:
+        outs[0][...] = packed.reshape(peers, cap, LANES)
     confs = cface.shape[1]
     eye = (iota((confs, confs), 0) == iota((confs, confs), 1)).astype(jnp.float32)
     conf_col = column(eye, (cface * elements + celem + 1).astype(jnp.float32))
@@ -185,9 +201,11 @@
     face_low[...] = get(6)
 
 
-def face_kernel(peers, row_cap, elements, get, incoming, conf, y, cols, table_high, table_low, out, spread):
+def face_kernel(peers, row_cap, elements, blocks, get, *refs):
+    incoming, refs = refs[:blocks], refs[blocks:]
+    conf, y, cols, table_high, table_low, *outs, spread = refs
     slots = peers * row_cap
-    x = jnp.concatenate([incoming[...].reshape(-1, LANES), conf[...]], axis=0)
+    x = jnp.concatenate([*[block[...].reshape(-1, LANES) for block in incoming], conf[...]], axis=0)
     count = x.shape[0]
     code_col = x[:, TAG_FACE : TAG_FACE + 1]
     code_row = jnp.sum(jnp.where(iota((count, count), 0) == iota((count, count), 1), code_col, 0.0), axis=0, keepdims=True)
@@ -208,14 +226,20 @@
     high, low = halves(wide)
     total = y[...] + dot3(high, low, table_high[...], table_low[...])
     for v in range(VARS):
-        out[:, :, v * ROW : (v + 1) * ROW] = total[v * slots : (v + 1) * slots].reshape(peers, row_cap, ROW)
-
-
-def place_kernel(peers, row_cap, get, arrived, tags, out):
+        part = total[v * slots : (v + 1) * slots]
+        if len(outs) > 1:
+            for k, out in enumerate(outs):
+                out[:, v * ROW : (v + 1) * ROW] = part[k * row_cap : (k + 1) * row_cap]
+        else:
+            outs[0][:, :, v * ROW : (v + 1) * ROW] = part.reshape(peers, row_cap, ROW)
+
+
+def place_kernel(peers, row_cap, blocks, get, *refs):
+    arrived, tags, out = refs[:blocks], refs[blocks : 2 * blocks], refs[-1]
     elements = out.shape[0]
     rows = peers * row_cap
-    x = arrived[...].reshape(rows, arrived.shape[2])
-    slot_col = tags[:, :row_cap, TAG_ROW : TAG_ROW + 1].reshape(rows, 1)
+    x = jnp.concatenate([block[...].reshape(-1, out.shape[1]) for block in arrived], axis=0)
+    slot_col = jnp.concatenate([tag[..., :row_cap, TAG_ROW : TAG_ROW + 1].reshape(-1, 1) for tag in tags], axis=0)
     slot_row = jnp.sum(jnp.where(iota((rows, rows), 0) == iota((rows, rows), 1), slot_col, 0.0), axis=0, keepdims=True)
     put = (iota((elements, rows), 0).astype(jnp.float32) + 1.0 == slot_row).astype(jnp.bfloat16)
     high, low = halves(x)
@@ -253,8 +277,20 @@
     )(*[pltpu.with_memory_space_constraint(a, pltpu.HBM) for a in far], *near)
 
 
-def exchange(block):
-    return lax.all_to_all(block, ("gx", "gy"), split_axis=0, concat_axis=0, tiled=True)
+def exchange(blocks):
+    if len(blocks) == 1:
+        return [lax.all_to_all(blocks[0], ("gx", "gy"), split_axis=0, concat_axis=0, tiled=True)]
+    peers = len(blocks)
+    arrived = {0: blocks[0]}
+    for k in reversed(range(1, peers)):
+        arrived[k] = lax.ppermute(blocks[k], ("gx", "gy"), [(i, i ^ k) for i in range(peers)])
+    return [arrived[k] for k in range(peers)]
+
+
+def message(peers, rows, lanes):
+    if pairwise(peers):
+        return [jax.ShapeDtypeStruct((rows, lanes), jnp.float32)] * peers
+    return [jax.ShapeDtypeStruct((peers, rows, lanes), jnp.float32)]
 
 
 def from_behind(block, axis, distance):
@@ -288,9 +324,9 @@
     f32 = jnp.float32
     line = lambda a: a.reshape(1, -1)
     order, coarse_row = line(order), line(coarse_row)
-    outgoing, conf = call(
+    conf, *outgoing = call(
         functools.partial(pack_kernel, peers, cap, elements),
-        (jax.ShapeDtypeStruct((peers, cap, LANES), f32), jax.ShapeDtypeStruct((confs, LANES), f32)),
+        [jax.ShapeDtypeStruct((confs, LANES), f32), *message(peers, cap, LANES)],
         (
             line(mortar_dest),
             line(mortar_elem),
@@ -317,18 +353,18 @@
         scratch=[pltpu.VMEM((2, VARS * slots, CELL_PAD), f32)],
     )
     rows = call(
-        functools.partial(face_kernel, peers, row_cap, elements),
-        jax.ShapeDtypeStruct((peers, row_cap, VARS * ROW), f32),
+        functools.partial(face_kernel, peers, row_cap, elements, len(incoming)),
+        message(peers, row_cap, VARS * ROW),
         (),
-        (incoming, conf, y, cols, *face),
+        (*incoming, conf, y, cols, *face),
         scratch=[pltpu.VMEM((VARS * slots, FACES * FACE_PAD), f32)],
     )
     arrived = exchange(rows)
     return call(
-        functools.partial(place_kernel, peers, row_cap),
+        functools.partial(place_kernel, peers, row_cap, len(arrived)),
         jax.ShapeDtypeStruct((elements, VARS * ROW), f32),
         (),
-        (arrived, incoming),
+        (*arrived, *incoming),
     )
 
 

time: 31.3 us -> 37.3 us (1.19)
  starting transfers between devices: 7.3 us -> 23.9 us
  blocking collectives: 10 us -> 0 us
  Pallas kernels: 7.5 us -> 6.86 us
    ppermute x0 -> x14, starting transfers between devices: none -> 23.4 us  [exchange(): lax.ppermute(blocks[k], ('gx', 'gy'), [(i, i ^ k) for i in range(peers)])]
    all_to_all x1 -> x0, blocking collectives: 10 us -> none  [exchange(): lax.all_to_all(block, ('gx', 'gy'), split_axis=0, concat_axis=0, tiled=True)]
    all_to_all x1 -> x0, starting transfers between devices: 7.29 us -> none  [exchange(): lax.all_to_all(block, ('gx', 'gy'), split_axis=0, concat_axis=0, tiled=True)]
    ppermute x0 -> x14, waiting for transfers between devices: none -> 6.33 us  [exchange(): lax.ppermute(blocks[k], ('gx', 'gy'), [(i, i ^ k) for i in range(peers)])]
    all_to_all x1 -> x0, waiting for transfers between devices: 5.03 us -> none  [exchange(): lax.all_to_all(block, ('gx', 'gy'), split_axis=0, concat_axis=0, tiled=True)]
    ppermute x1, waiting for transfers between devices: 1.16 us -> 0.01 us  [from_behind(): return lax.ppermute(block, axis, route)]
    pallas_call x4, Pallas kernels: 7.5 us -> 6.86 us  [call(): pl.pallas_call(functools.partial(fetched, kernel, len(far), len(near), le...]
    ppermute x1, starting transfers between devices: 0.01 us -> 0.5 us  [from_behind(): return lax.ppermute(block, axis, route)]
  transfers between devices with their start and end apart: 2 -> 15, of which waited for: 2 -> 3; matrix products, arithmetic and copies ran while one was open for 0% -> 0% of each run, Pallas kernels for 8% -> 7%
where the time goes in v2:
time: 37.3 us; the launch traced here: 37.2 us
  starting transfers between devices  23.9 us (64%)
  Pallas kernels  6.86 us (18%)
  waiting for transfers between devices  6.33 us (17%)
    ppermute x14, starting transfers between devices, exchange(): lax.ppermute(blocks[k], ('gx', 'gy'), [(i, i ^ k) for i in range(peers)])  23.4 us
    pallas_call x4, Pallas kernels, call(): pl.pallas_call(functools.partial(fetched, kernel, len(far), len(near), le...  6.86 us
    ppermute x14, waiting for transfers between devices, exchange(): lax.ppermute(blocks[k], ('gx', 'gy'), [(i, i ^ k) for i in range(peers)])  6.33 us
  transfers between devices with their start and end apart: 15, of which 3 were waited for; matrix products, arithmetic and copies ran while one was open for 0% of the time, Pallas kernels for 7%

profile of v2, /device:TPU:0, one launch (start us, length us, event | category | flops | bytes accessed | tf_op | source)
XLA Modules:
  0.0 37.2 jit_solution(7340086911884743979)
XLA Ops:
  0.0 2.2 %shard_map.163 = (f32[64,256]{1,0:T(8,128)S(1)}, f32[24,256]{1,0:T(8,128)S(1)}, f32[24,256]{1,0:T(8,128)S(1)}, f32[24,256]{1,0:T(8,128)S(1)}, f32[24,256]{1,0:T(...) custom-call(s32[1,96]{1,0:T(1,128)} %bitcast.10, ...), custom_call_target="tpu_custom_call" | custom-call | bytes 1469696 | tf_op jit(solution)/shard_map/pallas_call | solution.py:270
  2.2 0.5 %collective-permute-start.7 = (f32[64,256]{1,0:T(8,128)S(1)}, f32[64,256]{1,0:T(8,128)S(1)}, u32[]{:S(2)}, u32[]{:S(2)}) collective-permute-start(f32[64,256]{1,0:T(8,128)S(1)} %get-tuple-element.34), channel_id=1, source_target_pairs={{3,0},{0,1},{1,2},{2,3},{7,4},{4,5},{5,6},{6,7},{11,8},{8,9},{9,10... | collective-permute-start | bytes 196616 | tf_op jit(solution)/shard_map/ppermute | solution.py:299
  2.7 2.6 %collective-permute-start = (f32[24,256]{1,0:T(8,128)S(1)}, f32[24,256]{1,0:T(8,128)S(1)}, u32[]{:S(2)}, u32[]{:S(2)}) collective-permute-start(f32[24,256]{1,0:T(8,128)S(1)} %get-tuple-element.27), channel_id=1, source_target_pairs={{0,4},{4,0},{8,12},{12,8},{16,20},{20,16},{24,28},{28,24},{1,5},{5... | collective-permute-start | bytes 73736 | tf_op jit(solution)/shard_map/ppermute | solution.py:286
  5.3 2.6 %collective-permute-start.1 = (f32[24,256]{1,0:T(8,128)S(1)}, f32[24,256]{1,0:T(8,128)S(1)}, u32[]{:S(2)}, u32[]{:S(2)}) collective-permute-start(f32[24,256]{1,0:T(8,128)S(1)} %get-tuple-element.28), channel_id=1, source_target_pairs={{0,8},{4,12},{8,0},{12,4},{16,24},{20,28},{24,16},{28,20},{1,9},{5... | collective-permute-start | bytes 73736 | tf_op jit(solution)/shard_map/ppermute | solution.py:286
  7.9 0.0 collective-permute-start.2
  7.9 1.7 %collective-permute-start.3 = (f32[24,256]{1,0:T(8,128)S(1)}, f32[24,256]{1,0:T(8,128)S(1)}, u32[]{:S(2)}, u32[]{:S(2)}) collective-permute-start(f32[24,256]{1,0:T(8,128)S(1)} %get-tuple-element.30), channel_id=1, source_target_pairs={{0,16},{4,20},{8,24},{12,28},{16,0},{20,4},{24,8},{28,12},{1,17},{... | collective-permute-start | bytes 73736 | tf_op jit(solution)/shard_map/ppermute | solution.py:286
  9.7 0.0 collective-permute-done.refs_1_.refs_9_
  9.7 0.6 %collective-permute-start.4 = (f32[24,256]{1,0:T(8,128)S(1)}, f32[24,256]{1,0:T(8,128)S(1)}, u32[]{:S(2)}, u32[]{:S(2)}) collective-permute-start(f32[24,256]{1,0:T(8,128)S(1)} %get-tuple-element.31), channel_id=1, source_target_pairs={{0,20},{4,16},{8,28},{12,24},{16,4},{20,0},{24,12},{28,8},{1,21},{... | collective-permute-start | bytes 73736 | tf_op jit(solution)/shard_map/ppermute | solution.py:286
  10.3 0.2 collective-permute-done.1.refs_2_.refs_10_
  10.4 4.3 %collective-permute-start.5 = (f32[24,256]{1,0:T(8,128)S(1)}, f32[24,256]{1,0:T(8,128)S(1)}, u32[]{:S(2)}, u32[]{:S(2)}) collective-permute-start(f32[24,256]{1,0:T(8,128)S(1)} %get-tuple-element.32), channel_id=1, source_target_pairs={{0,24},{4,28},{8,16},{12,20},{16,8},{20,12},{24,0},{28,4},{1,25},{... | collective-permute-start | bytes 73736 | tf_op jit(solution)/shard_map/ppermute | solution.py:286
  14.7 0.0 collective-permute-done.2.refs_3_.refs_11_
  14.7 0.3 collective-permute-start.6
  15.1 2.5 %shard_map.164 = (f32[160,216]{1,0:T(8,128)S(1)}, f32[32,128]{1,0:T(8,128)S(1)}, bf16[1920,216]{1,0:T(8,128)(2,1)S(1)}, bf16[1920,216]{1,0:T(8,128)(2,1)S(1)}) custom-call(s32[1,32]{1,0:T(1,128)} %bitcast.16, s32[1,32]{1,0:T(1,128)} %bitcast.9, f32[32,1715]{1,0:T(8,128)} %refs_2_.1, bf16[1920,216]{1,0:T(8,128)(2,1)} %constant.14.clone.refs_3_, ...), custom_call_target="tpu_custom_call" | custom-call | bytes 5351040 | tf_op jit(solution)/shard_map/pallas_call | solution.py:270
  17.6 0.0 collective-permute-done.3.refs_4_.refs_12_
  17.6 0.0 collective-permute-done.4.refs_5_.refs_13_
  17.6 0.0 collective-permute-done.5.refs_6_.refs_14_
  17.6 3.7 %collective-permute-done.6.refs_7_.refs_15_ = f32[24,256]{1,0:T(8,128)S(1)} collective-permute-done((f32[24,256]{1,0:T(8,128)S(1)}, f32[24,256]{1,0:T(8,128)S(1)}, u32[]{:S(2)}, u32[]{:S(2)}) %collective-permute-start.6) | collective-permute-done | bytes 24608 | tf_op jit(solution)/shard_map/ppermute | solution.py:286
  21.3 0.0 collective-permute-done.7.refs_8_
  21.3 1.2 %shard_map.165 = (f32[4,1080]{1,0:T(4,128)S(1)}, f32[4,1080]{1,0:T(4,128)S(1)}, f32[4,1080]{1,0:T(4,128)S(1)}, f32[4,1080]{1,0:T(4,128)S(1)}, f32[4,1080]{1,0:T(...) custom-call(f32[24,256]{1,0:T(8,128)S(1)} %get-tuple-element.26.refs_0_.refs_8_, ...), custom_call_target="tpu_custom_call" | custom-call | bytes 2213888 | tf_op jit(solution)/shard_map/pallas_call | solution.py:270
  22.5 0.1 collective-permute-start.8
  22.6 0.8 %collective-permute-start.9 = (f32[4,1080]{1,0:T(4,128)S(1)}, f32[4,1080]{1,0:T(4,128)S(1)}, u32[]{:S(2)}, u32[]{:S(2)}) collective-permute-start(f32[4,1080]{1,0:T(4,128)S(1)} %get-tuple-element.41), channel_id=1, source_target_pairs={{0,8},{4,12},{8,0},{12,4},{16,24},{20,28},{24,16},{28,20},{1,9},{5... | collective-permute-start | bytes 51848 | tf_op jit(solution)/shard_map/ppermute | solution.py:286
  23.4 3.6 %collective-permute-start.10 = (f32[4,1080]{1,0:T(4,128)S(1)}, f32[4,1080]{1,0:T(4,128)S(1)}, u32[]{:S(2)}, u32[]{:S(2)}) collective-permute-start(f32[4,1080]{1,0:T(4,128)S(1)} %get-tuple-element.42), channel_id=1, source_target_pairs={{0,12},{4,8},{8,4},{12,0},{16,28},{20,24},{24,20},{28,16},{1,13},{... | collective-permute-start | bytes 51848 | tf_op jit(solution)/shard_map/ppermute | solution.py:286
  27.0 0.7 %collective-permute-start.11 = (f32[4,1080]{1,0:T(4,128)S(1)}, f32[4,1080]{1,0:T(4,128)S(1)}, u32[]{:S(2)}, u32[]{:S(2)}) collective-permute-start(f32[4,1080]{1,0:T(4,128)S(1)} %get-tuple-element.43), channel_id=1, source_target_pairs={{0,16},{4,20},{8,24},{12,28},{16,0},{20,4},{24,8},{28,12},{1,17},{... | collective-permute-start | bytes 51848 | tf_op jit(solution)/shard_map/ppermute | solution.py:286
  27.7 0.0 collective-permute-start.12
  27.7 0.0 collective-permute-done.8.refs_1_
  27.7 2.1 %collective-permute-start.13 = (f32[4,1080]{1,0:T(4,128)S(1)}, f32[4,1080]{1,0:T(4,128)S(1)}, u32[]{:S(2)}, u32[]{:S(2)}) collective-permute-start(f32[4,1080]{1,0:T(4,128)S(1)} %get-tuple-element.45), channel_id=1, source_target_pairs={{0,24},{4,28},{8,16},{12,20},{16,8},{20,12},{24,0},{28,4},{1,25},{... | collective-permute-start | bytes 51848 | tf_op jit(solution)/shard_map/ppermute | solution.py:286
  29.8 0.0 collective-permute-done.9.refs_2_
  29.8 4.0 %collective-permute-start.14 = (f32[4,1080]{1,0:T(4,128)S(1)}, f32[4,1080]{1,0:T(4,128)S(1)}, u32[]{:S(2)}, u32[]{:S(2)}) collective-permute-start(f32[4,1080]{1,0:T(4,128)S(1)} %get-tuple-element.46), channel_id=1, source_target_pairs={{0,28},{4,24},{8,20},{12,16},{16,12},{20,8},{24,4},{28,0},{1,29},{... | collective-permute-start | bytes 51848 | tf_op jit(solution)/shard_map/ppermute | solution.py:286
  33.7 0.0 collective-permute-done.10.refs_3_
  33.7 0.0 collective-permute-done.13.refs_6_
  33.7 2.5 %collective-permute-done.14.refs_7_ = f32[4,1080]{1,0:T(4,128)S(1)} collective-permute-done((f32[4,1080]{1,0:T(4,128)S(1)}, f32[4,1080]{1,0:T(4,128)S(1)}, u32[]{:S(2)}, u32[]{:S(2)}) %collective-permute-start.14) | collective-permute-done | bytes 17312 | tf_op jit(solution)/shard_map/ppermute | solution.py:286
  36.2 0.9 %shard_map.166 = f32[32,1080]{1,0:T(8,128)} custom-call(f32[4,1080]{1,0:T(4,128)S(1)} %get-tuple-element.39.refs_0_, f32[4,1080]{1,0:T(4,128)S(1)} %collective-permute-done.8.refs_1_, f32[4,1080]{1,0:T(4,128)S(1)} %collective-permute-done.9.refs_2_, f32[4,1080]{1,0:T(4,128)S(1)} %collective-permute-done.10.refs_3_, ...), custom_call_target="tpu_custom_call" | custom-call | bytes 473088 | tf_op jit(solution)/shard_map/pallas_call | solution.py:270
  (2 shorter events, 0.0 us)
Async XLA Ops:
  2.2 19.1 %collective-permute-start.7 = (f32[64,256]{1,0:T(8,128)S(1)}, f32[64,256]{1,0:T(8,128)S(1)}, u32[]{:S(2)}, u32[]{:S(2)}) collective-permute-start(f32[64,256]{1,0:T(8,128)S(1)} %get-tuple-element.34), channel_id=1, source_target_pairs={{3,0},{0,1},{1,2},{2,3},{7,4},{4,5},{5,6},{6,7},{11,8},{8,9},{9,10... | collective-permute-start | bytes 196616 | tf_op jit(solution)/shard_map/ppermute | solution.py:299
  2.7 7.0 %collective-permute-start = (f32[24,256]{1,0:T(8,128)S(1)}, f32[24,256]{1,0:T(8,128)S(1)}, u32[]{:S(2)}, u32[]{:S(2)}) collective-permute-start(f32[24,256]{1,0:T(8,128)S(1)} %get-tuple-element.27), channel_id=1, source_target_pairs={{0,4},{4,0},{8,12},{12,8},{16,20},{20,16},{24,28},{28,24},{1,5},{5... | collective-permute-start | bytes 73736 | tf_op jit(solution)/shard_map/ppermute | solution.py:286
  5.3 5.1 %collective-permute-start.1 = (f32[24,256]{1,0:T(8,128)S(1)}, f32[24,256]{1,0:T(8,128)S(1)}, u32[]{:S(2)}, u32[]{:S(2)}) collective-permute-start(f32[24,256]{1,0:T(8,128)S(1)} %get-tuple-element.28), channel_id=1, source_target_pairs={{0,8},{4,12},{8,0},{12,4},{16,24},{20,28},{24,16},{28,20},{1,9},{5... | collective-permute-start | bytes 73736 | tf_op jit(solution)/shard_map/ppermute | solution.py:286
  7.9 6.8 %collective-permute-start.2 = (f32[24,256]{1,0:T(8,128)S(1)}, f32[24,256]{1,0:T(8,128)S(1)}, u32[]{:S(2)}, u32[]{:S(2)}) collective-permute-start(f32[24,256]{1,0:T(8,128)S(1)} %get-tuple-element.29), channel_id=1, source_target_pairs={{0,12},{4,8},{8,4},{12,0},{16,28},{20,24},{24,20},{28,16},{1,13},{... | collective-permute-start | bytes 73736 | tf_op jit(solution)/shard_map/ppermute | solution.py:286
  7.9 9.7 %collective-permute-start.3 = (f32[24,256]{1,0:T(8,128)S(1)}, f32[24,256]{1,0:T(8,128)S(1)}, u32[]{:S(2)}, u32[]{:S(2)}) collective-permute-start(f32[24,256]{1,0:T(8,128)S(1)} %get-tuple-element.30), channel_id=1, source_target_pairs={{0,16},{4,20},{8,24},{12,28},{16,0},{20,4},{24,8},{28,12},{1,17},{... | collective-permute-start | bytes 73736 | tf_op jit(solution)/shard_map/ppermute | solution.py:286
  9.7 7.9 %collective-permute-start.4 = (f32[24,256]{1,0:T(8,128)S(1)}, f32[24,256]{1,0:T(8,128)S(1)}, u32[]{:S(2)}, u32[]{:S(2)}) collective-permute-start(f32[24,256]{1,0:T(8,128)S(1)} %get-tuple-element.31), channel_id=1, source_target_pairs={{0,20},{4,16},{8,28},{12,24},{16,4},{20,0},{24,12},{28,8},{1,21},{... | collective-permute-start | bytes 73736 | tf_op jit(solution)/shard_map/ppermute | solution.py:286
  10.4 7.1 %collective-permute-start.5 = (f32[24,256]{1,0:T(8,128)S(1)}, f32[24,256]{1,0:T(8,128)S(1)}, u32[]{:S(2)}, u32[]{:S(2)}) collective-permute-start(f32[24,256]{1,0:T(8,128)S(1)} %get-tuple-element.32), channel_id=1, source_target_pairs={{0,24},{4,28},{8,16},{12,20},{16,8},{20,12},{24,0},{28,4},{1,25},{... | collective-permute-start | bytes 73736 | tf_op jit(solution)/shard_map/ppermute | solution.py:286
  14.7 6.5 %collective-permute-start.6 = (f32[24,256]{1,0:T(8,128)S(1)}, f32[24,256]{1,0:T(8,128)S(1)}, u32[]{:S(2)}, u32[]{:S(2)}) collective-permute-start(f32[24,256]{1,0:T(8,128)S(1)} %get-tuple-element.33), channel_id=1, source_target_pairs={{0,28},{4,24},{8,20},{12,16},{16,12},{20,8},{24,4},{28,0},{1,29},{... | collective-permute-start | bytes 73736 | tf_op jit(solution)/shard_map/ppermute | solution.py:286
  22.5 5.1 %collective-permute-start.8 = (f32[4,1080]{1,0:T(4,128)S(1)}, f32[4,1080]{1,0:T(4,128)S(1)}, u32[]{:S(2)}, u32[]{:S(2)}) collective-permute-start(f32[4,1080]{1,0:T(4,128)S(1)} %get-tuple-element.40), channel_id=1, source_target_pairs={{0,4},{4,0},{8,12},{12,8},{16,20},{20,16},{24,28},{28,24},{1,5},{5... | collective-permute-start | bytes 51848 | tf_op jit(solution)/shard_map/ppermute | solution.py:286
  22.6 7.2 %collective-permute-start.9 = (f32[4,1080]{1,0:T(4,128)S(1)}, f32[4,1080]{1,0:T(4,128)S(1)}, u32[]{:S(2)}, u32[]{:S(2)}) collective-permute-start(f32[4,1080]{1,0:T(4,128)S(1)} %get-tuple-element.41), channel_id=1, source_target_pairs={{0,8},{4,12},{8,0},{12,4},{16,24},{20,28},{24,16},{28,20},{1,9},{5... | collective-permute-start | bytes 51848 | tf_op jit(solution)/shard_map/ppermute | solution.py:286
  23.4 10.4 %collective-permute-start.10 = (f32[4,1080]{1,0:T(4,128)S(1)}, f32[4,1080]{1,0:T(4,128)S(1)}, u32[]{:S(2)}, u32[]{:S(2)}) collective-permute-start(f32[4,1080]{1,0:T(4,128)S(1)} %get-tuple-element.42), channel_id=1, source_target_pairs={{0,12},{4,8},{8,4},{12,0},{16,28},{20,24},{24,20},{28,16},{1,13},{... | collective-permute-start | bytes 51848 | tf_op jit(solution)/shard_map/ppermute | solution.py:286
  27.0 6.8 %collective-permute-start.11 = (f32[4,1080]{1,0:T(4,128)S(1)}, f32[4,1080]{1,0:T(4,128)S(1)}, u32[]{:S(2)}, u32[]{:S(2)}) collective-permute-start(f32[4,1080]{1,0:T(4,128)S(1)} %get-tuple-element.43), channel_id=1, source_target_pairs={{0,16},{4,20},{8,24},{12,28},{16,0},{20,4},{24,8},{28,12},{1,17},{... | collective-permute-start | bytes 51848 | tf_op jit(solution)/shard_map/ppermute | solution.py:286
  27.7 6.1 %collective-permute-start.12 = (f32[4,1080]{1,0:T(4,128)S(1)}, f32[4,1080]{1,0:T(4,128)S(1)}, u32[]{:S(2)}, u32[]{:S(2)}) collective-permute-start(f32[4,1080]{1,0:T(4,128)S(1)} %get-tuple-element.44), channel_id=1, source_target_pairs={{0,20},{4,16},{8,28},{12,24},{16,4},{20,0},{24,12},{28,8},{1,21},{... | collective-permute-start | bytes 51848 | tf_op jit(solution)/shard_map/ppermute | solution.py:286
  27.7 6.1 %collective-permute-start.13 = (f32[4,1080]{1,0:T(4,128)S(1)}, f32[4,1080]{1,0:T(4,128)S(1)}, u32[]{:S(2)}, u32[]{:S(2)}) collective-permute-start(f32[4,1080]{1,0:T(4,128)S(1)} %get-tuple-element.45), channel_id=1, source_target_pairs={{0,24},{4,28},{8,16},{12,20},{16,8},{20,12},{24,0},{28,4},{1,25},{... | collective-permute-start | bytes 51848 | tf_op jit(solution)/shard_map/ppermute | solution.py:286
  29.8 6.5 %collective-permute-start.14 = (f32[4,1080]{1,0:T(4,128)S(1)}, f32[4,1080]{1,0:T(4,128)S(1)}, u32[]{:S(2)}, u32[]{:S(2)}) collective-permute-start(f32[4,1080]{1,0:T(4,128)S(1)} %get-tuple-element.46), channel_id=1, source_target_pairs={{0,28},{4,24},{8,20},{12,16},{16,12},{20,8},{24,4},{28,0},{1,29},{... | collective-permute-start | bytes 51848 | tf_op jit(solution)/shard_map/ppermute | solution.py:286

commit v3 on v2

--- a/solution.py
+++ b/solution.py
@@ -99,14 +99,12 @@
     return dot(member.astype(jnp.bfloat16), before.astype(jnp.bfloat16))
 
 
-def pairwise(peers):
-    return peers <= 8 and peers & (peers - 1) == 0
-
-
-def own_index(peers):
-    if not pairwise(peers):
-        return 0
-    return lax.axis_index("gx") * lax.axis_size("gy") + lax.axis_index("gy")
+def two_level():
+    return lax.axis_size("gx") == 2
+
+
+def own_index():
+    return lax.axis_index("gx") * lax.axis_size("gy") if two_level() else 0
 
 
 def owner_of(crow, peers, elements, me):
@@ -115,7 +113,7 @@
 
 
 def row_places(crow, peers, elements, stride):
-    me = own_index(peers)
+    me = own_index()
     member = owner_of(crow, peers, elements, me)
     rank = earlier(member)
     block = iota(member.shape, 0)
@@ -144,7 +142,7 @@
     dest, elem, face, sub, crow, cface, celem = [get(i) for i in range(7)]
     count = dest.shape[1]
     rows = peers * cap
-    member = ((iota((peers, count), 0) ^ own_index(peers)) == dest).astype(jnp.float32)
+    member = ((iota((peers, count), 0) ^ own_index()) == dest).astype(jnp.float32)
     base = iota(member.shape, 0).astype(jnp.float32) * cap
     place = jnp.sum(member * (base + earlier(member)), axis=0, keepdims=True)
     put = onehot_rows(place, rows)
@@ -164,11 +162,8 @@
     lane = iota((rows, LANES), 1)
     packed = jnp.where(lane == TAG_FACE, code_col, packed)
     packed = jnp.where(lane == TAG_ROW, row_col, packed)
-    if len(outs) > 1:
-        for k, out in enumerate(outs):
-            out[...] = packed[k * cap : (k + 1) * cap]
-    else:
-        outs[0][...] = packed.reshape(peers, cap, LANES)
+    for out, part in zip(outs, jnp.split(packed, len(outs))):
+        out[...] = part.reshape(out.shape)
     confs = cface.shape[1]
     eye = (iota((confs, confs), 0) == iota((confs, confs), 1)).astype(jnp.float32)
     conf_col = column(eye, (cface * elements + celem + 1).astype(jnp.float32))
@@ -226,12 +221,9 @@
     high, low = halves(wide)
     total = y[...] + dot3(high, low, table_high[...], table_low[...])
     for v in range(VARS):
-        part = total[v * slots : (v + 1) * slots]
-        if len(outs) > 1:
-            for k, out in enumerate(outs):
-                out[:, v * ROW : (v + 1) * ROW] = part[k * row_cap : (k + 1) * row_cap]
-        else:
-            outs[0][:, :, v * ROW : (v + 1) * ROW] = part.reshape(peers, row_cap, ROW)
+        parts = jnp.split(total[v * slots : (v + 1) * slots], len(outs))
+        for out, part in zip(outs, parts):
+            out[:, :, v * ROW : (v + 1) * ROW] = part.reshape(-1, row_cap, ROW)
 
 
 def place_kernel(peers, row_cap, blocks, get, *refs):
@@ -280,17 +272,15 @@
 def exchange(blocks):
     if len(blocks) == 1:
         return [lax.all_to_all(blocks[0], ("gx", "gy"), split_axis=0, concat_axis=0, tiled=True)]
-    peers = len(blocks)
-    arrived = {0: blocks[0]}
-    for k in reversed(range(1, peers)):
-        arrived[k] = lax.ppermute(blocks[k], ("gx", "gy"), [(i, i ^ k) for i in range(peers)])
-    return [arrived[k] for k in range(peers)]
-
-
-def message(peers, rows, lanes):
-    if pairwise(peers):
-        return [jax.ShapeDtypeStruct((rows, lanes), jnp.float32)] * peers
-    return [jax.ShapeDtypeStruct((peers, rows, lanes), jnp.float32)]
+    near, far = blocks
+    far = lax.ppermute(far, "gx", [(0, 1), (1, 0)])
+    return [lax.all_to_all(block, "gy", split_axis=0, concat_axis=0, tiled=True) for block in (near, far)]
+
+
+def message(rows, lanes):
+    size_x, size_y = lax.axis_size("gx"), lax.axis_size("gy")
+    blocks = 2 if two_level() else 1
+    return [jax.ShapeDtypeStruct((size_x * size_y // blocks, rows, lanes), jnp.float32)] * blocks
 
 
 def from_behind(block, axis, distance):
@@ -326,7 +316,7 @@
     order, coarse_row = line(order), line(coarse_row)
     conf, *outgoing = call(
         functools.partial(pack_kernel, peers, cap, elements),
-        [jax.ShapeDtypeStruct((confs, LANES), f32), *message(peers, cap, LANES)],
+        [jax.ShapeDtypeStruct((confs, LANES), f32), *message(cap, LANES)],
         (
             line(mortar_dest),
             line(mortar_elem),
@@ -354,7 +344,7 @@
     )
     rows = call(
         functools.partial(face_kernel, peers, row_cap, elements, len(incoming)),
-        message(peers, row_cap, VARS * ROW),
+        message(row_cap, VARS * ROW),
         (),
         (*incoming, conf, y, cols, *face),
         scratch=[pltpu.VMEM((VARS * slots, FACES * FACE_PAD), f32)],

time: 37.3 us -> 46.3 us (1.24)
  blocking collectives: 0 us -> 9.24 us
  starting transfers between devices: 23.9 us -> 16.7 us
  waiting for transfers between devices: 6.33 us -> 11.8 us
  Pallas kernels: 6.86 us -> 8.08 us
    ppermute x14 -> x2, starting transfers between devices: 23.4 us -> 3.1 us  [exchange(): far = lax.ppermute(far, 'gx', [(0, 1), (1, 0)])]
    all_to_all x0 -> x3, starting transfers between devices: none -> 13.6 us  [exchange(): lax.all_to_all(block, 'gy', split_axis=0, concat_axis=0, tiled=True)]
    all_to_all x0 -> x1, blocking collectives: none -> 9.24 us  [exchange(): lax.all_to_all(block, 'gy', split_axis=0, concat_axis=0, tiled=True)]
    all_to_all x0 -> x3, waiting for transfers between devices: none -> 4.56 us  [exchange(): lax.all_to_all(block, 'gy', split_axis=0, concat_axis=0, tiled=True)]
    pallas_call x4, Pallas kernels: 6.86 us -> 8.08 us  [call(): pl.pallas_call(functools.partial(fetched, kernel, len(far), len(near), le...]
    ppermute x1, waiting for transfers between devices: 0.01 us -> 1.17 us  [from_behind(): return lax.ppermute(block, axis, route)]
    ppermute x1, starting transfers between devices: 0.5 us -> 0.01 us  [from_behind(): return lax.ppermute(block, axis, route)]
    ppermute x14 -> x2, waiting for transfers between devices: 6.33 us -> 6.04 us  [exchange(): far = lax.ppermute(far, 'gx', [(0, 1), (1, 0)])]
  transfers between devices with their start and end apart: 15 -> 6, of which waited for: 3 -> 6; matrix products, arithmetic and copies ran while one was open for 0% -> 0% of each run, Pallas kernels for 7% -> 5%
where the time goes in v3:
time: 46.3 us; the launch traced here: 45.9 us
  starting transfers between devices  16.7 us (36%)
  waiting for transfers between devices  11.8 us (25%)
  blocking collectives  9.24 us (20%)
  Pallas kernels  8.08 us (17%)
    all_to_all x3, starting transfers between devices, exchange(): lax.all_to_all(block, 'gy', split_axis=0, concat_axis=0, tiled=True)  13.6 us
    all_to_all x1, blocking collectives, exchange(): lax.all_to_all(block, 'gy', split_axis=0, concat_axis=0, tiled=True)  9.24 us
    pallas_call x4, Pallas kernels, call(): pl.pallas_call(functools.partial(fetched, kernel, len(far), len(near), le...  8.08 us
    ppermute x2, waiting for transfers between devices, exchange(): far = lax.ppermute(far, 'gx', [(0, 1), (1, 0)])  6.04 us
    all_to_all x3, waiting for transfers between devices, exchange(): lax.all_to_all(block, 'gy', split_axis=0, concat_axis=0, tiled=True)  4.56 us
    ppermute x2, starting transfers between devices, exchange(): far = lax.ppermute(far, 'gx', [(0, 1), (1, 0)])  3.1 us
    ppermute x1, waiting for transfers between devices, from_behind(): return lax.ppermute(block, axis, route)  1.17 us
  transfers between devices with their start and end apart: 6, of which 6 were waited for; matrix products, arithmetic and copies ran while one was open for 0% of the time, Pallas kernels for 5%

profile of v3, /device:TPU:0, one launch (start us, length us, event | category | flops | bytes accessed | tf_op | source)
XLA Modules:
  0.0 45.9 jit_solution(11780146294131040343)
XLA Ops:
  0.0 2.8 %shard_map.163 = (f32[64,256]{1,0:T(8,128)S(1)}, f32[4,24,256]{2,1,0:T(8,128)}, f32[4,24,256]{2,1,0:T(8,128)S(1)}) custom-call(s32[1,96]{1,0:T(1,128)} %bitcast.10, s32[1,96]{1,0:T(1,128)} %bitcast.11, s32[1,96]{1,0:T(1,128)} %bitcast.12, s32[1,96]{1,0:T(1,128)} %bitcast.13, s32[1,32]{1,0:T(1,128)} %bitcast.8, s32[1,64]{1,0:T(1,128)} %bitcast.14, ...), custom_call_target="tpu_custom_call" | custom-call | bytes 1469696 | tf_op jit(solution)/shard_map/pallas_call | solution.py:262
  2.8 6.3 %all-to-all-start = ((f32[4,24,256]{2,1,0:T(8,128)}), f32[4,24,256]{2,1,0:T(8,128)S(1)}, u32[]{:S(2)}, u32[]{:S(2)}) async-start(f32[4,24,256]{2,1,0:T(8,128)} %get-tuple-element.14), calls=%async_computation | async-start | bytes 196608 | tf_op jit(solution)/shard_map/all_to_all | solution.py:277
  9.1 1.5 %collective-permute-start = (f32[4,24,256]{2,1,0:T(8,128)S(1)}, f32[4,24,256]{2,1,0:T(8,128)}, u32[]{:S(2)}, u32[]{:S(2)}) collective-permute-start(f32[4,24,256]{2,1,0:T(8,128)S(1)} %get-tuple-element.15), channel_id=1, source_target_pairs={{0,16},{16,0},{1,17},{17,1},{2,18},{18,2},{3,19},{19,3},{4,20},{20... | collective-permute-start | bytes 294920 | tf_op jit(solution)/shard_map/ppermute | solution.py:276
  10.6 3.2 %collective-permute-done = f32[4,24,256]{2,1,0:T(8,128)} collective-permute-done((f32[4,24,256]{2,1,0:T(8,128)S(1)}, f32[4,24,256]{2,1,0:T(8,128)}, u32[]{:S(2)}, u32[]{:S(2)}) %collective-permute-start) | collective-permute-done | bytes 98336 | tf_op jit(solution)/shard_map/ppermute | solution.py:276
  13.8 1.1 %all-to-all-done.refs_0_.refs_2_ = f32[4,24,256]{2,1,0:T(8,128)S(1)} async-done(((f32[4,24,256]{2,1,0:T(8,128)}), f32[4,24,256]{2,1,0:T(8,128)S(1)}, u32[]{:S(2)}, u32[]{:S(2)}) %all-to-all-start) | async-done | bytes 98336 | tf_op jit(solution)/shard_map/all_to_all | solution.py:277
  15.0 4.0 %all-to-all-start.1 = ((f32[4,24,256]{2,1,0:T(8,128)}), f32[4,24,256]{2,1,0:T(8,128)S(1)}, u32[]{:S(2)}, u32[]{:S(2)}) async-start(f32[4,24,256]{2,1,0:T(8,128)} %collective-permute-done), calls=%async_computation.1 | async-start | bytes 196608 | tf_op jit(solution)/shard_map/all_to_all | solution.py:277
  18.9 0.0 collective-permute-start.1
  18.9 2.5 %shard_map.164 = (f32[160,216]{1,0:T(8,128)S(1)}, f32[32,128]{1,0:T(8,128)S(1)}, bf16[1920,216]{1,0:T(8,128)(2,1)S(1)}, bf16[1920,216]{1,0:T(8,128)(2,1)S(1)}) custom-call(s32[1,32]{1,0:T(1,128)} %bitcast.16, s32[1,32]{1,0:T(1,128)} %bitcast.9, f32[32,1715]{1,0:T(8,128)} %refs_2_.1, bf16[1920,216]{1,0:T(8,128)(2,1)} %constant.14.clone.refs_3_, ...), custom_call_target="tpu_custom_call" | custom-call | bytes 5351040 | tf_op jit(solution)/shard_map/pallas_call | solution.py:262
  21.5 1.2 %collective-permute-done.1.refs_2_ = f32[64,256]{1,0:T(8,128)S(1)} collective-permute-done((f32[64,256]{1,0:T(8,128)S(1)}, f32[64,256]{1,0:T(8,128)S(1)}, u32[]{:S(2)}, u32[]{:S(2)}) %collective-permute-start.1) | collective-permute-done | bytes 65568 | tf_op jit(solution)/shard_map/ppermute | solution.py:289
  22.6 2.1 %all-to-all-done.1.refs_1_.refs_3_ = f32[4,24,256]{2,1,0:T(8,128)S(1)} async-done(((f32[4,24,256]{2,1,0:T(8,128)}), f32[4,24,256]{2,1,0:T(8,128)S(1)}, u32[]{:S(2)}, u32[]{:S(2)}) %all-to-all-start.1) | async-done | bytes 98336 | tf_op jit(solution)/shard_map/all_to_all | solution.py:277
  24.8 1.8 %shard_map.165 = (f32[4,4,1080]{2,1,0:T(4,128)}, f32[4,4,1080]{2,1,0:T(4,128)S(1)}) custom-call(f32[4,24,256]{2,1,0:T(8,128)S(1)} %all-to-all-done.refs_0_.refs_2_, f32[4,24,256]{2,1,0:T(8,128)S(1)} %all-to-all-done.1.refs_1_.refs_3_, f32[64,256]{1,0:T(8,128)S(1)} %collective-permute-done.1.refs_2_, f32[160,216]{1,0:T(8,128)S(1)} %get-tuple-element.17.refs_3_, ...), custom_call_target="tpu_custom_call" | custom-call | bytes 2213888 | tf_op jit(solution)/shard_map/pallas_call | solution.py:262
  26.6 3.3 %all-to-all-start.2 = ((f32[4,4,1080]{2,1,0:T(4,128)}), f32[4,4,1080]{2,1,0:T(4,128)S(1)}, u32[]{:S(2)}, u32[]{:S(2)}) async-start(f32[4,4,1080]{2,1,0:T(4,128)} %get-tuple-element.21), calls=%async_computation.2 | async-start | bytes 147456 | tf_op jit(solution)/shard_map/all_to_all | solution.py:277
  29.9 1.6 %collective-permute-start.2 = (f32[4,4,1080]{2,1,0:T(4,128)S(1)}, f32[4,4,1080]{2,1,0:T(4,128)S(1)}, u32[]{:S(2)}, u32[]{:S(2)}) collective-permute-start(f32[4,4,1080]{2,1,0:T(4,128)S(1)} %get-tuple-element.22), channel_id=1, source_target_pairs={{0,16},{16,0},{1,17},{17,1},{2,18},{18,2},{3,19},{19,3},{4,20},{20... | collective-permute-start | bytes 207368 | tf_op jit(solution)/shard_map/ppermute | solution.py:276
  31.5 2.8 %collective-permute-done.2 = f32[4,4,1080]{2,1,0:T(4,128)S(1)} collective-permute-done((f32[4,4,1080]{2,1,0:T(4,128)S(1)}, f32[4,4,1080]{2,1,0:T(4,128)S(1)}, u32[]{:S(2)}, u32[]{:S(2)}) %collective-permute-start.2) | collective-permute-done | bytes 69152 | tf_op jit(solution)/shard_map/ppermute | solution.py:276
  34.4 1.3 %all-to-all-done.2.refs_0_ = f32[4,4,1080]{2,1,0:T(4,128)S(1)} async-done(((f32[4,4,1080]{2,1,0:T(4,128)}), f32[4,4,1080]{2,1,0:T(4,128)S(1)}, u32[]{:S(2)}, u32[]{:S(2)}) %all-to-all-start.2) | async-done | bytes 69152 | tf_op jit(solution)/shard_map/all_to_all | solution.py:277
  35.7 9.2 %all_to_all.20.refs_1_ = f32[4,4,1080]{2,1,0:T(4,128)S(1)} all-to-all(f32[4,4,1080]{2,1,0:T(4,128)S(1)} %collective-permute-done.2), channel_id=1, replica_groups=mesh['gx'=2,'gy'=4,'gz'=4] {'gy'}, dimensions={0} | all-to-all | bytes 138240 | tf_op jit(solution)/shard_map/all_to_all | solution.py:277
  44.9 0.9 %shard_map.166 = f32[32,1080]{1,0:T(8,128)} custom-call(f32[4,4,1080]{2,1,0:T(4,128)S(1)} %all-to-all-done.2.refs_0_, f32[4,4,1080]{2,1,0:T(4,128)S(1)} %all_to_all.20.refs_1_, f32[4,24,256]{2,1,0:T(8,128)S(1)} %all-to-all-done.refs_0_.refs_2_, f32[4,24,256]{2,1,0:T(8,128)S(1)} %all-to-all-done.1.refs_1_.refs_3_), custom_call_target="tpu_custom_call" | custom-call | bytes 473088 | tf_op jit(solution)/shard_map/pallas_call | solution.py:262
Async XLA Ops:
  2.8 12.2 %all-to-all-start = ((f32[4,24,256]{2,1,0:T(8,128)}), f32[4,24,256]{2,1,0:T(8,128)S(1)}, u32[]{:S(2)}, u32[]{:S(2)}) async-start(f32[4,24,256]{2,1,0:T(8,128)} %get-tuple-element.14), calls=%async_computation | async-start | bytes 196608 | tf_op jit(solution)/shard_map/all_to_all | solution.py:277
  9.1 4.7 %collective-permute-start = (f32[4,24,256]{2,1,0:T(8,128)S(1)}, f32[4,24,256]{2,1,0:T(8,128)}, u32[]{:S(2)}, u32[]{:S(2)}) collective-permute-start(f32[4,24,256]{2,1,0:T(8,128)S(1)} %get-tuple-element.15), channel_id=1, source_target_pairs={{0,16},{16,0},{1,17},{17,1},{2,18},{18,2},{3,19},{19,3},{4,20},{20... | collective-permute-start | bytes 294920 | tf_op jit(solution)/shard_map/ppermute | solution.py:276
  15.0 9.8 %all-to-all-start.1 = ((f32[4,24,256]{2,1,0:T(8,128)}), f32[4,24,256]{2,1,0:T(8,128)S(1)}, u32[]{:S(2)}, u32[]{:S(2)}) async-start(f32[4,24,256]{2,1,0:T(8,128)} %collective-permute-done), calls=%async_computation.1 | async-start | bytes 196608 | tf_op jit(solution)/shard_map/all_to_all | solution.py:277
  18.9 3.7 %collective-permute-start.1 = (f32[64,256]{1,0:T(8,128)S(1)}, f32[64,256]{1,0:T(8,128)S(1)}, u32[]{:S(2)}, u32[]{:S(2)}) collective-permute-start(f32[64,256]{1,0:T(8,128)S(1)} %get-tuple-element.16), channel_id=1, source_target_pairs={{3,0},{0,1},{1,2},{2,3},{7,4},{4,5},{5,6},{6,7},{11,8},{8,9},{9,10... | collective-permute-start | bytes 196616 | tf_op jit(solution)/shard_map/ppermute | solution.py:289
  26.6 9.0 %all-to-all-start.2 = ((f32[4,4,1080]{2,1,0:T(4,128)}), f32[4,4,1080]{2,1,0:T(4,128)S(1)}, u32[]{:S(2)}, u32[]{:S(2)}) async-start(f32[4,4,1080]{2,1,0:T(4,128)} %get-tuple-element.21), calls=%async_computation.2 | async-start | bytes 147456 | tf_op jit(solution)/shard_map/all_to_all | solution.py:277
  29.9 4.4 %collective-permute-start.2 = (f32[4,4,1080]{2,1,0:T(4,128)S(1)}, f32[4,4,1080]{2,1,0:T(4,128)S(1)}, u32[]{:S(2)}, u32[]{:S(2)}) collective-permute-start(f32[4,4,1080]{2,1,0:T(4,128)S(1)} %get-tuple-element.22), channel_id=1, source_target_pairs={{0,16},{16,0},{1,17},{17,1},{2,18},{18,2},{3,19},{19,3},{4,20},{20... | collective-permute-start | bytes 207368 | tf_op jit(solution)/shard_map/ppermute | solution.py:276

commit v4 on v1

--- a/solution.py
+++ b/solution.py
@@ -22,6 +22,7 @@
 TAG_ROW = TRACE + 1
 CELL_PAD = 384
 FACE_PAD = 64
+ROWS_PAD = 1152
 
 
 def grid_nodes(degree):
@@ -121,6 +122,16 @@
     return jnp.sum(onehot * values, axis=1, keepdims=True)
 
 
+def lift_traces(trace, sub, table_high, table_low):
+    count = trace.shape[0]
+    eye = (iota((count, count), 0) == iota((count, count), 1)).astype(jnp.float32)
+    sub_col = column(eye, sub.astype(jnp.float32))
+    x = jnp.concatenate([trace, jnp.zeros((count, LANES - TRACE), jnp.float32)], axis=1)
+    wide = jnp.concatenate([jnp.where(sub_col == float(s), x, 0.0) for s in range(4)], axis=1)
+    high, low = halves(wide)
+    return dot3(high, low, table_high, table_low)
+
+
 def pack_kernel(
     peers,
     cap,
@@ -140,13 +151,7 @@
     code_col = column(put, code)
     row_place, row_slot = row_places(crow, peers, elements, cap)
     row_col = column(onehot_rows(row_place, rows), row_slot + 1.0)
-    eye = (iota((count, count), 0) == iota((count, count), 1)).astype(jnp.float32)
-    sub_col = column(eye, sub.astype(jnp.float32))
-    x = jnp.concatenate([get(7), jnp.zeros((count, LANES - TRACE), jnp.float32)], axis=1)
-    wide = jnp.concatenate([jnp.where(sub_col == float(s), x, 0.0) for s in range(4)], axis=1)
-    high, low = halves(wide)
-    lifted = dot3(high, low, get(9), get(10))
-    lifted_high, lifted_low = halves(lifted)
+    lifted_high, lifted_low = halves(lift_traces(get(7), sub, get(9), get(10)))
     put = put.astype(jnp.bfloat16)
     packed = dot(put, lifted_high) + dot(put, lifted_low)
     lane = iota((rows, LANES), 1)
@@ -160,7 +165,38 @@
     conf_out[...] = jnp.where(iota((confs, LANES), 1) == TAG_FACE, conf_col, c)
 
 
-def cell_kernel(peers, row_cap, get, y_out, col_out, face_high, face_low, spread):
+def restrict_cells(take, order_col, adjoint, table_high, table_low, spread):
+    slots = take.shape[0]
+    take = take.astype(jnp.bfloat16)
+    spread[...] = jnp.zeros_like(spread)
+    for half, part in enumerate(halves(adjoint)):
+        moved = dot(take, part)
+        for v in range(VARS):
+            spread[half, v * slots : (v + 1) * slots, :CELL] = moved[:, v * CELL : (v + 1) * CELL]
+    order_rows = jnp.concatenate([order_col] * VARS, axis=0)
+    wide = [
+        jnp.concatenate([jnp.where(order_rows == float(p), spread[half], 0.0).astype(jnp.bfloat16) for p in ORDERS], axis=1)
+        for half in range(2)
+    ]
+    return dot3(*wide, table_high[...], table_low[...])
+
+
+def restrict_faces(face_sum, order_col, table_high, table_low, spread):
+    slots = order_col.shape[0]
+    spread[...] = jnp.zeros_like(spread)
+    for f in range(FACES):
+        for v in range(VARS):
+            spread[v * slots : (v + 1) * slots, f * FACE_PAD : f * FACE_PAD + FACE] = face_sum[
+                f * slots : (f + 1) * slots, v * FACE : (v + 1) * FACE
+            ]
+    order_rows = jnp.concatenate([order_col] * VARS, axis=0)
+    z = spread[...]
+    wide = jnp.concatenate([jnp.where(order_rows == float(p), z, 0.0) for p in ORDERS], axis=1)
+    high, low = halves(wide)
+    return dot3(high, low, table_high[...], table_low[...])
+
+
+def cell_kernel(peers, row_cap, get, y_out, col_out, spread):
     order, crow = get(0), get(1)
     elements = order.shape[1]
     slots = peers * row_cap
@@ -170,19 +206,7 @@
     elem_col = column(take, iota((1, elements), 1).astype(jnp.float32) + 1.0)
     lane = iota((slots, 128), 1)
     col_out[...] = jnp.where(lane == 0, order_col, jnp.where(lane == 1, elem_col, 0.0))
-    take = take.astype(jnp.bfloat16)
-    spread[...] = jnp.zeros_like(spread)
-    for half, part in enumerate(halves(get(2))):
-        moved = dot(take, part)
-        for v in range(VARS):
-            spread[half, v * slots : (v + 1) * slots, :CELL] = moved[:, v * CELL : (v + 1) * CELL]
-    order_rows = jnp.concatenate([order_col] * VARS, axis=0)
-    high, low = spread[0], spread[1]
-    wide_high = jnp.concatenate([jnp.where(order_rows == float(p), high, 0.0).astype(jnp.bfloat16) for p in ORDERS], axis=1)
-    wide_low = jnp.concatenate([jnp.where(order_rows == float(p), low, 0.0).astype(jnp.bfloat16) for p in ORDERS], axis=1)
-    y_out[...] = dot3(wide_high, wide_low, get(3), get(4))
-    face_high[...] = get(5)
-    face_low[...] = get(6)
+    y_out[...] = restrict_cells(take, order_col, get(2), get(3), get(4), spread)
 
 
 def face_kernel(peers, row_cap, elements, get, incoming, conf, y, cols, table_high, table_low, out, spread):
@@ -196,19 +220,18 @@
     gather = (wanted == code_row).astype(jnp.bfloat16)
     high, low = halves(x)
     face_sum = dot(gather, high) + dot(gather, low)
-    spread[...] = jnp.zeros_like(spread)
-    for f in range(FACES):
-        for v in range(VARS):
-            spread[v * slots : (v + 1) * slots, f * FACE_PAD : f * FACE_PAD + FACE] = face_sum[
-                f * slots : (f + 1) * slots, v * FACE : (v + 1) * FACE
-            ]
-    order_rows = jnp.concatenate([order_col] * VARS, axis=0)
-    z = spread[...]
-    wide = jnp.concatenate([jnp.where(order_rows == float(p), z, 0.0) for p in ORDERS], axis=1)
-    high, low = halves(wide)
-    total = y[...] + dot3(high, low, table_high[...], table_low[...])
+    total = y[...] + restrict_faces(face_sum, order_col, table_high, table_low, spread)
     for v in range(VARS):
         out[:, :, v * ROW : (v + 1) * ROW] = total[v * slots : (v + 1) * slots].reshape(peers, row_cap, ROW)
+
+
+def place_rows(x, slot_col, elements):
+    rows = x.shape[0]
+    slot_row = jnp.sum(jnp.where(iota((rows, rows), 0) == iota((rows, rows), 1), slot_col, 0.0), axis=0, keepdims=True)
+    put = (iota((elements, rows), 0).astype(jnp.float32) + 1.0 == slot_row).astype(jnp.bfloat16)
+    high, low = halves(x)
+    rest = (x - high.astype(jnp.float32) - low.astype(jnp.float32)).astype(jnp.bfloat16)
+    return dot(put, high) + dot(put, low) + dot(put, rest)
 
 
 def place_kernel(peers, row_cap, get, arrived, tags, out):
@@ -216,17 +239,82 @@
     rows = peers * row_cap
     x = arrived[...].reshape(rows, arrived.shape[2])
     slot_col = tags[:, :row_cap, TAG_ROW : TAG_ROW + 1].reshape(rows, 1)
-    slot_row = jnp.sum(jnp.where(iota((rows, rows), 0) == iota((rows, rows), 1), slot_col, 0.0), axis=0, keepdims=True)
-    put = (iota((elements, rows), 0).astype(jnp.float32) + 1.0 == slot_row).astype(jnp.bfloat16)
-    high, low = halves(x)
-    rest = (x - high.astype(jnp.float32) - low.astype(jnp.float32)).astype(jnp.bfloat16)
-    out[...] = dot(put, high) + dot(put, low) + dot(put, rest)
-
-
-def fetched(kernel, n_far, n_near, n_out, *refs):
+    out[...] = place_rows(x, slot_col, elements)
+
+
+def lift_kernel(peers, elements, get, out):
+    dest, elem, face, sub = [get(i) for i in range(4)]
+    count = dest.shape[1]
+    code = ((face * peers + dest) * elements + elem + 1).astype(jnp.float32)
+    tags = jnp.concatenate([code, jnp.zeros((1, LANES - count), jnp.float32)], axis=1)
+    out[count:, :] = jnp.where(iota((8, LANES), 0) == 0, tags, 0.0)
+    out[:count, :] = lift_traces(get(4), sub, get(5), get(6))
+
+
+def rows_kernel(
+    peers,
+    row_cap,
+    get,
+    adjoint,
+    order,
+    crow,
+    cell_high,
+    cell_low,
+    face_high,
+    face_low,
+    conf,
+    celem,
+    cface,
+    out,
+    cell_spread,
+    face_spread,
+):
+    elements = order.shape[1]
+    slots = peers * row_cap
+    place, slot = row_places(crow[...], peers, elements, row_cap)
+    take = onehot_rows(place, slots)
+    order_col = column(take, order[...].astype(jnp.float32))
+    elem_col = column(take, iota((1, elements), 1).astype(jnp.float32) + 1.0)
+    slot_col = column(take, slot + 1.0)
+    wanted = jnp.concatenate([elem_col + float(f * elements) for f in range(FACES)], axis=0)
+    code = (cface[...] * elements + celem[...] + 1).astype(jnp.float32)
+    gather = (wanted == code).astype(jnp.bfloat16)
+    high, low = halves(conf[...])
+    face_sum = dot(gather, high) + dot(gather, low)
+    total = restrict_cells(take, order_col, adjoint[...], cell_high, cell_low, cell_spread)
+    total = total + restrict_faces(face_sum, order_col, face_high, face_low, face_spread)
+    for v in range(VARS):
+        part = total[v * slots : (v + 1) * slots]
+        out[:, :, v * ROW : (v + 1) * ROW] = part.reshape(peers, row_cap, ROW)
+    tags = jnp.concatenate([elem_col, order_col, slot_col], axis=1)
+    out[:, :, VARS * ROW : VARS * ROW + 3] = tags.reshape(peers, row_cap, 3)
+
+
+def finish_kernel(peers, row_cap, elements, get, arrived, traces, face_high, face_low, out, spread):
+    rows = peers * row_cap
+    block = traces.shape[0] // peers
+    x = arrived[...].reshape(rows, arrived.shape[2])
+    elem_col, order_col, slot_col = [x[:, VARS * ROW + i : VARS * ROW + i + 1] for i in range(3)]
+    source = (iota((rows, 1), 0) // row_cap * elements).astype(jnp.float32)
+    wanted = jnp.concatenate([elem_col + source + float(f * peers * elements) for f in range(FACES)], axis=0)
+    face_sum = None
+    for k in range(peers):
+        part = traces[k * block : (k + 1) * block, :]
+        gather = (wanted == part[block - 8 : block - 7, :block]).astype(jnp.bfloat16)
+        high, low = halves(part)
+        add = dot(gather, high) + dot(gather, low)
+        face_sum = add if face_sum is None else face_sum + add
+    total = restrict_faces(face_sum, order_col, face_high, face_low, spread)
+    total = x[:, : VARS * ROW] + jnp.concatenate([total[v * rows : (v + 1) * rows] for v in range(VARS)], axis=1)
+    out[...] = place_rows(total, slot_col, elements)
+
+
+def fetched(kernel, n_far, n_pass, n_near, n_out, *refs):
     far, near, outs = refs[:n_far], refs[n_far : n_far + n_near], refs[n_far + n_near : n_far + n_near + n_out]
     rest = refs[n_far + n_near + n_out :]
-    held, sems, scratch = rest[:n_far], rest[n_far], rest[n_far + 1 :]
+    n_held = n_far - n_pass
+    held, sems, scratch = rest[:n_held], rest[n_held], rest[n_held + 1 :]
+    held = (*held, *outs[n_out - n_pass :])
     copies = [pltpu.make_async_copy(src, dst, sems.at[i]) for i, (src, dst) in enumerate(zip(far, held))]
     for copy in copies:
         copy.start()
@@ -235,19 +323,26 @@
         copies[i].wait()
         return held[i][...]
 
-    kernel(get, *near, *outs, *scratch)
-
-
-def call(kernel, outs, far, near=(), scratch=(), flops=0):
-    shapes = jax.tree.leaves(outs)
-    sizes = [np.prod(a.shape) * a.dtype.itemsize for a in (*far, *near, *shapes)]
+    kernel(get, *near, *outs[: n_out - n_pass], *scratch)
+    for copy in copies[n_held:]:
+        copy.wait()
+
+
+def like(a):
+    return jax.ShapeDtypeStruct(a.shape, a.dtype)
+
+
+def call(kernel, outs, far, near=(), scratch=(), hand_on=(), flops=0):
+    outs = [*outs, *[like(a) for a in hand_on]]
+    sizes = [np.prod(a.shape) * a.dtype.itemsize for a in (*far, *near, *outs)]
+    held = [pltpu.VMEM(a.shape, a.dtype) for a in far]
+    far = (*far, *hand_on)
     in_specs = [pl.BlockSpec(memory_space=pltpu.HBM)] * len(far) + [pl.BlockSpec(memory_space=pltpu.VMEM)] * len(near)
-    scratch = [*[pltpu.VMEM(a.shape, a.dtype) for a in far], pltpu.SemaphoreType.DMA((max(1, len(far)),)), *scratch]
     return pl.pallas_call(
-        functools.partial(fetched, kernel, len(far), len(near), len(shapes)),
+        functools.partial(fetched, kernel, len(far), len(hand_on), len(near), len(outs)),
         in_specs=in_specs,
         out_shape=outs,
-        scratch_shapes=scratch,
+        scratch_shapes=[*held, pltpu.SemaphoreType.DMA((max(1, len(far)),)), *scratch],
         compiler_params=pltpu.CompilerParams(vmem_limit_bytes=48 * 1024 * 1024),
         cost_estimate=pl.CostEstimate(flops=flops, bytes_accessed=int(sum(sizes)), transcendentals=0),
     )(*[pltpu.with_memory_space_constraint(a, pltpu.HBM) for a in far], *near)
@@ -288,48 +383,63 @@
     f32 = jnp.float32
     line = lambda a: a.reshape(1, -1)
     order, coarse_row = line(order), line(coarse_row)
+    whole = (adjoint, order, coarse_row, *cell, *face)
+    mortar = (line(mortar_dest), line(mortar_elem), line(mortar_face), line(mortar_sub))
+    if peers <= 8:
+        conf, conf_elem, conf_face = [from_behind(a, "gz", 1) for a in (conf_trace, line(conf_elem), line(conf_face))]
+        lifted, *whole = call(
+            functools.partial(lift_kernel, peers, elements),
+            [jax.ShapeDtypeStruct((count + 8, LANES), f32)],
+            (*mortar, mortar_trace, *lift),
+            hand_on=whole,
+        )
+        lifted = lax.all_gather(lifted, ("gx", "gy"), axis=0, tiled=True)
+        (rows,) = call(
+            functools.partial(rows_kernel, peers, row_cap),
+            [jax.ShapeDtypeStruct((peers, row_cap, ROWS_PAD), f32)],
+            (),
+            (*whole, conf, conf_elem, conf_face),
+            scratch=[
+                pltpu.VMEM((2, VARS * slots, CELL_PAD), f32),
+                pltpu.VMEM((VARS * slots, FACES * FACE_PAD), f32),
+            ],
+        )
+        (out,) = call(
+            functools.partial(finish_kernel, peers, row_cap, elements),
+            [jax.ShapeDtypeStruct((elements, VARS * ROW), f32)],
+            (),
+            (exchange(rows), lifted, *whole[-2:]),
+            scratch=[pltpu.VMEM((VARS * slots, FACES * FACE_PAD), f32)],
+        )
+        return out
     outgoing, conf = call(
         functools.partial(pack_kernel, peers, cap, elements),
-        (jax.ShapeDtypeStruct((peers, cap, LANES), f32), jax.ShapeDtypeStruct((confs, LANES), f32)),
-        (
-            line(mortar_dest),
-            line(mortar_elem),
-            line(mortar_face),
-            line(mortar_sub),
-            coarse_row,
-            line(conf_face),
-            line(conf_elem),
-            mortar_trace,
-            conf_trace,
-            *lift,
-        ),
+        [jax.ShapeDtypeStruct((peers, cap, LANES), f32), jax.ShapeDtypeStruct((confs, LANES), f32)],
+        (*mortar, coarse_row, line(conf_face), line(conf_elem), mortar_trace, conf_trace, *lift),
     )
     incoming = exchange(outgoing)
     conf = from_behind(conf, "gz", 1)
     y, cols, *face = call(
         functools.partial(cell_kernel, peers, row_cap),
-        (
-            jax.ShapeDtypeStruct((VARS * slots, ROW), f32),
-            jax.ShapeDtypeStruct((slots, 128), f32),
-            *[jax.ShapeDtypeStruct(t.shape, t.dtype) for t in face],
-        ),
-        (order, coarse_row, adjoint, *cell, *face),
+        [jax.ShapeDtypeStruct((VARS * slots, ROW), f32), jax.ShapeDtypeStruct((slots, 128), f32)],
+        (order, coarse_row, adjoint, *cell),
         scratch=[pltpu.VMEM((2, VARS * slots, CELL_PAD), f32)],
-    )
-    rows = call(
+        hand_on=face,
+    )
+    (rows,) = call(
         functools.partial(face_kernel, peers, row_cap, elements),
-        jax.ShapeDtypeStruct((peers, row_cap, VARS * ROW), f32),
+        [jax.ShapeDtypeStruct((peers, row_cap, VARS * ROW), f32)],
         (),
         (incoming, conf, y, cols, *face),
         scratch=[pltpu.VMEM((VARS * slots, FACES * FACE_PAD), f32)],
     )
-    arrived = exchange(rows)
-    return call(
+    (out,) = call(
         functools.partial(place_kernel, peers, row_cap),
-        jax.ShapeDtypeStruct((elements, VARS * ROW), f32),
+        [jax.ShapeDtypeStruct((elements, VARS * ROW), f32)],
         (),
-        (arrived, incoming),
-    )
+        (exchange(rows), incoming),
+    )
+    return out
 
 
 def solution(mesh):

time: 31.3 us -> 54.5 us (1.74)
  blocking collectives: 10 us -> 36.2 us
  waiting for transfers between devices: 6.2 us -> 0.01 us
  starting transfers between devices: 7.3 us -> 9.35 us
  Pallas kernels: 7.5 us -> 8.44 us
    all_gather x0 -> x1, blocking collectives: none -> 36.2 us  [body(): lifted = lax.all_gather(lifted, ('gx', 'gy'), axis=0, tiled=True)]
    all_to_all x1 -> x0, blocking collectives: 10 us -> none  [exchange(): lax.all_to_all(block, ('gx', 'gy'), split_axis=0, concat_axis=0, tiled=True)]
    all_to_all x1, waiting for transfers between devices: 5.03 us -> 0.01 us  [exchange(): lax.all_to_all(block, ('gx', 'gy'), split_axis=0, concat_axis=0, tiled=True)]
    ppermute x1 -> x3, starting transfers between devices: 0.01 us -> 3.51 us  [from_behind(): return lax.ppermute(block, axis, route)]
    all_to_all x1, starting transfers between devices: 7.29 us -> 5.85 us  [exchange(): lax.all_to_all(block, ('gx', 'gy'), split_axis=0, concat_axis=0, tiled=True)]
    ppermute x1 -> x3, waiting for transfers between devices: 1.16 us -> 0.01 us  [from_behind(): return lax.ppermute(block, axis, route)]
    pallas_call x4 -> x3, Pallas kernels: 7.5 us -> 8.44 us  [call(): pl.pallas_call(functools.partial(fetched, kernel, len(far), len(hand_on),...]
  transfers between devices with their start and end apart: 2 -> 4, of which waited for: 2 -> 0; matrix products, arithmetic and copies ran while one was open for 0% -> 0% of each run, Pallas kernels for 8% -> 5%
where the time goes in v4:
time: 54.5 us; the launch traced here: 54.3 us
  blocking collectives  36.2 us (66%)
  starting transfers between devices  9.35 us (17%)
  Pallas kernels  8.44 us (15%)
    all_gather x1, blocking collectives, body(): lifted = lax.all_gather(lifted, ('gx', 'gy'), axis=0, tiled=True)  36.2 us
    pallas_call x3, Pallas kernels, call(): pl.pallas_call(functools.partial(fetched, kernel, len(far), len(hand_on),...  8.44 us
    all_to_all x1, starting transfers between devices, exchange(): lax.all_to_all(block, ('gx', 'gy'), split_axis=0, concat_axis=0, tiled=True)  5.85 us
    ppermute x3, starting transfers between devices, from_behind(): return lax.ppermute(block, axis, route)  3.51 us
  transfers between devices with their start and end apart: 4, of which 0 were waited for; matrix products, arithmetic and copies ran while one was open for 0% of the time, Pallas kernels for 5%

profile of v4, /device:TPU:0, one launch (start us, length us, event | category | flops | bytes accessed | tf_op | source)
XLA Modules:
  0.0 54.3 jit_solution(5780813184077925567)
XLA Ops:
  0.0 0.0 copy-start
  0.0 0.5 collective-permute-start
  0.5 0.2 copy-done
  0.7 0.0 copy-start.1
  0.7 2.4 %collective-permute-start.1 = (s32[1,64]{1,0:T(1,128)S(1)}, s32[1,64]{1,0:T(1,128)S(1)}, u32[]{:S(2)}, u32[]{:S(2)}) collective-permute-start(s32[1,64]{1,0:T(1,128)S(1)} %bitcast.14), channel_id=1, source_target_pairs={{3,0},{0,1},{1,2},{2,3},{7,4},{4,5},{5,6},{6,7},{11,8},{8,9},{9,10... | collective-permute-start | bytes 776 | tf_op jit(solution)/shard_map/ppermute | solution.py:358
  3.1 0.0 copy-done.1
  3.1 0.7 %collective-permute-start.2 = (s32[1,64]{1,0:T(1,128)S(1)}, s32[1,64]{1,0:T(1,128)S(1)}, u32[]{:S(2)}, u32[]{:S(2)}) collective-permute-start(s32[1,64]{1,0:T(1,128)S(1)} %bitcast.15), channel_id=1, source_target_pairs={{3,0},{0,1},{1,2},{2,3},{7,4},{4,5},{5,6},{6,7},{11,8},{8,9},{9,10... | collective-permute-start | bytes 776 | tf_op jit(solution)/shard_map/ppermute | solution.py:358
  3.7 2.7 %shard_map.163 = (f32[104,256]{1,0:T(8,128)S(1)}, f32[32,1715]{1,0:T(8,128)S(1)}, s32[1,32]{1,0:T(1,128)S(1)}, s32[1,32]{1,0:T(1,128)S(1)}, bf16[1920,216]{1,0:T...) custom-call(s32[1,96]{1,0:T(1,128)} %bitcast.8, ...), custom_call_target="tpu_custom_call" | custom-call | bytes 4788224 | tf_op jit(solution)/shard_map/pallas_call | solution.py:341
  6.4 0.0 collective-permute-done.1.refs_8_
  6.4 0.0 collective-permute-done.2.refs_9_
  6.5 0.0 collective-permute-done.refs_7_
  6.5 2.5 %shard_map.164 = f32[8,4,1152]{2,1,0:T(4,128)} custom-call(f32[32,1715]{1,0:T(8,128)S(1)} %get-tuple-element.13.refs_0_, s32[1,32]{1,0:T(1,128)S(1)} %get-tuple-element.14.refs_1_, s32[1,32]{1,0:T(1,128)S(1)} %get-tuple-element.15.refs_2_, bf16[1920,216]{1,0:T(8,128)(2,1)S(1)} %get-tuple-element.16.refs_3_, bf16[1920,216]{1,0:T(8,128)(2,1)S(1)} %get-tuple-element.17.refs_4_, ...), custom_call_target="tpu_custom_call" | custom-call | bytes 3748224 | tf_op jit(solution)/shard_map/pallas_call | solution.py:341
  9.0 5.8 %all-to-all-start = ((f32[8,4,1152]{2,1,0:T(4,128)}), f32[8,4,1152]{2,1,0:T(4,128)S(1)}, u32[]{:S(2)}, u32[]{:S(2)}) async-start(f32[8,4,1152]{2,1,0:T(4,128)} %shard_map.164), calls=%async_computation | async-start | bytes 294912 | tf_op jit(solution)/shard_map/all_to_all | solution.py:352
  14.8 36.2 %all_gather.3.refs_1_ = f32[832,256]{1,0:T(8,128)S(1)} all-gather(f32[104,256]{1,0:T(8,128)S(1)} %get-tuple-element.20), channel_id=1, replica_groups=mesh['gx'=2,'gy'=4,'gz'=4] {'gx','gy'}, dimensions={0}, use_global_device_ids=true | all-gather | bytes 958464 | tf_op jit(solution)/shard_map/all_gather | solution.py:396
  51.1 0.0 all-to-all-done.refs_0_
  51.1 3.2 %shard_map.165 = f32[32,1080]{1,0:T(8,128)} custom-call(f32[8,4,1152]{2,1,0:T(4,128)S(1)} %all-to-all-done.refs_0_, f32[832,256]{1,0:T(8,128)S(1)} %all_gather.3.refs_1_, bf16[1920,216]{1,0:T(8,128)(2,1)S(1)} %get-tuple-element.18.refs_5_.refs_2_, bf16[1920,216]{1,0:T(8,128)(2,1)S(1)} %get-tuple-element.19.refs_6_.refs_3_), custom_call_target="tpu_custom_call" | custom-call | bytes 2796544 | tf_op jit(solution)/shard_map/pallas_call | solution.py:341
Async XLA Ops:
  0.0 0.7 %copy-start = (s32[64]{0:T(128)S(1)}, s32[64]{0:T(128)}, u32[]{:S(2)}) copy-start(s32[64]{0:T(128)} %param.25) | copy-start | bytes 772
  0.0 6.5 %collective-permute-start = (f32[64,245]{1,0:T(8,128)}, f32[64,245]{1,0:T(8,128)S(1)}, u32[]{:S(2)}, u32[]{:S(2)}) collective-permute-start(f32[64,245]{1,0:T(8,128)} %param.24), channel_id=1, source_target_pairs={{3,0},{0,1},{1,2},{2,3},{7,4},{4,5},{5,6},{6,7},{11,8},{8,9},{9,10... | collective-permute-start | bytes 188168 | tf_op jit(solution)/shard_map/ppermute | solution.py:358
  0.7 2.4 %copy-start.1 = (s32[64]{0:T(128)S(1)}, s32[64]{0:T(128)}, u32[]{:S(2)}) copy-start(s32[64]{0:T(128)} %param.26) | copy-start | bytes 772
  0.7 5.8 %collective-permute-start.1 = (s32[1,64]{1,0:T(1,128)S(1)}, s32[1,64]{1,0:T(1,128)S(1)}, u32[]{:S(2)}, u32[]{:S(2)}) collective-permute-start(s32[1,64]{1,0:T(1,128)S(1)} %bitcast.14), channel_id=1, source_target_pairs={{3,0},{0,1},{1,2},{2,3},{7,4},{4,5},{5,6},{6,7},{11,8},{8,9},{9,10... | collective-permute-start | bytes 776 | tf_op jit(solution)/shard_map/ppermute | solution.py:358
  3.1 3.4 %collective-permute-start.2 = (s32[1,64]{1,0:T(1,128)S(1)}, s32[1,64]{1,0:T(1,128)S(1)}, u32[]{:S(2)}, u32[]{:S(2)}) collective-permute-start(s32[1,64]{1,0:T(1,128)S(1)} %bitcast.15), channel_id=1, source_target_pairs={{3,0},{0,1},{1,2},{2,3},{7,4},{4,5},{5,6},{6,7},{11,8},{8,9},{9,10... | collective-permute-start | bytes 776 | tf_op jit(solution)/shard_map/ppermute | solution.py:358
  9.0 42.1 %all-to-all-start = ((f32[8,4,1152]{2,1,0:T(4,128)}), f32[8,4,1152]{2,1,0:T(4,128)S(1)}, u32[]{:S(2)}, u32[]{:S(2)}) async-start(f32[8,4,1152]{2,1,0:T(4,128)} %shard_map.164), calls=%async_computation | async-start | bytes 294912 | tf_op jit(solution)/shard_map/all_to_all | solution.py:352

commit v5 on v4

--- a/solution.py
+++ b/solution.py
@@ -290,8 +290,9 @@
     out[:, :, VARS * ROW : VARS * ROW + 3] = tags.reshape(peers, row_cap, 3)
 
 
-def finish_kernel(peers, row_cap, elements, get, arrived, traces, face_high, face_low, out, spread):
+def finish_kernel(peers, row_cap, elements, get, arrived, face_high, face_low, out, spread):
     rows = peers * row_cap
+    traces = get(0)
     block = traces.shape[0] // peers
     x = arrived[...].reshape(rows, arrived.shape[2])
     elem_col, order_col, slot_col = [x[:, VARS * ROW + i : VARS * ROW + i + 1] for i in range(3)]
@@ -389,7 +390,7 @@
         conf, conf_elem, conf_face = [from_behind(a, "gz", 1) for a in (conf_trace, line(conf_elem), line(conf_face))]
         lifted, *whole = call(
             functools.partial(lift_kernel, peers, elements),
-            [jax.ShapeDtypeStruct((count + 8, LANES), f32)],
+            [pltpu.HBM((count + 8, LANES), f32)],
             (*mortar, mortar_trace, *lift),
             hand_on=whole,
         )
@@ -407,8 +408,8 @@
         (out,) = call(
             functools.partial(finish_kernel, peers, row_cap, elements),
             [jax.ShapeDtypeStruct((elements, VARS * ROW), f32)],
-            (),
-            (exchange(rows), lifted, *whole[-2:]),
+            (lifted,),
+            (exchange(rows), *whole[-2:]),
             scratch=[pltpu.VMEM((VARS * slots, FACES * FACE_PAD), f32)],
         )
         return out

time: 54.5 us -> 58.1 us (1.066)
  Pallas kernels: 8.44 us -> 10.3 us
  blocking collectives: 36.2 us -> 37.7 us
    pallas_call x3, Pallas kernels: 8.44 us -> 10.3 us  [call(): pl.pallas_call(functools.partial(fetched, kernel, len(far), len(hand_on),...]
    all_gather x1, blocking collectives: 36.2 us -> 37.7 us  [body(): lifted = lax.all_gather(lifted, ('gx', 'gy'), axis=0, tiled=True)]
  transfers between devices with their start and end apart: 4 -> 4, of which waited for: 0 -> 0; matrix products, arithmetic and copies ran while one was open for 0% -> 0% of each run, Pallas kernels for 5% -> 6%
where the time goes in v5:
time: 58.1 us; the launch traced here: 57.8 us
  blocking collectives  37.7 us (65%)
  Pallas kernels  10.3 us (18%)
  starting transfers between devices  9.48 us (16%)
    all_gather x1, blocking collectives, body(): lifted = lax.all_gather(lifted, ('gx', 'gy'), axis=0, tiled=True)  37.7 us
    pallas_call x3, Pallas kernels, call(): pl.pallas_call(functools.partial(fetched, kernel, len(far), len(hand_on),...  10.3 us
    all_to_all x1, starting transfers between devices, exchange(): lax.all_to_all(block, ('gx', 'gy'), split_axis=0, concat_axis=0, tiled=True)  5.98 us
    ppermute x3, starting transfers between devices, from_behind(): return lax.ppermute(block, axis, route)  3.51 us
  transfers between devices with their start and end apart: 4, of which 0 were waited for; matrix products, arithmetic and copies ran while one was open for 0% of the time, Pallas kernels for 6%

profile of v5, /device:TPU:0, one launch (start us, length us, event | category | flops | bytes accessed | tf_op | source)
XLA Modules:
  0.0 57.8 jit_solution(11135074473485658506)
XLA Ops:
  0.0 0.0 copy-start.1
  0.0 0.5 collective-permute-start
  0.5 0.2 copy-done.1
  0.7 0.0 copy-start.2
  0.7 2.4 %collective-permute-start.1 = (s32[1,64]{1,0:T(1,128)S(1)}, s32[1,64]{1,0:T(1,128)S(1)}, u32[]{:S(2)}, u32[]{:S(2)}) collective-permute-start(s32[1,64]{1,0:T(1,128)S(1)} %bitcast.14), channel_id=1, source_target_pairs={{3,0},{0,1},{1,2},{2,3},{7,4},{4,5},{5,6},{6,7},{11,8},{8,9},{9,10... | collective-permute-start | bytes 776 | tf_op jit(solution)/shard_map/ppermute | solution.py:359
  3.1 0.0 copy-done.2
  3.1 0.7 %collective-permute-start.2 = (s32[1,64]{1,0:T(1,128)S(1)}, s32[1,64]{1,0:T(1,128)S(1)}, u32[]{:S(2)}, u32[]{:S(2)}) collective-permute-start(s32[1,64]{1,0:T(1,128)S(1)} %bitcast.15), channel_id=1, source_target_pairs={{3,0},{0,1},{1,2},{2,3},{7,4},{4,5},{5,6},{6,7},{11,8},{8,9},{9,10... | collective-permute-start | bytes 776 | tf_op jit(solution)/shard_map/ppermute | solution.py:359
  3.7 3.3 %shard_map.163 = (f32[104,256]{1,0:T(8,128)}, f32[32,1715]{1,0:T(8,128)S(1)}, s32[1,32]{1,0:T(1,128)S(1)}, s32[1,32]{1,0:T(1,128)S(1)}, bf16[1920,216]{1,0:T(8,1...) custom-call(s32[1,96]{1,0:T(1,128)} %bitcast.8, ...), custom_call_target="tpu_custom_call" | custom-call | bytes 4788224 | tf_op jit(solution)/shard_map/pallas_call | solution.py:342
  7.1 0.0 collective-permute-done.1.refs_8_
  7.1 0.0 collective-permute-done.2.refs_9_
  7.1 0.0 collective-permute-done.refs_7_
  7.1 2.5 %shard_map.164 = f32[8,4,1152]{2,1,0:T(4,128)} custom-call(f32[32,1715]{1,0:T(8,128)S(1)} %get-tuple-element.14.refs_0_, s32[1,32]{1,0:T(1,128)S(1)} %get-tuple-element.15.refs_1_, s32[1,32]{1,0:T(1,128)S(1)} %get-tuple-element.16.refs_2_, bf16[1920,216]{1,0:T(8,128)(2,1)S(1)} %get-tuple-element.17.refs_3_, bf16[1920,216]{1,0:T(8,128)(2,1)S(1)} %get-tuple-element.18.refs_4_, ...), custom_call_target="tpu_custom_call" | custom-call | bytes 3748224 | tf_op jit(solution)/shard_map/pallas_call | solution.py:342
  9.7 0.0 copy-start
  9.7 6.0 %all-to-all-start = ((f32[8,4,1152]{2,1,0:T(4,128)}), f32[8,4,1152]{2,1,0:T(4,128)S(1)}, u32[]{:S(2)}, u32[]{:S(2)}) async-start(f32[8,4,1152]{2,1,0:T(4,128)} %shard_map.164), calls=%async_computation | async-start | bytes 294912 | tf_op jit(solution)/shard_map/all_to_all | solution.py:353
  15.6 0.0 copy-done
  15.6 37.7 %all_gather.3.refs_0_ = f32[832,256]{1,0:T(8,128)} all-gather(f32[104,256]{1,0:T(8,128)S(1)} %copy-done), channel_id=1, replica_groups=mesh['gx'=2,'gy'=4,'gz'=4] {'gx','gy'}, dimensions={0}, use_global_device_ids=true | all-gather | bytes 958464 | tf_op jit(solution)/shard_map/all_gather | solution.py:397
  53.4 0.0 all-to-all-done.refs_1_
  53.4 4.4 %shard_map.165 = f32[32,1080]{1,0:T(8,128)} custom-call(f32[832,256]{1,0:T(8,128)} %all_gather.3.refs_0_, f32[8,4,1152]{2,1,0:T(4,128)S(1)} %all-to-all-done.refs_1_, bf16[1920,216]{1,0:T(8,128)(2,1)S(1)} %get-tuple-element.19.refs_5_.refs_2_, bf16[1920,216]{1,0:T(8,128)(2,1)S(1)} %get-tuple-element.20.refs_6_.refs_3_), custom_call_target="tpu_custom_call" | custom-call | bytes 2796544 | tf_op jit(solution)/shard_map/pallas_call | solution.py:342
Async XLA Ops:
  0.0 0.7 %copy-start.1 = (s32[64]{0:T(128)S(1)}, s32[64]{0:T(128)}, u32[]{:S(2)}) copy-start(s32[64]{0:T(128)} %param.25) | copy-start | bytes 772
  0.0 7.1 %collective-permute-start = (f32[64,245]{1,0:T(8,128)}, f32[64,245]{1,0:T(8,128)S(1)}, u32[]{:S(2)}, u32[]{:S(2)}) collective-permute-start(f32[64,245]{1,0:T(8,128)} %param.24), channel_id=1, source_target_pairs={{3,0},{0,1},{1,2},{2,3},{7,4},{4,5},{5,6},{6,7},{11,8},{8,9},{9,10... | collective-permute-start | bytes 188168 | tf_op jit(solution)/shard_map/ppermute | solution.py:359
  0.7 2.4 %copy-start.2 = (s32[64]{0:T(128)S(1)}, s32[64]{0:T(128)}, u32[]{:S(2)}) copy-start(s32[64]{0:T(128)} %param.26) | copy-start | bytes 772
  0.7 6.4 %collective-permute-start.1 = (s32[1,64]{1,0:T(1,128)S(1)}, s32[1,64]{1,0:T(1,128)S(1)}, u32[]{:S(2)}, u32[]{:S(2)}) collective-permute-start(s32[1,64]{1,0:T(1,128)S(1)} %bitcast.14), channel_id=1, source_target_pairs={{3,0},{0,1},{1,2},{2,3},{7,4},{4,5},{5,6},{6,7},{11,8},{8,9},{9,10... | collective-permute-start | bytes 776 | tf_op jit(solution)/shard_map/ppermute | solution.py:359
  3.1 4.0 %collective-permute-start.2 = (s32[1,64]{1,0:T(1,128)S(1)}, s32[1,64]{1,0:T(1,128)S(1)}, u32[]{:S(2)}, u32[]{:S(2)}) collective-permute-start(s32[1,64]{1,0:T(1,128)S(1)} %bitcast.15), channel_id=1, source_target_pairs={{3,0},{0,1},{1,2},{2,3},{7,4},{4,5},{5,6},{6,7},{11,8},{8,9},{9,10... | collective-permute-start | bytes 776 | tf_op jit(solution)/shard_map/ppermute | solution.py:359
  9.7 6.0 %copy-start = (f32[104,256]{1,0:T(8,128)S(1)}, f32[104,256]{1,0:T(8,128)}, u32[]{:S(2)}) copy-start(f32[104,256]{1,0:T(8,128)} %get-tuple-element.13) | copy-start | bytes 319492
  9.7 43.7 %all-to-all-start = ((f32[8,4,1152]{2,1,0:T(4,128)}), f32[8,4,1152]{2,1,0:T(4,128)S(1)}, u32[]{:S(2)}, u32[]{:S(2)}) async-start(f32[8,4,1152]{2,1,0:T(4,128)} %shard_map.164), calls=%async_computation | async-start | bytes 294912 | tf_op jit(solution)/shard_map/all_to_all | solution.py:353

commit v6 on v1

--- a/solution.py
+++ b/solution.py
@@ -17,11 +17,12 @@
 FACES = 6
 ORDERS = (2, 3, 4, 5, 6)
 TRACE = VARS * FACE
-LANES = 256
-TAG_FACE = TRACE
-TAG_ROW = TRACE + 1
+TRACE_PAD = 256
+FLAT = 36
+SENT = VARS * FLAT
 CELL_PAD = 384
-FACE_PAD = 64
+FACE_PAD = 40
+FACES_PAD = 256
 
 
 def grid_nodes(degree):
@@ -49,27 +50,27 @@
 def basis_tables():
     top_nodes = grid_nodes(6)
     mortar = [lagrange_rows(6, (top_nodes - 1.0) / 2.0), lagrange_rows(6, (top_nodes + 1.0) / 2.0)]
-    lift = np.zeros((4, LANES, LANES))
-    for sub in range(4):
-        both = np.kron(mortar[sub // 2], mortar[sub % 2])
+    flat = lagrange_rows(5, top_nodes)
+    lift = np.zeros((5, TRACE_PAD, SENT))
+    for sub in range(5):
+        both = (mortar[sub // 2] @ flat, mortar[sub % 2] @ flat) if sub < 4 else (flat, flat)
         for v in range(VARS):
-            part = slice(v * FACE, (v + 1) * FACE)
-            lift[sub, part, part] = both
+            lift[sub, v * FACE : (v + 1) * FACE, v * FLAT : (v + 1) * FLAT] = np.kron(*both)
     cell = np.zeros((len(ORDERS), CELL_PAD, ROW))
-    face = np.zeros((len(ORDERS), FACES, FACE_PAD, ROW))
+    face = np.zeros((len(ORDERS), FACES_PAD, ROW))
     for index, p in enumerate(ORDERS):
         shrink = np.zeros((6, NODE))
         shrink[:p, : p + 1] = lagrange_rows(p - 1, grid_nodes(p)).T
-        reduce = np.zeros((NODE, NODE))
-        reduce[: p + 1, :] = lagrange_rows(p, top_nodes).T
         cell[index, :CELL] = np.einsum("ai,bj,ck->ijkabc", shrink, shrink, shrink).reshape(CELL, ROW)
-        flat = shrink @ reduce
+        lower = np.zeros((6, 6))
+        lower[:p] = lagrange_rows(p - 1, grid_nodes(5)).T
         low, high = shrink[:, 0], shrink[:, p]
         for axis, spec in enumerate(("c,ai,bj->ijcab", "c,ai,bj->ijacb", "c,ai,bj->ijabc")):
             for side, edge in enumerate((low, high)):
-                face[index, 2 * axis + side, :FACE] = np.einsum(spec, edge, flat, flat).reshape(FACE, ROW)
+                first = (2 * axis + side) * FACE_PAD
+                face[index, first : first + FLAT] = np.einsum(spec, edge, lower, lower).reshape(FLAT, ROW)
     return (
-        split_table(lift.reshape(4 * LANES, LANES)),
+        split_table(lift.reshape(-1, SENT)),
         split_table(cell.reshape(-1, ROW)),
         split_table(face.reshape(-1, ROW)),
     )
@@ -121,43 +122,42 @@
     return jnp.sum(onehot * values, axis=1, keepdims=True)
 
 
-def pack_kernel(
-    peers,
-    cap,
-    elements,
-    get,
-    out,
-    conf_out,
-):
+def pad_lanes(x, lanes):
+    return jnp.concatenate([x, jnp.zeros((x.shape[0], lanes - x.shape[1]), x.dtype)], axis=1)
+
+
+def pack_kernel(peers, cap, row_cap, elements, get, out, conf_out):
     dest, elem, face, sub, crow, cface, celem = [get(i) for i in range(7)]
-    count = dest.shape[1]
-    rows = peers * cap
+    count, confs = dest.shape[1], cface.shape[1]
+    groups, slots = -(-cap // row_cap), peers * row_cap
     member = (iota((peers, count), 0) == dest).astype(jnp.float32)
-    base = iota(member.shape, 0).astype(jnp.float32) * cap
-    place = jnp.sum(member * (base + earlier(member)), axis=0, keepdims=True)
-    put = onehot_rows(place, rows)
-    code = (face * elements + elem + 1).astype(jnp.float32)
-    code_col = column(put, code)
-    row_place, row_slot = row_places(crow, peers, elements, cap)
-    row_col = column(onehot_rows(row_place, rows), row_slot + 1.0)
+    rank = jnp.sum(member * earlier(member), axis=0, keepdims=True)
+    group = sum([(rank >= float(g * row_cap)).astype(jnp.float32) for g in range(1, groups)], jnp.zeros_like(rank))
+    place = group * float(slots - row_cap) + dest.astype(jnp.float32) * float(row_cap) + rank
+    put = onehot_rows(place, groups * slots)
+    code_col = column(put, (face * elements + elem + 1).astype(jnp.float32))
+    row_place, row_slot = row_places(crow, peers, elements, row_cap)
+    row_col = column(onehot_rows(row_place, slots), row_slot + 1.0)
     eye = (iota((count, count), 0) == iota((count, count), 1)).astype(jnp.float32)
     sub_col = column(eye, sub.astype(jnp.float32))
-    x = jnp.concatenate([get(7), jnp.zeros((count, LANES - TRACE), jnp.float32)], axis=1)
+    x = pad_lanes(get(7), TRACE_PAD)
     wide = jnp.concatenate([jnp.where(sub_col == float(s), x, 0.0) for s in range(4)], axis=1)
-    high, low = halves(wide)
-    lifted = dot3(high, low, get(9), get(10))
+    table_high, table_low = get(9), get(10)
+    split = 4 * TRACE_PAD
+    lifted = dot3(*halves(wide), table_high[:split], table_low[:split])
     lifted_high, lifted_low = halves(lifted)
     put = put.astype(jnp.bfloat16)
     packed = dot(put, lifted_high) + dot(put, lifted_low)
-    lane = iota((rows, LANES), 1)
-    packed = jnp.where(lane == TAG_FACE, code_col, packed)
-    packed = jnp.where(lane == TAG_ROW, row_col, packed)
-    out[...] = packed.reshape(peers, cap, LANES)
-    confs = cface.shape[1]
+    for g in range(groups):
+        part = packed[g * slots : (g + 1) * slots]
+        out[:, :, g * SENT : (g + 1) * SENT] = part.reshape(peers, row_cap, SENT)
+    tags = jnp.concatenate([*[code_col[g * slots : (g + 1) * slots] for g in range(groups)], row_col], axis=1)
+    out[:, :, groups * SENT : groups * (SENT + 1) + 1] = tags.reshape(peers, row_cap, groups + 1)
     eye = (iota((confs, confs), 0) == iota((confs, confs), 1)).astype(jnp.float32)
     conf_col = column(eye, (cface * elements + celem + 1).astype(jnp.float32))
-    c = jnp.concatenate([get(8), jnp.zeros((confs, LANES - TRACE), jnp.float32)], axis=1)
-    conf_out[...] = jnp.where(iota((confs, LANES), 1) == TAG_FACE, conf_col, c)
+    conf = dot3(*halves(pad_lanes(get(8), TRACE_PAD)), table_high[split:], table_low[split:])
+    conf_out[:, :SENT] = conf
+    conf_out[:, SENT : SENT + 1] = conf_col
 
 
 def cell_kernel(peers, row_cap, get, y_out, col_out, face_high, face_low, spread):
@@ -185,11 +185,15 @@
     face_low[...] = get(6)
 
 
-def face_kernel(peers, row_cap, elements, get, incoming, conf, y, cols, table_high, table_low, out, spread):
+def face_kernel(peers, row_cap, elements, groups, get, incoming, conf, y, cols, table_high, table_low, out, spread):
     slots = peers * row_cap
-    x = jnp.concatenate([incoming[...].reshape(-1, LANES), conf[...]], axis=0)
+    message = incoming[...].reshape(slots, incoming.shape[2])
+    first_tag = groups * SENT
+    x = jnp.concatenate([*[message[:, g * SENT : (g + 1) * SENT] for g in range(groups)], conf[:, :SENT]], axis=0)
+    code_col = jnp.concatenate(
+        [*[message[:, first_tag + g : first_tag + g + 1] for g in range(groups)], conf[:, SENT : SENT + 1]], axis=0
+    )
     count = x.shape[0]
-    code_col = x[:, TAG_FACE : TAG_FACE + 1]
     code_row = jnp.sum(jnp.where(iota((count, count), 0) == iota((count, count), 1), code_col, 0.0), axis=0, keepdims=True)
     order_col, elem_col = cols[:, 0:1], cols[:, 1:2]
     wanted = jnp.concatenate([jnp.where(elem_col > 0.0, elem_col + float(f * elements), -1.0) for f in range(FACES)], axis=0)
@@ -199,8 +203,8 @@
     spread[...] = jnp.zeros_like(spread)
     for f in range(FACES):
         for v in range(VARS):
-            spread[v * slots : (v + 1) * slots, f * FACE_PAD : f * FACE_PAD + FACE] = face_sum[
-                f * slots : (f + 1) * slots, v * FACE : (v + 1) * FACE
+            spread[v * slots : (v + 1) * slots, f * FACE_PAD : f * FACE_PAD + FLAT] = face_sum[
+                f * slots : (f + 1) * slots, v * FLAT : (v + 1) * FLAT
             ]
     order_rows = jnp.concatenate([order_col] * VARS, axis=0)
     z = spread[...]
@@ -211,11 +215,11 @@
         out[:, :, v * ROW : (v + 1) * ROW] = total[v * slots : (v + 1) * slots].reshape(peers, row_cap, ROW)
 
 
-def place_kernel(peers, row_cap, get, arrived, tags, out):
+def place_kernel(peers, row_cap, tag, get, arrived, message, out):
     elements = out.shape[0]
     rows = peers * row_cap
     x = arrived[...].reshape(rows, arrived.shape[2])
-    slot_col = tags[:, :row_cap, TAG_ROW : TAG_ROW + 1].reshape(rows, 1)
+    slot_col = message[:, :, tag : tag + 1].reshape(rows, 1)
     slot_row = jnp.sum(jnp.where(iota((rows, rows), 0) == iota((rows, rows), 1), slot_col, 0.0), axis=0, keepdims=True)
     put = (iota((elements, rows), 0).astype(jnp.float32) + 1.0 == slot_row).astype(jnp.bfloat16)
     high, low = halves(x)
@@ -283,14 +287,15 @@
     cap = max(2, 2 * count // peers)
     row_cap = max(2, elements // peers)
     slots = peers * row_cap
-    assert row_cap <= cap
+    groups = -(-cap // row_cap)
+    lanes = -(-(groups * (SENT + 1) + 1) // 128) * 128
     lift, cell, face = [tuple(jnp.asarray(t) for t in pair) for pair in basis_tables()]
     f32 = jnp.float32
     line = lambda a: a.reshape(1, -1)
     order, coarse_row = line(order), line(coarse_row)
     outgoing, conf = call(
-        functools.partial(pack_kernel, peers, cap, elements),
-        (jax.ShapeDtypeStruct((peers, cap, LANES), f32), jax.ShapeDtypeStruct((confs, LANES), f32)),
+        functools.partial(pack_kernel, peers, cap, row_cap, elements),
+        (jax.ShapeDtypeStruct((peers, row_cap, lanes), f32), jax.ShapeDtypeStruct((confs, TRACE_PAD), f32)),
         (
             line(mortar_dest),
             line(mortar_elem),
@@ -317,15 +322,15 @@
         scratch=[pltpu.VMEM((2, VARS * slots, CELL_PAD), f32)],
     )
     rows = call(
-        functools.partial(face_kernel, peers, row_cap, elements),
+        functools.partial(face_kernel, peers, row_cap, elements, groups),
         jax.ShapeDtypeStruct((peers, row_cap, VARS * ROW), f32),
         (),
         (incoming, conf, y, cols, *face),
-        scratch=[pltpu.VMEM((VARS * slots, FACES * FACE_PAD), f32)],
+        scratch=[pltpu.VMEM((VARS * slots, FACES_PAD), f32)],
     )
     arrived = exchange(rows)
     return call(
-        functools.partial(place_kernel, peers, row_cap),
+        functools.partial(place_kernel, peers, row_cap, groups * (SENT + 1)),
         jax.ShapeDtypeStruct((elements, VARS * ROW), f32),
         (),
         (arrived, incoming),

time: 31.3 us -> 30.5 us (0.974)
  waiting for transfers between devices: 6.2 us -> 5.33 us
    all_to_all x1, waiting for transfers between devices: 5.03 us -> 4.12 us  [exchange(): lax.all_to_all(block, ('gx', 'gy'), split_axis=0, concat_axis=0, tiled=True)]
where the time goes in v6:
time: 30.5 us; the launch traced here: 30.3 us
  blocking collectives  10.1 us (33%)
  Pallas kernels  7.51 us (25%)
  starting transfers between devices  7.3 us (24%)
  waiting for transfers between devices  5.33 us (17%)
    all_to_all x1, blocking collectives, exchange(): lax.all_to_all(block, ('gx', 'gy'), split_axis=0, concat_axis=0, tiled=True)  10.1 us
    pallas_call x4, Pallas kernels, call(): pl.pallas_call(functools.partial(fetched, kernel, len(far), len(near), le...  7.51 us
    all_to_all x1, starting transfers between devices, exchange(): lax.all_to_all(block, ('gx', 'gy'), split_axis=0, concat_axis=0, tiled=True)  7.29 us
    all_to_all x1, waiting for transfers between devices, exchange(): lax.all_to_all(block, ('gx', 'gy'), split_axis=0, concat_axis=0, tiled=True)  4.12 us
    ppermute x1, waiting for transfers between devices, from_behind(): return lax.ppermute(block, axis, route)  1.2 us
  transfers between devices with their start and end apart: 2, of which 2 were waited for; matrix products, arithmetic and copies ran while one was open for 0% of the time, Pallas kernels for 8%

profile of v6, /device:TPU:0, one launch (start us, length us, event | category | flops | bytes accessed | tf_op | source)
XLA Modules:
  0.0 30.3 jit_solution(2825263421292783085)
XLA Ops:
  0.0 3.0 %shard_map.163 = (f32[8,4,1152]{2,1,0:T(4,128)}, f32[64,256]{1,0:T(8,128)S(1)}) custom-call(s32[1,96]{1,0:T(1,128)} %bitcast.10, s32[1,96]{1,0:T(1,128)} %bitcast.11, s32[1,96]{1,0:T(1,128)} %bitcast.12, s32[1,96]{1,0:T(1,128)} %bitcast.13, s32[1,32]{1,0:T(1,128)} %bitcast.8, s32[1,64]{1,0:T(1,128)} %bitcast.14, s32[1,64]{1,0:T(1,128)} %bitcast.15, ...), custom_call_target="tpu_custom_call" | custom-call | bytes 1293568 | tf_op jit(solution)/shard_map/pallas_call | solution.py:250
  3.0 7.3 %all-to-all-start = ((f32[8,4,1152]{2,1,0:T(4,128)}), f32[8,4,1152]{2,1,0:T(4,128)S(1)}, u32[]{:S(2)}, u32[]{:S(2)}) async-start(f32[8,4,1152]{2,1,0:T(4,128)} %get-tuple-element.11), calls=%async_computation | async-start | bytes 294912 | tf_op jit(solution)/shard_map/all_to_all | solution.py:261
  10.3 0.0 collective-permute-start
  10.3 2.5 %shard_map.164 = (f32[160,216]{1,0:T(8,128)S(1)}, f32[32,128]{1,0:T(8,128)S(1)}, bf16[1280,216]{1,0:T(8,128)(2,1)S(1)}, bf16[1280,216]{1,0:T(8,128)(2,1)S(1)}) custom-call(s32[1,32]{1,0:T(1,128)} %bitcast.16, s32[1,32]{1,0:T(1,128)} %bitcast.9, f32[32,1715]{1,0:T(8,128)} %refs_2_.1, bf16[1920,216]{1,0:T(8,128)(2,1)} %constant.14.clone.refs_3_, ...), custom_call_target="tpu_custom_call" | custom-call | bytes 4245120 | tf_op jit(solution)/shard_map/pallas_call | solution.py:250
  12.8 1.2 %collective-permute-done.refs_1_ = f32[64,256]{1,0:T(8,128)S(1)} collective-permute-done((f32[64,256]{1,0:T(8,128)S(1)}, f32[64,256]{1,0:T(8,128)S(1)}, u32[]{:S(2)}, u32[]{:S(2)}) %collective-permute-start) | collective-permute-done | bytes 65568 | tf_op jit(solution)/shard_map/ppermute | solution.py:267
  14.0 4.1 %all-to-all-done.refs_0_.refs_1_ = f32[8,4,1152]{2,1,0:T(4,128)S(1)} async-done(((f32[8,4,1152]{2,1,0:T(4,128)}), f32[8,4,1152]{2,1,0:T(4,128)S(1)}, u32[]{:S(2)}, u32[]{:S(2)}) %all-to-all-start) | async-done | bytes 147488 | tf_op jit(solution)/shard_map/all_to_all | solution.py:261
  18.1 1.1 %shard_map.165 = f32[8,4,1080]{2,1,0:T(4,128)S(1)} custom-call(f32[8,4,1152]{2,1,0:T(4,128)S(1)} %all-to-all-done.refs_0_.refs_1_, f32[64,256]{1,0:T(8,128)S(1)} %collective-permute-done.refs_1_, f32[160,216]{1,0:T(8,128)S(1)} %get-tuple-element.13.refs_2_, f32[32,128]{1,0:T(8,128)S(1)} %get-tuple-element.14.refs_3_, ...), custom_call_target="tpu_custom_call" | custom-call | bytes 1611776 | tf_op jit(solution)/shard_map/pallas_call | solution.py:250
  19.2 10.1 %all_to_all.10.refs_0_ = f32[8,4,1080]{2,1,0:T(4,128)S(1)} all-to-all(f32[8,4,1080]{2,1,0:T(4,128)S(1)} %shard_map.165), channel_id=1, replica_groups=mesh['gx'=2,'gy'=4,'gz'=4] {'gx','gy'}, dimensions={0} | all-to-all | bytes 276480 | tf_op jit(solution)/shard_map/all_to_all | solution.py:261
  29.3 0.9 %shard_map.166 = f32[32,1080]{1,0:T(8,128)} custom-call(f32[8,4,1080]{2,1,0:T(4,128)S(1)} %all_to_all.10.refs_0_, f32[8,4,1152]{2,1,0:T(4,128)S(1)} %all-to-all-done.refs_0_.refs_1_), custom_call_target="tpu_custom_call" | custom-call | bytes 423936 | tf_op jit(solution)/shard_map/pallas_call | solution.py:250
Async XLA Ops:
  3.0 15.1 %all-to-all-start = ((f32[8,4,1152]{2,1,0:T(4,128)}), f32[8,4,1152]{2,1,0:T(4,128)S(1)}, u32[]{:S(2)}, u32[]{:S(2)}) async-start(f32[8,4,1152]{2,1,0:T(4,128)} %get-tuple-element.11), calls=%async_computation | async-start | bytes 294912 | tf_op jit(solution)/shard_map/all_to_all | solution.py:261
  10.3 3.7 %collective-permute-start = (f32[64,256]{1,0:T(8,128)S(1)}, f32[64,256]{1,0:T(8,128)S(1)}, u32[]{:S(2)}, u32[]{:S(2)}) collective-permute-start(f32[64,256]{1,0:T(8,128)S(1)} %get-tuple-element.12), channel_id=1, source_target_pairs={{3,0},{0,1},{1,2},{2,3},{7,4},{4,5},{5,6},{6,7},{11,8},{8,9},{9,10... | collective-permute-start | bytes 196616 | tf_op jit(solution)/shard_map/ppermute | solution.py:267

commit v7 on v6

--- a/solution.py
+++ b/solution.py
@@ -160,46 +160,24 @@
     conf_out[:, SENT : SENT + 1] = conf_col
 
 
-def cell_kernel(peers, row_cap, get, y_out, col_out, face_high, face_low, spread):
-    order, crow = get(0), get(1)
-    elements = order.shape[1]
-    slots = peers * row_cap
-    place, _ = row_places(crow, peers, elements, row_cap)
-    take = onehot_rows(place, slots)
-    order_col = column(take, order.astype(jnp.float32))
-    elem_col = column(take, iota((1, elements), 1).astype(jnp.float32) + 1.0)
-    lane = iota((slots, 128), 1)
-    col_out[...] = jnp.where(lane == 0, order_col, jnp.where(lane == 1, elem_col, 0.0))
+def restrict_cells(take, order_col, adjoint, table_high, table_low, spread):
+    slots = take.shape[0]
     take = take.astype(jnp.bfloat16)
     spread[...] = jnp.zeros_like(spread)
-    for half, part in enumerate(halves(get(2))):
+    for half, part in enumerate(halves(adjoint)):
         moved = dot(take, part)
         for v in range(VARS):
             spread[half, v * slots : (v + 1) * slots, :CELL] = moved[:, v * CELL : (v + 1) * CELL]
     order_rows = jnp.concatenate([order_col] * VARS, axis=0)
-    high, low = spread[0], spread[1]
-    wide_high = jnp.concatenate([jnp.where(order_rows == float(p), high, 0.0).astype(jnp.bfloat16) for p in ORDERS], axis=1)
-    wide_low = jnp.concatenate([jnp.where(order_rows == float(p), low, 0.0).astype(jnp.bfloat16) for p in ORDERS], axis=1)
-    y_out[...] = dot3(wide_high, wide_low, get(3), get(4))
-    face_high[...] = get(5)
-    face_low[...] = get(6)
-
-
-def face_kernel(peers, row_cap, elements, groups, get, incoming, conf, y, cols, table_high, table_low, out, spread):
-    slots = peers * row_cap
-    message = incoming[...].reshape(slots, incoming.shape[2])
-    first_tag = groups * SENT
-    x = jnp.concatenate([*[message[:, g * SENT : (g + 1) * SENT] for g in range(groups)], conf[:, :SENT]], axis=0)
-    code_col = jnp.concatenate(
-        [*[message[:, first_tag + g : first_tag + g + 1] for g in range(groups)], conf[:, SENT : SENT + 1]], axis=0
-    )
-    count = x.shape[0]
-    code_row = jnp.sum(jnp.where(iota((count, count), 0) == iota((count, count), 1), code_col, 0.0), axis=0, keepdims=True)
-    order_col, elem_col = cols[:, 0:1], cols[:, 1:2]
-    wanted = jnp.concatenate([jnp.where(elem_col > 0.0, elem_col + float(f * elements), -1.0) for f in range(FACES)], axis=0)
-    gather = (wanted == code_row).astype(jnp.bfloat16)
-    high, low = halves(x)
-    face_sum = dot(gather, high) + dot(gather, low)
+    wide = [
+        jnp.concatenate([jnp.where(order_rows == float(p), spread[half], 0.0).astype(jnp.bfloat16) for p in ORDERS], axis=1)
+        for half in range(2)
+    ]
+    return dot3(*wide, table_high[...], table_low[...])
+
+
+def restrict_faces(face_sum, order_col, table_high, table_low, spread):
+    slots = order_col.shape[0]
     spread[...] = jnp.zeros_like(spread)
     for f in range(FACES):
         for v in range(VARS):
@@ -210,7 +188,47 @@
     z = spread[...]
     wide = jnp.concatenate([jnp.where(order_rows == float(p), z, 0.0) for p in ORDERS], axis=1)
     high, low = halves(wide)
-    total = y[...] + dot3(high, low, table_high[...], table_low[...])
+    return dot3(high, low, table_high[...], table_low[...])
+
+
+def rows_kernel(
+    peers,
+    row_cap,
+    elements,
+    groups,
+    get,
+    order,
+    crow,
+    adjoint,
+    cell_high,
+    cell_low,
+    face_high,
+    face_low,
+    incoming,
+    conf,
+    out,
+    cell_spread,
+    face_spread,
+):
+    slots = peers * row_cap
+    place, _ = row_places(crow[...], peers, elements, row_cap)
+    take = onehot_rows(place, slots)
+    order_col = column(take, order[...].astype(jnp.float32))
+    elem_col = column(take, iota((1, elements), 1).astype(jnp.float32) + 1.0)
+    total = restrict_cells(take, order_col, adjoint[...], cell_high, cell_low, cell_spread)
+    message = incoming[...].reshape(slots, incoming.shape[2])
+    first_tag = groups * SENT
+    x = jnp.concatenate([*[message[:, g * SENT : (g + 1) * SENT] for g in range(groups)], conf[:, :SENT]], axis=0)
+    code_col = jnp.concatenate(
+        [*[message[:, first_tag + g : first_tag + g + 1] for g in range(groups)], conf[:, SENT : SENT + 1]], axis=0
+    )
+    count = x.shape[0]
+    code_row = jnp.sum(jnp.where(iota((count, count), 0) == iota((count, count), 1), code_col, 0.0), axis=0, keepdims=True)
+    wanted = jnp.concatenate([jnp.where(elem_col > 0.0, elem_col + float(f * elements), -1.0) for f in range(FACES)], axis=0)
+    gather = (wanted == code_row).astype(jnp.bfloat16)
+    high, low = halves(x)
+    face_sum = dot(gather, high) + dot(gather, low)
+    total = total + restrict_faces(face_sum, order_col, face_high, face_low, face_spread)
     for v in range(VARS):
         out[:, :, v * ROW : (v + 1) * ROW] = total[v * slots : (v + 1) * slots].reshape(peers, row_cap, ROW)
 
@@ -227,10 +245,12 @@
     out[...] = dot(put, high) + dot(put, low) + dot(put, rest)
 
 
-def fetched(kernel, n_far, n_near, n_out, *refs):
+def fetched(kernel, n_far, n_pass, n_near, n_out, *refs):
     far, near, outs = refs[:n_far], refs[n_far : n_far + n_near], refs[n_far + n_near : n_far + n_near + n_out]
     rest = refs[n_far + n_near + n_out :]
-    held, sems, scratch = rest[:n_far], rest[n_far], rest[n_far + 1 :]
+    n_held = n_far - n_pass
+    held, sems, scratch = rest[:n_held], rest[n_held], rest[n_held + 1 :]
+    held = (*held, *outs[n_out - n_pass :])
     copies = [pltpu.make_async_copy(src, dst, sems.at[i]) for i, (src, dst) in enumerate(zip(far, held))]
     for copy in copies:
         copy.start()
@@ -239,19 +259,26 @@
         copies[i].wait()
         return held[i][...]
 
-    kernel(get, *near, *outs, *scratch)
-
-
-def call(kernel, outs, far, near=(), scratch=(), flops=0):
-    shapes = jax.tree.leaves(outs)
-    sizes = [np.prod(a.shape) * a.dtype.itemsize for a in (*far, *near, *shapes)]
+    kernel(get, *near, *outs[: n_out - n_pass], *scratch)
+    for copy in copies[n_held:]:
+        copy.wait()
+
+
+def like(a):
+    return jax.ShapeDtypeStruct(a.shape, a.dtype)
+
+
+def call(kernel, outs, far, near=(), scratch=(), hand_on=(), flops=0):
+    outs = [*outs, *[like(a) for a in hand_on]]
+    sizes = [np.prod(a.shape) * a.dtype.itemsize for a in (*far, *near, *outs)]
+    held = [pltpu.VMEM(a.shape, a.dtype) for a in far]
+    far = (*far, *hand_on)
     in_specs = [pl.BlockSpec(memory_space=pltpu.HBM)] * len(far) + [pl.BlockSpec(memory_space=pltpu.VMEM)] * len(near)
-    scratch = [*[pltpu.VMEM(a.shape, a.dtype) for a in far], pltpu.SemaphoreType.DMA((max(1, len(far)),)), *scratch]
     return pl.pallas_call(
-        functools.partial(fetched, kernel, len(far), len(near), len(shapes)),
+        functools.partial(fetched, kernel, len(far), len(hand_on), len(near), len(outs)),
         in_specs=in_specs,
         out_shape=outs,
-        scratch_shapes=scratch,
+        scratch_shapes=[*held, pltpu.SemaphoreType.DMA((max(1, len(far)),)), *scratch],
         compiler_params=pltpu.CompilerParams(vmem_limit_bytes=48 * 1024 * 1024),
         cost_estimate=pl.CostEstimate(flops=flops, bytes_accessed=int(sum(sizes)), transcendentals=0),
     )(*[pltpu.with_memory_space_constraint(a, pltpu.HBM) for a in far], *near)
@@ -293,9 +320,9 @@
     f32 = jnp.float32
     line = lambda a: a.reshape(1, -1)
     order, coarse_row = line(order), line(coarse_row)
-    outgoing, conf = call(
+    outgoing, conf, *whole = call(
         functools.partial(pack_kernel, peers, cap, row_cap, elements),
-        (jax.ShapeDtypeStruct((peers, row_cap, lanes), f32), jax.ShapeDtypeStruct((confs, TRACE_PAD), f32)),
+        [jax.ShapeDtypeStruct((peers, row_cap, lanes), f32), jax.ShapeDtypeStruct((confs, TRACE_PAD), f32)],
         (
             line(mortar_dest),
             line(mortar_elem),
@@ -308,33 +335,24 @@
             conf_trace,
             *lift,
         ),
-    )
+        hand_on=(order, coarse_row, adjoint, *cell, *face),
+    )
+    conf = from_behind(conf, "gz", 1)
     incoming = exchange(outgoing)
-    conf = from_behind(conf, "gz", 1)
-    y, cols, *face = call(
-        functools.partial(cell_kernel, peers, row_cap),
-        (
-            jax.ShapeDtypeStruct((VARS * slots, ROW), f32),
-            jax.ShapeDtypeStruct((slots, 128), f32),
-            *[jax.ShapeDtypeStruct(t.shape, t.dtype) for t in face],
-        ),
-        (order, coarse_row, adjoint, *cell, *face),
-        scratch=[pltpu.VMEM((2, VARS * slots, CELL_PAD), f32)],
-    )
-    rows = call(
-        functools.partial(face_kernel, peers, row_cap, elements, groups),
-        jax.ShapeDtypeStruct((peers, row_cap, VARS * ROW), f32),
+    (rows,) = call(
+        functools.partial(rows_kernel, peers, row_cap, elements, groups),
+        [jax.ShapeDtypeStruct((peers, row_cap, VARS * ROW), f32)],
         (),
-        (incoming, conf, y, cols, *face),
-        scratch=[pltpu.VMEM((VARS * slots, FACES_PAD), f32)],
-    )
-    arrived = exchange(rows)
-    return call(
+        (*whole, incoming, conf),
+        scratch=[pltpu.VMEM((2, VARS * slots, CELL_PAD), f32), pltpu.VMEM((VARS * slots, FACES_PAD), f32)],
+    )
+    (out,) = call(
         functools.partial(place_kernel, peers, row_cap, groups * (SENT + 1)),
-        jax.ShapeDtypeStruct((elements, VARS * ROW), f32),
+        [jax.ShapeDtypeStruct((elements, VARS * ROW), f32)],
         (),
-        (arrived, incoming),
-    )
+        (exchange(rows), incoming),
+    )
+    return out
 
 
 def solution(mesh):

time: 30.5 us -> 34.4 us (1.13)
  local copies, waits for them, and re-layouts: 0 us -> 2.9 us
  waiting for transfers between devices: 5.33 us -> 7.81 us
  Pallas kernels: 7.51 us -> 6.02 us
    unnamed x0 -> x8, local copies, waits for them, and re-layouts: none -> 2.9 us
    ppermute x1, waiting for transfers between devices: 1.2 us -> 3.89 us  [from_behind(): return lax.ppermute(block, axis, route)]
    pallas_call x4 -> x3, Pallas kernels: 7.51 us -> 6.02 us  [call(): pl.pallas_call(functools.partial(fetched, kernel, len(far), len(hand_on),...]
  transfers between devices with their start and end apart: 2 -> 2, of which waited for: 2 -> 2; matrix products, arithmetic and copies ran while one was open for 0% -> 0% of each run, Pallas kernels for 8% -> 0%
where the time goes in v7:
time: 34.4 us; the launch traced here: 34.1 us
  blocking collectives  10 us (29%)
  waiting for transfers between devices  7.81 us (23%)
  starting transfers between devices  7.28 us (21%)
  Pallas kernels  6.02 us (18%)
  local copies, waits for them, and re-layouts  2.9 us (8%)
    all_to_all x1, blocking collectives, exchange(): lax.all_to_all(block, ('gx', 'gy'), split_axis=0, concat_axis=0, tiled=True)  10 us
    all_to_all x1, starting transfers between devices, exchange(): lax.all_to_all(block, ('gx', 'gy'), split_axis=0, concat_axis=0, tiled=True)  7.28 us
    pallas_call x3, Pallas kernels, call(): pl.pallas_call(functools.partial(fetched, kernel, len(far), len(hand_on),...  6.02 us
    all_to_all x1, waiting for transfers between devices, exchange(): lax.all_to_all(block, ('gx', 'gy'), split_axis=0, concat_axis=0, tiled=True)  3.91 us
    ppermute x1, waiting for transfers between devices, from_behind(): return lax.ppermute(block, axis, route)  3.89 us
    unnamed x8, local copies, waits for them, and re-layouts  2.9 us
  transfers between devices with their start and end apart: 2, of which 2 were waited for; matrix products, arithmetic and copies ran while one was open for 0% of the time, Pallas kernels for 0%

profile of v7, /device:TPU:0, one launch (start us, length us, event | category | flops | bytes accessed | tf_op | source)
XLA Modules:
  0.0 34.1 jit_solution(417188475302771156)
XLA Ops:
  0.0 2.7 %shard_map.163 = (f32[8,4,1152]{2,1,0:T(4,128)S(1)}, f32[64,256]{1,0:T(8,128)S(1)}, s32[1,32]{1,0:T(1,128)S(1)}, s32[1,32]{1,0:T(1,128)S(1)}, f32[32,1715]{1,0:T...) custom-call(s32[1,96]{1,0:T(1,128)} %bitcast.10, ...), custom_call_target="tpu_custom_call" | custom-call | bytes 4278144 | tf_op jit(solution)/shard_map/pallas_call | solution.py:277
  2.7 0.0 copy-start
  2.7 0.7 %copy-done = f32[32,1715]{1,0:T(8,128)} copy-done((f32[32,1715]{1,0:T(8,128)}, f32[32,1715]{1,0:T(8,128)S(1)}, u32[]{:S(2)}) %copy-start) | copy-done | bytes 219544
  3.4 0.0 copy-start.2
  3.4 0.7 %copy-done.2 = f32[8,4,1152]{2,1,0:T(4,128)} copy-done((f32[8,4,1152]{2,1,0:T(4,128)}, f32[8,4,1152]{2,1,0:T(4,128)S(1)}, u32[]{:S(2)}) %copy-start.2) | copy-done | bytes 147480
  4.1 0.0 copy-start.3
  4.1 0.6 %copy-done.3 = f32[64,256]{1,0:T(8,128)} copy-done((f32[64,256]{1,0:T(8,128)}, f32[64,256]{1,0:T(8,128)S(1)}, u32[]{:S(2)}) %copy-start.3) | copy-done | bytes 65560
  4.7 7.3 %all-to-all-start = ((f32[8,4,1152]{2,1,0:T(4,128)}), f32[8,4,1152]{2,1,0:T(4,128)S(1)}, u32[]{:S(2)}, u32[]{:S(2)}) async-start(f32[8,4,1152]{2,1,0:T(4,128)} %copy-done.2), calls=%async_computation | async-start | bytes 294912 | tf_op jit(solution)/shard_map/all_to_all | solution.py:288
  12.0 0.0 collective-permute-start
  12.0 3.9 %collective-permute-done.refs_8_ = f32[64,256]{1,0:T(8,128)S(1)} collective-permute-done((f32[64,256]{1,0:T(8,128)}, f32[64,256]{1,0:T(8,128)S(1)}, u32[]{:S(2)}, u32[]{:S(2)}) %collective-permute-start) | collective-permute-done | bytes 65568 | tf_op jit(solution)/shard_map/ppermute | solution.py:294
  15.9 3.9 %all-to-all-done.refs_7_.refs_1_ = f32[8,4,1152]{2,1,0:T(4,128)S(1)} async-done(((f32[8,4,1152]{2,1,0:T(4,128)}), f32[8,4,1152]{2,1,0:T(4,128)S(1)}, u32[]{:S(2)}, u32[]{:S(2)}) %all-to-all-start) | async-done | bytes 147488 | tf_op jit(solution)/shard_map/all_to_all | solution.py:288
  19.8 0.0 copy-start.1
  19.8 0.9 %copy-done.1 = f32[32,1715]{1,0:T(8,128)S(1)} copy-done((f32[32,1715]{1,0:T(8,128)S(1)}, f32[32,1715]{1,0:T(8,128)}, u32[]{:S(2)}) %copy-start.1) | copy-done | bytes 219544
  20.7 2.4 %shard_map.164 = f32[8,4,1080]{2,1,0:T(4,128)S(1)} custom-call(s32[1,32]{1,0:T(1,128)S(1)} %get-tuple-element.14.refs_0_, s32[1,32]{1,0:T(1,128)S(1)} %get-tuple-element.15.refs_1_, f32[32,1715]{1,0:T(8,128)S(1)} %copy-done.1, bf16[1920,216]{1,0:T(8,128)(2,1)S(1)} %get-tuple-element.17.refs_3_, bf16[1920,216]{1,0:T(8,128)(2,1)S(1)} %get-tuple-element.18.refs_4_, ...), custom_call_target="tpu_custom_call" | custom-call | bytes 3335808 | tf_op jit(solution)/shard_map/pallas_call | solution.py:277
  23.1 10.0 %all_to_all.10.refs_0_ = f32[8,4,1080]{2,1,0:T(4,128)S(1)} all-to-all(f32[8,4,1080]{2,1,0:T(4,128)S(1)} %shard_map.164), channel_id=1, replica_groups=mesh['gx'=2,'gy'=4,'gz'=4] {'gx','gy'}, dimensions={0} | all-to-all | bytes 276480 | tf_op jit(solution)/shard_map/all_to_all | solution.py:288
  33.1 0.9 %shard_map.165 = f32[32,1080]{1,0:T(8,128)} custom-call(f32[8,4,1080]{2,1,0:T(4,128)S(1)} %all_to_all.10.refs_0_, f32[8,4,1152]{2,1,0:T(4,128)S(1)} %all-to-all-done.refs_7_.refs_1_), custom_call_target="tpu_custom_call" | custom-call | bytes 423936 | tf_op jit(solution)/shard_map/pallas_call | solution.py:277
Async XLA Ops:
  2.7 0.7 %copy-start = (f32[32,1715]{1,0:T(8,128)}, f32[32,1715]{1,0:T(8,128)S(1)}, u32[]{:S(2)}) copy-start(f32[32,1715]{1,0:T(8,128)S(1)} %get-tuple-element.16.refs_2_) | copy-start | bytes 658564
  3.4 0.7 %copy-start.2 = (f32[8,4,1152]{2,1,0:T(4,128)}, f32[8,4,1152]{2,1,0:T(4,128)S(1)}, u32[]{:S(2)}) copy-start(f32[8,4,1152]{2,1,0:T(4,128)S(1)} %get-tuple-element.21) | copy-start | bytes 442372
  4.1 0.6 %copy-start.3 = (f32[64,256]{1,0:T(8,128)}, f32[64,256]{1,0:T(8,128)S(1)}, u32[]{:S(2)}) copy-start(f32[64,256]{1,0:T(8,128)S(1)} %get-tuple-element.22) | copy-start | bytes 196612
  4.7 15.1 %all-to-all-start = ((f32[8,4,1152]{2,1,0:T(4,128)}), f32[8,4,1152]{2,1,0:T(4,128)S(1)}, u32[]{:S(2)}, u32[]{:S(2)}) async-start(f32[8,4,1152]{2,1,0:T(4,128)} %copy-done.2), calls=%async_computation | async-start | bytes 294912 | tf_op jit(solution)/shard_map/all_to_all | solution.py:288
  12.0 3.9 %collective-permute-start = (f32[64,256]{1,0:T(8,128)}, f32[64,256]{1,0:T(8,128)S(1)}, u32[]{:S(2)}, u32[]{:S(2)}) collective-permute-start(f32[64,256]{1,0:T(8,128)} %copy-done.3), channel_id=1, source_target_pairs={{3,0},{0,1},{1,2},{2,3},{7,4},{4,5},{5,6},{6,7},{11,8},{8,9},{9,10... | collective-permute-start | bytes 196616 | tf_op jit(solution)/shard_map/ppermute | solution.py:294
  19.8 0.9 %copy-start.1 = (f32[32,1715]{1,0:T(8,128)S(1)}, f32[32,1715]{1,0:T(8,128)}, u32[]{:S(2)}) copy-start(f32[32,1715]{1,0:T(8,128)} %copy-done) | copy-start | bytes 658564

commit v8 on v6

--- a/solution.py
+++ b/solution.py
@@ -70,7 +70,8 @@
                 first = (2 * axis + side) * FACE_PAD
                 face[index, first : first + FLAT] = np.einsum(spec, edge, lower, lower).reshape(FLAT, ROW)
     return (
-        split_table(lift.reshape(-1, SENT)),
+        split_table(lift[:4].reshape(-1, SENT)),
+        split_table(lift[4]),
         split_table(cell.reshape(-1, ROW)),
         split_table(face.reshape(-1, ROW)),
     )
@@ -126,9 +127,18 @@
     return jnp.concatenate([x, jnp.zeros((x.shape[0], lanes - x.shape[1]), x.dtype)], axis=1)
 
 
-def pack_kernel(peers, cap, row_cap, elements, get, out, conf_out):
-    dest, elem, face, sub, crow, cface, celem = [get(i) for i in range(7)]
-    count, confs = dest.shape[1], cface.shape[1]
+def conf_kernel(elements, get, out):
+    cface, celem = get(0), get(1)
+    confs = cface.shape[1]
+    eye = (iota((confs, confs), 0) == iota((confs, confs), 1)).astype(jnp.float32)
+    code_col = column(eye, (cface * elements + celem + 1).astype(jnp.float32))
+    out[...] = jnp.where(iota((confs, TRACE_PAD), 1) == TRACE, code_col, pad_lanes(get(2), TRACE_PAD))
+
+
+def pack_kernel(peers, cap, row_cap, elements, get, *refs):
+    *ints, trace, table_high, table_low, out = refs
+    dest, elem, face, sub, crow = [ref[...] for ref in ints]
+    count = dest.shape[1]
     groups, slots = -(-cap // row_cap), peers * row_cap
     member = (iota((peers, count), 0) == dest).astype(jnp.float32)
     rank = jnp.sum(member * earlier(member), axis=0, keepdims=True)
@@ -140,11 +150,9 @@
     row_col = column(onehot_rows(row_place, slots), row_slot + 1.0)
     eye = (iota((count, count), 0) == iota((count, count), 1)).astype(jnp.float32)
     sub_col = column(eye, sub.astype(jnp.float32))
-    x = pad_lanes(get(7), TRACE_PAD)
+    x = pad_lanes(trace[...], TRACE_PAD)
     wide = jnp.concatenate([jnp.where(sub_col == float(s), x, 0.0) for s in range(4)], axis=1)
-    table_high, table_low = get(9), get(10)
-    split = 4 * TRACE_PAD
-    lifted = dot3(*halves(wide), table_high[:split], table_low[:split])
+    lifted = dot3(*halves(wide), table_high[...], table_low[...])
     lifted_high, lifted_low = halves(lifted)
     put = put.astype(jnp.bfloat16)
     packed = dot(put, lifted_high) + dot(put, lifted_low)
@@ -153,14 +161,9 @@
         out[:, :, g * SENT : (g + 1) * SENT] = part.reshape(peers, row_cap, SENT)
     tags = jnp.concatenate([*[code_col[g * slots : (g + 1) * slots] for g in range(groups)], row_col], axis=1)
     out[:, :, groups * SENT : groups * (SENT + 1) + 1] = tags.reshape(peers, row_cap, groups + 1)
-    eye = (iota((confs, confs), 0) == iota((confs, confs), 1)).astype(jnp.float32)
-    conf_col = column(eye, (cface * elements + celem + 1).astype(jnp.float32))
-    conf = dot3(*halves(pad_lanes(get(8), TRACE_PAD)), table_high[split:], table_low[split:])
-    conf_out[:, :SENT] = conf
-    conf_out[:, SENT : SENT + 1] = conf_col
-
-
-def cell_kernel(peers, row_cap, get, y_out, col_out, face_high, face_low, spread):
+
+
+def cell_kernel(peers, row_cap, get, conf, y_out, col_out, conf_out, spread):
     order, crow = get(0), get(1)
     elements = order.shape[1]
     slots = peers * row_cap
@@ -181,8 +184,8 @@
     wide_high = jnp.concatenate([jnp.where(order_rows == float(p), high, 0.0).astype(jnp.bfloat16) for p in ORDERS], axis=1)
     wide_low = jnp.concatenate([jnp.where(order_rows == float(p), low, 0.0).astype(jnp.bfloat16) for p in ORDERS], axis=1)
     y_out[...] = dot3(wide_high, wide_low, get(3), get(4))
-    face_high[...] = get(5)
-    face_low[...] = get(6)
+    conf_out[:, :SENT] = dot3(*halves(conf[...]), get(5), get(6))
+    conf_out[:, SENT : SENT + 1] = conf[:, TRACE : TRACE + 1]
 
 
 def face_kernel(peers, row_cap, elements, groups, get, incoming, conf, y, cols, table_high, table_low, out, spread):
@@ -227,10 +230,12 @@
     out[...] = dot(put, high) + dot(put, low) + dot(put, rest)
 
 
-def fetched(kernel, n_far, n_near, n_out, *refs):
+def fetched(kernel, n_far, n_pass, n_near, n_out, *refs):
     far, near, outs = refs[:n_far], refs[n_far : n_far + n_near], refs[n_far + n_near : n_far + n_near + n_out]
     rest = refs[n_far + n_near + n_out :]
-    held, sems, scratch = rest[:n_far], rest[n_far], rest[n_far + 1 :]
+    n_held = n_far - n_pass
+    held, sems, scratch = rest[:n_held], rest[n_held], rest[n_held + 1 :]
+    held = (*held, *outs[n_out - n_pass :])
     copies = [pltpu.make_async_copy(src, dst, sems.at[i]) for i, (src, dst) in enumerate(zip(far, held))]
     for copy in copies:
         copy.start()
@@ -239,19 +244,26 @@
         copies[i].wait()
         return held[i][...]
 
-    kernel(get, *near, *outs, *scratch)
-
-
-def call(kernel, outs, far, near=(), scratch=(), flops=0):
-    shapes = jax.tree.leaves(outs)
-    sizes = [np.prod(a.shape) * a.dtype.itemsize for a in (*far, *near, *shapes)]
+    kernel(get, *near, *outs[: n_out - n_pass], *scratch)
+    for copy in copies[n_held:]:
+        copy.wait()
+
+
+def like(a):
+    return jax.ShapeDtypeStruct(a.shape, a.dtype)
+
+
+def call(kernel, outs, far, near=(), scratch=(), hand_on=(), flops=0):
+    outs = [*outs, *[like(a) for a in hand_on]]
+    sizes = [np.prod(a.shape) * a.dtype.itemsize for a in (*far, *near, *outs)]
+    held = [pltpu.VMEM(a.shape, a.dtype) for a in far]
+    far = (*far, *hand_on)
     in_specs = [pl.BlockSpec(memory_space=pltpu.HBM)] * len(far) + [pl.BlockSpec(memory_space=pltpu.VMEM)] * len(near)
-    scratch = [*[pltpu.VMEM(a.shape, a.dtype) for a in far], pltpu.SemaphoreType.DMA((max(1, len(far)),)), *scratch]
     return pl.pallas_call(
-        functools.partial(fetched, kernel, len(far), len(near), len(shapes)),
+        functools.partial(fetched, kernel, len(far), len(hand_on), len(near), len(outs)),
         in_specs=in_specs,
         out_shape=outs,
-        scratch_shapes=scratch,
+        scratch_shapes=[*held, pltpu.SemaphoreType.DMA((max(1, len(far)),)), *scratch],
         compiler_params=pltpu.CompilerParams(vmem_limit_bytes=48 * 1024 * 1024),
         cost_estimate=pl.CostEstimate(flops=flops, bytes_accessed=int(sum(sizes)), transcendentals=0),
     )(*[pltpu.with_memory_space_constraint(a, pltpu.HBM) for a in far], *near)
@@ -289,52 +301,58 @@
     slots = peers * row_cap
     groups = -(-cap // row_cap)
     lanes = -(-(groups * (SENT + 1) + 1) // 128) * 128
-    lift, cell, face = [tuple(jnp.asarray(t) for t in pair) for pair in basis_tables()]
+    lift, conf_lift, cell, face = [tuple(jnp.asarray(t) for t in pair) for pair in basis_tables()]
     f32 = jnp.float32
     line = lambda a: a.reshape(1, -1)
     order, coarse_row = line(order), line(coarse_row)
-    outgoing, conf = call(
-        functools.partial(pack_kernel, peers, cap, row_cap, elements),
-        (jax.ShapeDtypeStruct((peers, row_cap, lanes), f32), jax.ShapeDtypeStruct((confs, TRACE_PAD), f32)),
-        (
+    conf, *mortar = call(
+        functools.partial(conf_kernel, elements),
+        [jax.ShapeDtypeStruct((confs, TRACE_PAD), f32)],
+        (line(conf_face), line(conf_elem), conf_trace),
+        hand_on=(
             line(mortar_dest),
             line(mortar_elem),
             line(mortar_face),
             line(mortar_sub),
             coarse_row,
-            line(conf_face),
-            line(conf_elem),
             mortar_trace,
-            conf_trace,
             *lift,
         ),
     )
+    conf = from_behind(conf, "gz", 1)
+    (outgoing,) = call(
+        functools.partial(pack_kernel, peers, cap, row_cap, elements),
+        [jax.ShapeDtypeStruct((peers, row_cap, lanes), f32)],
+        (),
+        mortar,
+    )
     incoming = exchange(outgoing)
-    conf = from_behind(conf, "gz", 1)
-    y, cols, *face = call(
+    y, cols, conf, *face = call(
         functools.partial(cell_kernel, peers, row_cap),
-        (
+        [
             jax.ShapeDtypeStruct((VARS * slots, ROW), f32),
             jax.ShapeDtypeStruct((slots, 128), f32),
-            *[jax.ShapeDtypeStruct(t.shape, t.dtype) for t in face],
-        ),
-        (order, coarse_row, adjoint, *cell, *face),
+            jax.ShapeDtypeStruct((confs, TRACE_PAD), f32),
+        ],
+        (order, coarse_row, adjoint, *cell, *conf_lift),
+        (conf,),
         scratch=[pltpu.VMEM((2, VARS * slots, CELL_PAD), f32)],
-    )
-    rows = call(
+        hand_on=face,
+    )
+    (rows,) = call(
         functools.partial(face_kernel, peers, row_cap, elements, groups),
-        jax.ShapeDtypeStruct((peers, row_cap, VARS * ROW), f32),
+        [jax.ShapeDtypeStruct((peers, row_cap, VARS * ROW), f32)],
         (),
         (incoming, conf, y, cols, *face),
         scratch=[pltpu.VMEM((VARS * slots, FACES_PAD), f32)],
     )
-    arrived = exchange(rows)
-    return call(
+    (out,) = call(
         functools.partial(place_kernel, peers, row_cap, groups * (SENT + 1)),
-        jax.ShapeDtypeStruct((elements, VARS * ROW), f32),
+        [jax.ShapeDtypeStruct((elements, VARS * ROW), f32)],
         (),
-        (arrived, incoming),
-    )
+        (exchange(rows), incoming),
+    )
+    return out
 
 
 def solution(mesh):

time: 30.5 us -> 32.5 us (1.066)
  blocking collectives: 10.1 us -> 12 us
    all_to_all x1, waiting for transfers between devices: 4.12 us -> 1.42 us  [exchange(): lax.all_to_all(block, ('gx', 'gy'), split_axis=0, concat_axis=0, tiled=True)]
    ppermute x1, waiting for transfers between devices: 1.2 us -> 3.68 us  [from_behind(): return lax.ppermute(block, axis, route)]
    all_to_all x1, blocking collectives: 10.1 us -> 12 us  [exchange(): lax.all_to_all(block, ('gx', 'gy'), split_axis=0, concat_axis=0, tiled=True)]
    pallas_call x4 -> x5, Pallas kernels: 7.51 us -> 7.7 us  [call(): pl.pallas_call(functools.partial(fetched, kernel, len(far), len(hand_on),...]
where the time goes in v8:
time: 32.5 us; the launch traced here: 32.2 us
  blocking collectives  12 us (37%)
  Pallas kernels  7.7 us (24%)
  starting transfers between devices  7.3 us (22%)
  waiting for transfers between devices  5.1 us (16%)
    all_to_all x1, blocking collectives, exchange(): lax.all_to_all(block, ('gx', 'gy'), split_axis=0, concat_axis=0, tiled=True)  12 us
    pallas_call x5, Pallas kernels, call(): pl.pallas_call(functools.partial(fetched, kernel, len(far), len(hand_on),...  7.7 us
    all_to_all x1, starting transfers between devices, exchange(): lax.all_to_all(block, ('gx', 'gy'), split_axis=0, concat_axis=0, tiled=True)  7.3 us
    ppermute x1, waiting for transfers between devices, from_behind(): return lax.ppermute(block, axis, route)  3.68 us
    all_to_all x1, waiting for transfers between devices, exchange(): lax.all_to_all(block, ('gx', 'gy'), split_axis=0, concat_axis=0, tiled=True)  1.42 us
  transfers between devices with their start and end apart: 2, of which 2 were waited for; matrix products, arithmetic and copies ran while one was open for 0% of the time, Pallas kernels for 8%

profile of v8, /device:TPU:0, one launch (start us, length us, event | category | flops | bytes accessed | tf_op | source)
XLA Modules:
  0.0 32.2 jit_solution(1165224842228748683)
XLA Ops:
  0.0 1.5 %shard_map.181 = (f32[64,256]{1,0:T(8,128)S(1)}, s32[1,96]{1,0:T(1,128)S(1)}, s32[1,96]{1,0:T(1,128)S(1)}, s32[1,96]{1,0:T(1,128)S(1)}, s32[1,96]{1,0:T(1,128)S(...) custom-call(s32[1,64]{1,0:T(1,128)} %bitcast.10, ...), custom_call_target="tpu_custom_call" | custom-call | bytes 961792 | tf_op jit(solution)/shard_map/pallas_call | solution.py:262
  1.5 1.5 %shard_map.182 = f32[8,4,1152]{2,1,0:T(4,128)} custom-call(s32[1,96]{1,0:T(1,128)S(1)} %get-tuple-element.19.refs_0_, s32[1,96]{1,0:T(1,128)S(1)} %get-tuple-element.20.refs_1_, s32[1,96]{1,0:T(1,128)S(1)} %get-tuple-element.21.refs_2_, s32[1,96]{1,0:T(1,128)S(1)} %get-tuple-element.22.refs_3_, s32[1,32]{1,0:T(1,128)S(1)} %get-tuple-element.23.refs_4_, ...), custom_call_target="tpu_custom_call" | custom-call | bytes 980480 | tf_op jit(solution)/shard_map/pallas_call | solution.py:262
  3.0 7.3 %all-to-all-start = ((f32[8,4,1152]{2,1,0:T(4,128)}), f32[8,4,1152]{2,1,0:T(4,128)S(1)}, u32[]{:S(2)}, u32[]{:S(2)}) async-start(f32[8,4,1152]{2,1,0:T(4,128)} %shard_map.182), calls=%async_computation | async-start | bytes 294912 | tf_op jit(solution)/shard_map/all_to_all | solution.py:273
  10.3 0.0 collective-permute-start
  10.3 3.7 %collective-permute-done.refs_9_ = f32[64,256]{1,0:T(8,128)S(1)} collective-permute-done((f32[64,256]{1,0:T(8,128)S(1)}, f32[64,256]{1,0:T(8,128)S(1)}, u32[]{:S(2)}, u32[]{:S(2)}) %collective-permute-start) | collective-permute-done | bytes 65568 | tf_op jit(solution)/shard_map/ppermute | solution.py:279
  14.0 2.7 %shard_map.183 = (f32[160,216]{1,0:T(8,128)S(1)}, f32[32,128]{1,0:T(8,128)S(1)}, f32[64,256]{1,0:T(8,128)S(1)}, bf16[1280,216]{1,0:T(8,128)(2,1)S(1)}, bf16[1280,216]{1,0:T(8,128)(2,1)S(1)}) custom-call(s32[1,32]{1,0:T(1,128)} %bitcast.16, s32[1,32]{1,0:T(1,128)} %bitcast.9, f32[32,1715]{1,0:T(8,128)} %refs_2_.3, bf16[1920,216]{1,0:T(8,128)(2,1)} %constant.20.clone.refs_3_, ...), custom_call_target="tpu_custom_call" | custom-call | bytes 3454592 | tf_op jit(solution)/shard_map/pallas_call | solution.py:262
  16.7 1.4 %all-to-all-done.refs_0_.refs_1_ = f32[8,4,1152]{2,1,0:T(4,128)S(1)} async-done(((f32[8,4,1152]{2,1,0:T(4,128)}), f32[8,4,1152]{2,1,0:T(4,128)S(1)}, u32[]{:S(2)}, u32[]{:S(2)}) %all-to-all-start) | async-done | bytes 147488 | tf_op jit(solution)/shard_map/all_to_all | solution.py:273
  18.1 1.1 %shard_map.184 = f32[8,4,1080]{2,1,0:T(4,128)S(1)} custom-call(f32[8,4,1152]{2,1,0:T(4,128)S(1)} %all-to-all-done.refs_0_.refs_1_, f32[64,256]{1,0:T(8,128)S(1)} %get-tuple-element.28.refs_1_, f32[160,216]{1,0:T(8,128)S(1)} %get-tuple-element.29.refs_2_, f32[32,128]{1,0:T(8,128)S(1)} %get-tuple-element.30.refs_3_, ...), custom_call_target="tpu_custom_call" | custom-call | bytes 1611776 | tf_op jit(solution)/shard_map/pallas_call | solution.py:262
  19.2 12.0 %all_to_all.10.refs_0_ = f32[8,4,1080]{2,1,0:T(4,128)S(1)} all-to-all(f32[8,4,1080]{2,1,0:T(4,128)S(1)} %shard_map.184), channel_id=1, replica_groups=mesh['gx'=2,'gy'=4,'gz'=4] {'gx','gy'}, dimensions={0} | all-to-all | bytes 276480 | tf_op jit(solution)/shard_map/all_to_all | solution.py:273
  31.2 0.9 %shard_map.185 = f32[32,1080]{1,0:T(8,128)} custom-call(f32[8,4,1080]{2,1,0:T(4,128)S(1)} %all_to_all.10.refs_0_, f32[8,4,1152]{2,1,0:T(4,128)S(1)} %all-to-all-done.refs_0_.refs_1_), custom_call_target="tpu_custom_call" | custom-call | bytes 423936 | tf_op jit(solution)/shard_map/pallas_call | solution.py:262
Async XLA Ops:
  3.0 15.1 %all-to-all-start = ((f32[8,4,1152]{2,1,0:T(4,128)}), f32[8,4,1152]{2,1,0:T(4,128)S(1)}, u32[]{:S(2)}, u32[]{:S(2)}) async-start(f32[8,4,1152]{2,1,0:T(4,128)} %shard_map.182), calls=%async_computation | async-start | bytes 294912 | tf_op jit(solution)/shard_map/all_to_all | solution.py:273
  10.3 3.7 %collective-permute-start = (f32[64,256]{1,0:T(8,128)S(1)}, f32[64,256]{1,0:T(8,128)S(1)}, u32[]{:S(2)}, u32[]{:S(2)}) collective-permute-start(f32[64,256]{1,0:T(8,128)S(1)} %get-tuple-element.27), channel_id=1, source_target_pairs={{3,0},{0,1},{1,2},{2,3},{7,4},{4,5},{5,6},{6,7},{11,8},{8,9},{9,10... | collective-permute-start | bytes 196616 | tf_op jit(solution)/shard_map/ppermute | solution.py:279

commit v9 on v6

--- a/solution.py
+++ b/solution.py
@@ -100,17 +100,24 @@
     return dot(member.astype(jnp.bfloat16), before.astype(jnp.bfloat16))
 
 
+def device_of(shape):
+    size_x, size_y = lax.axis_size("gx"), lax.axis_size("gy")
+    rank = iota(shape, 0)
+    return rank % size_x * size_y + rank // size_x
+
+
 def owner_of(crow, peers, elements):
-    first = iota((peers, crow.shape[1]), 0) * elements
+    first = device_of((peers, crow.shape[1])) * elements
     return ((crow >= first) & (crow < first + elements)).astype(jnp.float32)
 
 
 def row_places(crow, peers, elements, stride):
     member = owner_of(crow, peers, elements)
     rank = earlier(member)
-    base = iota(member.shape, 0).astype(jnp.float32)
-    place = jnp.sum(member * (base * stride + rank), axis=0, keepdims=True)
-    slot = crow.astype(jnp.float32) - jnp.sum(member * (base * elements), axis=0, keepdims=True)
+    block = iota(member.shape, 0).astype(jnp.float32)
+    place = jnp.sum(member * (block * stride + rank), axis=0, keepdims=True)
+    owned = (device_of(member.shape) * elements).astype(jnp.float32)
+    slot = crow.astype(jnp.float32) - jnp.sum(member * owned, axis=0, keepdims=True)
     return place, slot
 
 
@@ -130,10 +137,11 @@
     dest, elem, face, sub, crow, cface, celem = [get(i) for i in range(7)]
     count, confs = dest.shape[1], cface.shape[1]
     groups, slots = -(-cap // row_cap), peers * row_cap
-    member = (iota((peers, count), 0) == dest).astype(jnp.float32)
+    member = (device_of((peers, count)) == dest).astype(jnp.float32)
+    block = jnp.sum(member * iota(member.shape, 0).astype(jnp.float32), axis=0, keepdims=True)
     rank = jnp.sum(member * earlier(member), axis=0, keepdims=True)
     group = sum([(rank >= float(g * row_cap)).astype(jnp.float32) for g in range(1, groups)], jnp.zeros_like(rank))
-    place = group * float(slots - row_cap) + dest.astype(jnp.float32) * float(row_cap) + rank
+    place = group * float(slots - row_cap) + block * float(row_cap) + rank
     put = onehot_rows(place, groups * slots)
     code_col = column(put, (face * elements + elem + 1).astype(jnp.float32))
     row_place, row_slot = row_places(crow, peers, elements, row_cap)
@@ -258,7 +266,7 @@
 
 
 def exchange(block):
-    return lax.all_to_all(block, ("gx", "gy"), split_axis=0, concat_axis=0, tiled=True)
+    return lax.all_to_all(block, ("gy", "gx"), split_axis=0, concat_axis=0, tiled=True)
 
 
 def from_behind(block, axis, distance):

time: 30.5 us -> 29.9 us (0.980)
  waiting for transfers between devices: 5.33 us -> 4.97 us
    all_to_all x1, waiting for transfers between devices: 4.12 us -> 3.76 us  [exchange(): lax.all_to_all(block, ('gy', 'gx'), split_axis=0, concat_axis=0, tiled=True)]
where the time goes in v9:
time: 29.9 us; the launch traced here: 29.7 us
  blocking collectives  9.85 us (33%)
  Pallas kernels  7.51 us (25%)
  starting transfers between devices  7.3 us (24%)
  waiting for transfers between devices  4.97 us (17%)
    all_to_all x1, blocking collectives, exchange(): lax.all_to_all(block, ('gy', 'gx'), split_axis=0, concat_axis=0, tiled=True)  9.85 us
    pallas_call x4, Pallas kernels, call(): pl.pallas_call(functools.partial(fetched, kernel, len(far), len(near), le...  7.51 us
    all_to_all x1, starting transfers between devices, exchange(): lax.all_to_all(block, ('gy', 'gx'), split_axis=0, concat_axis=0, tiled=True)  7.29 us
    all_to_all x1, waiting for transfers between devices, exchange(): lax.all_to_all(block, ('gy', 'gx'), split_axis=0, concat_axis=0, tiled=True)  3.76 us
    ppermute x1, waiting for transfers between devices, from_behind(): return lax.ppermute(block, axis, route)  1.2 us
  transfers between devices with their start and end apart: 2, of which 2 were waited for; matrix products, arithmetic and copies ran while one was open for 0% of the time, Pallas kernels for 8%

profile of v9, /device:TPU:0, one launch (start us, length us, event | category | flops | bytes accessed | tf_op | source)
XLA Modules:
  0.0 29.7 jit_solution(9398656789876196810)
XLA Ops:
  0.0 3.0 %shard_map.163 = (f32[8,4,1152]{2,1,0:T(4,128)}, f32[64,256]{1,0:T(8,128)S(1)}) custom-call(s32[1,96]{1,0:T(1,128)} %bitcast.10, s32[1,96]{1,0:T(1,128)} %bitcast.11, s32[1,96]{1,0:T(1,128)} %bitcast.12, s32[1,96]{1,0:T(1,128)} %bitcast.13, s32[1,32]{1,0:T(1,128)} %bitcast.8, s32[1,64]{1,0:T(1,128)} %bitcast.14, s32[1,64]{1,0:T(1,128)} %bitcast.15, ...), custom_call_target="tpu_custom_call" | custom-call | bytes 1293568 | tf_op jit(solution)/shard_map/pallas_call | solution.py:258
  3.0 7.3 %all-to-all-start = ((f32[8,4,1152]{2,1,0:T(4,128)}), f32[8,4,1152]{2,1,0:T(4,128)S(1)}, u32[]{:S(2)}, u32[]{:S(2)}) async-start(f32[8,4,1152]{2,1,0:T(4,128)} %get-tuple-element.11), calls=%async_computation | async-start | bytes 294912 | tf_op jit(solution)/shard_map/all_to_all | solution.py:269
  10.3 0.0 collective-permute-start
  10.3 2.5 %shard_map.164 = (f32[160,216]{1,0:T(8,128)S(1)}, f32[32,128]{1,0:T(8,128)S(1)}, bf16[1280,216]{1,0:T(8,128)(2,1)S(1)}, bf16[1280,216]{1,0:T(8,128)(2,1)S(1)}) custom-call(s32[1,32]{1,0:T(1,128)} %bitcast.16, s32[1,32]{1,0:T(1,128)} %bitcast.9, f32[32,1715]{1,0:T(8,128)} %refs_2_.1, bf16[1920,216]{1,0:T(8,128)(2,1)} %constant.14.clone.refs_3_, ...), custom_call_target="tpu_custom_call" | custom-call | bytes 4245120 | tf_op jit(solution)/shard_map/pallas_call | solution.py:258
  12.8 1.2 %collective-permute-done.refs_1_ = f32[64,256]{1,0:T(8,128)S(1)} collective-permute-done((f32[64,256]{1,0:T(8,128)S(1)}, f32[64,256]{1,0:T(8,128)S(1)}, u32[]{:S(2)}, u32[]{:S(2)}) %collective-permute-start) | collective-permute-done | bytes 65568 | tf_op jit(solution)/shard_map/ppermute | solution.py:275
  14.0 3.8 %all-to-all-done.refs_0_.refs_1_ = f32[8,4,1152]{2,1,0:T(4,128)S(1)} async-done(((f32[8,4,1152]{2,1,0:T(4,128)}), f32[8,4,1152]{2,1,0:T(4,128)S(1)}, u32[]{:S(2)}, u32[]{:S(2)}) %all-to-all-start) | async-done | bytes 147488 | tf_op jit(solution)/shard_map/all_to_all | solution.py:269
  17.7 1.1 %shard_map.165 = f32[8,4,1080]{2,1,0:T(4,128)S(1)} custom-call(f32[8,4,1152]{2,1,0:T(4,128)S(1)} %all-to-all-done.refs_0_.refs_1_, f32[64,256]{1,0:T(8,128)S(1)} %collective-permute-done.refs_1_, f32[160,216]{1,0:T(8,128)S(1)} %get-tuple-element.13.refs_2_, f32[32,128]{1,0:T(8,128)S(1)} %get-tuple-element.14.refs_3_, ...), custom_call_target="tpu_custom_call" | custom-call | bytes 1611776 | tf_op jit(solution)/shard_map/pallas_call | solution.py:258
  18.9 9.8 %all_to_all.10.refs_0_ = f32[8,4,1080]{2,1,0:T(4,128)S(1)} all-to-all(f32[8,4,1080]{2,1,0:T(4,128)S(1)} %shard_map.165), channel_id=1, replica_groups=mesh['gx'=2,'gy'=4,'gz'=4] {'gy','gx'}, dimensions={0} | all-to-all | bytes 276480 | tf_op jit(solution)/shard_map/all_to_all | solution.py:269
  28.7 0.9 %shard_map.166 = f32[32,1080]{1,0:T(8,128)} custom-call(f32[8,4,1080]{2,1,0:T(4,128)S(1)} %all_to_all.10.refs_0_, f32[8,4,1152]{2,1,0:T(4,128)S(1)} %all-to-all-done.refs_0_.refs_1_), custom_call_target="tpu_custom_call" | custom-call | bytes 423936 | tf_op jit(solution)/shard_map/pallas_call | solution.py:258
Async XLA Ops:
  3.0 14.7 %all-to-all-start = ((f32[8,4,1152]{2,1,0:T(4,128)}), f32[8,4,1152]{2,1,0:T(4,128)S(1)}, u32[]{:S(2)}, u32[]{:S(2)}) async-start(f32[8,4,1152]{2,1,0:T(4,128)} %get-tuple-element.11), calls=%async_computation | async-start | bytes 294912 | tf_op jit(solution)/shard_map/all_to_all | solution.py:269
  10.3 3.7 %collective-permute-start = (f32[64,256]{1,0:T(8,128)S(1)}, f32[64,256]{1,0:T(8,128)S(1)}, u32[]{:S(2)}, u32[]{:S(2)}) collective-permute-start(f32[64,256]{1,0:T(8,128)S(1)} %get-tuple-element.12), channel_id=1, source_target_pairs={{3,0},{0,1},{1,2},{2,3},{7,4},{4,5},{5,6},{6,7},{11,8},{8,9},{9,10... | collective-permute-start | bytes 196616 | tf_op jit(solution)/shard_map/ppermute | solution.py:275

commit v10 on v9

--- a/solution.py
+++ b/solution.py
@@ -20,6 +20,9 @@
 TRACE_PAD = 256
 FLAT = 36
 SENT = VARS * FLAT
+STEP = 192
+TAG_FACE = SENT
+TAG_ROW = SENT + 1
 CELL_PAD = 384
 FACE_PAD = 40
 FACES_PAD = 256
@@ -51,7 +54,7 @@
     top_nodes = grid_nodes(6)
     mortar = [lagrange_rows(6, (top_nodes - 1.0) / 2.0), lagrange_rows(6, (top_nodes + 1.0) / 2.0)]
     flat = lagrange_rows(5, top_nodes)
-    lift = np.zeros((5, TRACE_PAD, SENT))
+    lift = np.zeros((5, TRACE_PAD, STEP))
     for sub in range(5):
         both = (mortar[sub // 2] @ flat, mortar[sub % 2] @ flat) if sub < 4 else (flat, flat)
         for v in range(VARS):
@@ -70,7 +73,8 @@
                 first = (2 * axis + side) * FACE_PAD
                 face[index, first : first + FLAT] = np.einsum(spec, edge, lower, lower).reshape(FLAT, ROW)
     return (
-        split_table(lift.reshape(-1, SENT)),
+        split_table(lift[:4].reshape(-1, STEP)),
+        split_table(lift[4]),
         split_table(cell.reshape(-1, ROW)),
         split_table(face.reshape(-1, ROW)),
     )
@@ -133,9 +137,9 @@
     return jnp.concatenate([x, jnp.zeros((x.shape[0], lanes - x.shape[1]), x.dtype)], axis=1)
 
 
-def pack_kernel(peers, cap, row_cap, elements, get, out, conf_out):
-    dest, elem, face, sub, crow, cface, celem = [get(i) for i in range(7)]
-    count, confs = dest.shape[1], cface.shape[1]
+def pack_kernel(peers, cap, row_cap, elements, get, out, conf_out, message, sent):
+    dest, sub, elem, face, crow = [get(i) for i in range(5)]
+    count = dest.shape[1]
     groups, slots = -(-cap // row_cap), peers * row_cap
     member = (device_of((peers, count)) == dest).astype(jnp.float32)
     block = jnp.sum(member * iota(member.shape, 0).astype(jnp.float32), axis=0, keepdims=True)
@@ -148,27 +152,29 @@
     row_col = column(onehot_rows(row_place, slots), row_slot + 1.0)
     eye = (iota((count, count), 0) == iota((count, count), 1)).astype(jnp.float32)
     sub_col = column(eye, sub.astype(jnp.float32))
-    x = pad_lanes(get(7), TRACE_PAD)
+    x = pad_lanes(get(5), TRACE_PAD)
     wide = jnp.concatenate([jnp.where(sub_col == float(s), x, 0.0) for s in range(4)], axis=1)
-    table_high, table_low = get(9), get(10)
-    split = 4 * TRACE_PAD
-    lifted = dot3(*halves(wide), table_high[:split], table_low[:split])
-    lifted_high, lifted_low = halves(lifted)
+    lifted_high, lifted_low = halves(dot3(*halves(wide), get(6), get(7)))
     put = put.astype(jnp.bfloat16)
     packed = dot(put, lifted_high) + dot(put, lifted_low)
+    packed = jnp.where(iota(packed.shape, 1) == TAG_FACE, code_col, packed)
     for g in range(groups):
         part = packed[g * slots : (g + 1) * slots]
-        out[:, :, g * SENT : (g + 1) * SENT] = part.reshape(peers, row_cap, SENT)
-    tags = jnp.concatenate([*[code_col[g * slots : (g + 1) * slots] for g in range(groups)], row_col], axis=1)
-    out[:, :, groups * SENT : groups * (SENT + 1) + 1] = tags.reshape(peers, row_cap, groups + 1)
+        if g == 0:
+            part = jnp.where(iota(part.shape, 1) == TAG_ROW, row_col, part)
+        message[:, :, g * STEP : (g + 1) * STEP] = part.reshape(peers, row_cap, STEP)
+    send = pltpu.make_async_copy(message, out, sent.at[0])
+    send.start()
+    cface, celem = get(8), get(9)
+    confs = cface.shape[1]
     eye = (iota((confs, confs), 0) == iota((confs, confs), 1)).astype(jnp.float32)
     conf_col = column(eye, (cface * elements + celem + 1).astype(jnp.float32))
-    conf = dot3(*halves(pad_lanes(get(8), TRACE_PAD)), table_high[split:], table_low[split:])
-    conf_out[:, :SENT] = conf
-    conf_out[:, SENT : SENT + 1] = conf_col
-
-
-def cell_kernel(peers, row_cap, get, y_out, col_out, face_high, face_low, spread):
+    conf = dot3(*halves(pad_lanes(get(10), TRACE_PAD)), get(11), get(12))
+    conf_out[...] = jnp.where(iota(conf.shape, 1) == TAG_FACE, conf_col, conf)
+    send.wait()
+
+
+def cell_kernel(peers, row_cap, get, y_out, col_out, spread):
     order, crow = get(0), get(1)
     elements = order.shape[1]
     slots = peers * row_cap
@@ -189,18 +195,13 @@
     wide_high = jnp.concatenate([jnp.where(order_rows == float(p), high, 0.0).astype(jnp.bfloat16) for p in ORDERS], axis=1)
     wide_low = jnp.concatenate([jnp.where(order_rows == float(p), low, 0.0).astype(jnp.bfloat16) for p in ORDERS], axis=1)
     y_out[...] = dot3(wide_high, wide_low, get(3), get(4))
-    face_high[...] = get(5)
-    face_low[...] = get(6)
 
 
 def face_kernel(peers, row_cap, elements, groups, get, incoming, conf, y, cols, table_high, table_low, out, spread):
     slots = peers * row_cap
     message = incoming[...].reshape(slots, incoming.shape[2])
-    first_tag = groups * SENT
-    x = jnp.concatenate([*[message[:, g * SENT : (g + 1) * SENT] for g in range(groups)], conf[:, :SENT]], axis=0)
-    code_col = jnp.concatenate(
-        [*[message[:, first_tag + g : first_tag + g + 1] for g in range(groups)], conf[:, SENT : SENT + 1]], axis=0
-    )
+    x = jnp.concatenate([*[message[:, g * STEP : (g + 1) * STEP] for g in range(groups)], conf[...]], axis=0)
+    code_col = x[:, TAG_FACE : TAG_FACE + 1]
     count = x.shape[0]
     code_row = jnp.sum(jnp.where(iota((count, count), 0) == iota((count, count), 1), code_col, 0.0), axis=0, keepdims=True)
     order_col, elem_col = cols[:, 0:1], cols[:, 1:2]
@@ -223,11 +224,11 @@
         out[:, :, v * ROW : (v + 1) * ROW] = total[v * slots : (v + 1) * slots].reshape(peers, row_cap, ROW)
 
 
-def place_kernel(peers, row_cap, tag, get, arrived, message, out):
+def place_kernel(peers, row_cap, get, arrived, message, out):
     elements = out.shape[0]
     rows = peers * row_cap
     x = arrived[...].reshape(rows, arrived.shape[2])
-    slot_col = message[:, :, tag : tag + 1].reshape(rows, 1)
+    slot_col = message[:, :, TAG_ROW : TAG_ROW + 1].reshape(rows, 1)
     slot_row = jnp.sum(jnp.where(iota((rows, rows), 0) == iota((rows, rows), 1), slot_col, 0.0), axis=0, keepdims=True)
     put = (iota((elements, rows), 0).astype(jnp.float32) + 1.0 == slot_row).astype(jnp.bfloat16)
     high, low = halves(x)
@@ -235,10 +236,12 @@
     out[...] = dot(put, high) + dot(put, low) + dot(put, rest)
 
 
-def fetched(kernel, n_far, n_near, n_out, *refs):
+def fetched(kernel, n_far, n_pass, n_near, n_out, *refs):
     far, near, outs = refs[:n_far], refs[n_far : n_far + n_near], refs[n_far + n_near : n_far + n_near + n_out]
     rest = refs[n_far + n_near + n_out :]
-    held, sems, scratch = rest[:n_far], rest[n_far], rest[n_far + 1 :]
+    n_held = n_far - n_pass
+    held, sems, scratch = rest[:n_held], rest[n_held], rest[n_held + 1 :]
+    held = (*held, *outs[n_out - n_pass :])
     copies = [pltpu.make_async_copy(src, dst, sems.at[i]) for i, (src, dst) in enumerate(zip(far, held))]
     for copy in copies:
         copy.start()
@@ -247,19 +250,29 @@
         copies[i].wait()
         return held[i][...]
 
-    kernel(get, *near, *outs, *scratch)
-
-
-def call(kernel, outs, far, near=(), scratch=(), flops=0):
-    shapes = jax.tree.leaves(outs)
-    sizes = [np.prod(a.shape) * a.dtype.itemsize for a in (*far, *near, *shapes)]
+    kernel(get, *near, *outs[: n_out - n_pass], *scratch)
+    for copy in copies[n_held:]:
+        copy.wait()
+
+
+def like(a):
+    return jax.ShapeDtypeStruct(a.shape, a.dtype)
+
+
+def call(kernel, outs, far, near=(), scratch=(), hand_on=(), out_far=(), flops=0):
+    outs = [*outs, *[like(a) for a in hand_on]]
+    out_specs = [pl.BlockSpec(memory_space=pltpu.HBM if i in out_far else pltpu.VMEM) for i in range(len(outs))]
+    outs = [pltpu.HBM(a.shape, a.dtype) if i in out_far else a for i, a in enumerate(outs)]
+    sizes = [np.prod(a.shape) * a.dtype.itemsize for a in (*far, *near, *outs)]
+    held = [pltpu.VMEM(a.shape, a.dtype) for a in far]
+    far = (*far, *hand_on)
     in_specs = [pl.BlockSpec(memory_space=pltpu.HBM)] * len(far) + [pl.BlockSpec(memory_space=pltpu.VMEM)] * len(near)
-    scratch = [*[pltpu.VMEM(a.shape, a.dtype) for a in far], pltpu.SemaphoreType.DMA((max(1, len(far)),)), *scratch]
     return pl.pallas_call(
-        functools.partial(fetched, kernel, len(far), len(near), len(shapes)),
+        functools.partial(fetched, kernel, len(far), len(hand_on), len(near), len(outs)),
         in_specs=in_specs,
+        out_specs=out_specs,
         out_shape=outs,
-        scratch_shapes=scratch,
+        scratch_shapes=[*held, pltpu.SemaphoreType.DMA((max(1, len(far)),)), *scratch],
         compiler_params=pltpu.CompilerParams(vmem_limit_bytes=48 * 1024 * 1024),
         cost_estimate=pl.CostEstimate(flops=flops, bytes_accessed=int(sum(sizes)), transcendentals=0),
     )(*[pltpu.with_memory_space_constraint(a, pltpu.HBM) for a in far], *near)
@@ -296,53 +309,53 @@
     row_cap = max(2, elements // peers)
     slots = peers * row_cap
     groups = -(-cap // row_cap)
-    lanes = -(-(groups * (SENT + 1) + 1) // 128) * 128
-    lift, cell, face = [tuple(jnp.asarray(t) for t in pair) for pair in basis_tables()]
+    lanes = groups * STEP
+    lift, conf_lift, cell, face = [tuple(jnp.asarray(t) for t in pair) for pair in basis_tables()]
     f32 = jnp.float32
     line = lambda a: a.reshape(1, -1)
     order, coarse_row = line(order), line(coarse_row)
     outgoing, conf = call(
         functools.partial(pack_kernel, peers, cap, row_cap, elements),
-        (jax.ShapeDtypeStruct((peers, row_cap, lanes), f32), jax.ShapeDtypeStruct((confs, TRACE_PAD), f32)),
+        [jax.ShapeDtypeStruct((peers, row_cap, lanes), f32), jax.ShapeDtypeStruct((confs, STEP), f32)],
         (
             line(mortar_dest),
+            line(mortar_sub),
             line(mortar_elem),
             line(mortar_face),
-            line(mortar_sub),
             coarse_row,
+            mortar_trace,
+            *lift,
             line(conf_face),
             line(conf_elem),
-            mortar_trace,
             conf_trace,
-            *lift,
+            *conf_lift,
         ),
+        scratch=[pltpu.VMEM((peers, row_cap, lanes), f32), pltpu.SemaphoreType.DMA((1,))],
+        out_far=(0,),
     )
     incoming = exchange(outgoing)
     conf = from_behind(conf, "gz", 1)
     y, cols, *face = call(
         functools.partial(cell_kernel, peers, row_cap),
-        (
-            jax.ShapeDtypeStruct((VARS * slots, ROW), f32),
-            jax.ShapeDtypeStruct((slots, 128), f32),
-            *[jax.ShapeDtypeStruct(t.shape, t.dtype) for t in face],
-        ),
-        (order, coarse_row, adjoint, *cell, *face),
+        [jax.ShapeDtypeStruct((VARS * slots, ROW), f32), jax.ShapeDtypeStruct((slots, 128), f32)],
+        (order, coarse_row, adjoint, *cell),
         scratch=[pltpu.VMEM((2, VARS * slots, CELL_PAD), f32)],
-    )
-    rows = call(
+        hand_on=face,
+    )
+    (rows,) = call(
         functools.partial(face_kernel, peers, row_cap, elements, groups),
-        jax.ShapeDtypeStruct((peers, row_cap, VARS * ROW), f32),
+        [jax.ShapeDtypeStruct((peers, row_cap, VARS * ROW), f32)],
         (),
         (incoming, conf, y, cols, *face),
         scratch=[pltpu.VMEM((VARS * slots, FACES_PAD), f32)],
     )
-    arrived = exchange(rows)
-    return call(
-        functools.partial(place_kernel, peers, row_cap, groups * (SENT + 1)),
-        jax.ShapeDtypeStruct((elements, VARS * ROW), f32),
+    (out,) = call(
+        functools.partial(place_kernel, peers, row_cap),
+        [jax.ShapeDtypeStruct((elements, VARS * ROW), f32)],
         (),
-        (arrived, incoming),
-    )
+        (exchange(rows), incoming),
+    )
+    return out
 
 
 def solution(mesh):

time: 29.9 us -> 29.8 us (level)
  no operation moved by 1% of the time
where the time goes in v10:
time: 29.8 us; the launch traced here: 29.5 us
  blocking collectives  9.85 us (33%)
  starting transfers between devices  7.3 us (24%)
  Pallas kernels  7.28 us (24%)
  waiting for transfers between devices  5.05 us (17%)
    all_to_all x1, blocking collectives, exchange(): lax.all_to_all(block, ('gy', 'gx'), split_axis=0, concat_axis=0, tiled=True)  9.85 us
    all_to_all x1, starting transfers between devices, exchange(): lax.all_to_all(block, ('gy', 'gx'), split_axis=0, concat_axis=0, tiled=True)  7.29 us
    pallas_call x4, Pallas kernels, call(): pl.pallas_call(functools.partial(fetched, kernel, len(far), len(hand_on),...  7.28 us
    all_to_all x1, waiting for transfers between devices, exchange(): lax.all_to_all(block, ('gy', 'gx'), split_axis=0, concat_axis=0, tiled=True)  3.76 us
    ppermute x1, waiting for transfers between devices, from_behind(): return lax.ppermute(block, axis, route)  1.29 us
  transfers between devices with their start and end apart: 2, of which 2 were waited for; matrix products, arithmetic and copies ran while one was open for 0% of the time, Pallas kernels for 8%

profile of v10, /device:TPU:0, one launch (start us, length us, event | category | flops | bytes accessed | tf_op | source)
XLA Modules:
  0.0 29.5 jit_solution(14576433762464138342)
XLA Ops:
  0.0 2.9 %shard_map.181 = (f32[8,4,1152]{2,1,0:T(4,128)}, f32[64,192]{1,0:T(8,128)S(1)}) custom-call(s32[1,96]{1,0:T(1,128)} %bitcast.10, s32[1,96]{1,0:T(1,128)} %bitcast.11, s32[1,96]{1,0:T(1,128)} %bitcast.12, s32[1,96]{1,0:T(1,128)} %bitcast.13, s32[1,32]{1,0:T(1,128)} %bitcast.8, f32[96,245]{1,0:T(8,128)} %refs_5_.2, bf16[1024,192]{1,0:T(8,128)(2,1)} %constant.16.clone.refs_6_, ...), custom_call_target="tpu_custom_call" | custom-call | bytes 1338624 | tf_op jit(solution)/shard_map/pallas_call | solution.py:270
  2.9 7.3 %all-to-all-start = ((f32[8,4,1152]{2,1,0:T(4,128)}), f32[8,4,1152]{2,1,0:T(4,128)S(1)}, u32[]{:S(2)}, u32[]{:S(2)}) async-start(f32[8,4,1152]{2,1,0:T(4,128)} %get-tuple-element.11), calls=%async_computation | async-start | bytes 294912 | tf_op jit(solution)/shard_map/all_to_all | solution.py:282
  10.2 0.0 collective-permute-start
  10.2 2.4 %shard_map.182 = (f32[160,216]{1,0:T(8,128)S(1)}, f32[32,128]{1,0:T(8,128)S(1)}, bf16[1280,216]{1,0:T(8,128)(2,1)S(1)}, bf16[1280,216]{1,0:T(8,128)(2,1)S(1)}) custom-call(s32[1,32]{1,0:T(1,128)} %bitcast.16, s32[1,32]{1,0:T(1,128)} %bitcast.9, f32[32,1715]{1,0:T(8,128)} %refs_2_.1, bf16[1920,216]{1,0:T(8,128)(2,1)} %constant.20.clone.refs_3_, ...), custom_call_target="tpu_custom_call" | custom-call | bytes 3139200 | tf_op jit(solution)/shard_map/pallas_call | solution.py:270
  12.6 1.3 %collective-permute-done.refs_1_ = f32[64,192]{1,0:T(8,128)S(1)} collective-permute-done((f32[64,192]{1,0:T(8,128)S(1)}, f32[64,192]{1,0:T(8,128)S(1)}, u32[]{:S(2)}, u32[]{:S(2)}) %collective-permute-start) | collective-permute-done | bytes 49184 | tf_op jit(solution)/shard_map/ppermute | solution.py:288
  13.9 3.8 %all-to-all-done.refs_0_.refs_1_ = f32[8,4,1152]{2,1,0:T(4,128)S(1)} async-done(((f32[8,4,1152]{2,1,0:T(4,128)}), f32[8,4,1152]{2,1,0:T(4,128)S(1)}, u32[]{:S(2)}, u32[]{:S(2)}) %all-to-all-start) | async-done | bytes 147488 | tf_op jit(solution)/shard_map/all_to_all | solution.py:282
  17.6 1.1 %shard_map.183 = f32[8,4,1080]{2,1,0:T(4,128)S(1)} custom-call(f32[8,4,1152]{2,1,0:T(4,128)S(1)} %all-to-all-done.refs_0_.refs_1_, f32[64,192]{1,0:T(8,128)S(1)} %collective-permute-done.refs_1_, f32[160,216]{1,0:T(8,128)S(1)} %get-tuple-element.13.refs_2_, f32[32,128]{1,0:T(8,128)S(1)} %get-tuple-element.14.refs_3_, ...), custom_call_target="tpu_custom_call" | custom-call | bytes 1595392 | tf_op jit(solution)/shard_map/pallas_call | solution.py:270
  18.7 9.9 %all_to_all.10.refs_0_ = f32[8,4,1080]{2,1,0:T(4,128)S(1)} all-to-all(f32[8,4,1080]{2,1,0:T(4,128)S(1)} %shard_map.183), channel_id=1, replica_groups=mesh['gx'=2,'gy'=4,'gz'=4] {'gy','gx'}, dimensions={0} | all-to-all | bytes 276480 | tf_op jit(solution)/shard_map/all_to_all | solution.py:282
  28.6 0.9 %shard_map.184 = f32[32,1080]{1,0:T(8,128)} custom-call(f32[8,4,1080]{2,1,0:T(4,128)S(1)} %all_to_all.10.refs_0_, f32[8,4,1152]{2,1,0:T(4,128)S(1)} %all-to-all-done.refs_0_.refs_1_), custom_call_target="tpu_custom_call" | custom-call | bytes 423936 | tf_op jit(solution)/shard_map/pallas_call | solution.py:270
Async XLA Ops:
  2.9 14.7 %all-to-all-start = ((f32[8,4,1152]{2,1,0:T(4,128)}), f32[8,4,1152]{2,1,0:T(4,128)S(1)}, u32[]{:S(2)}, u32[]{:S(2)}) async-start(f32[8,4,1152]{2,1,0:T(4,128)} %get-tuple-element.11), calls=%async_computation | async-start | bytes 294912 | tf_op jit(solution)/shard_map/all_to_all | solution.py:282
  10.2 3.7 %collective-permute-start = (f32[64,192]{1,0:T(8,128)S(1)}, f32[64,192]{1,0:T(8,128)S(1)}, u32[]{:S(2)}, u32[]{:S(2)}) collective-permute-start(f32[64,192]{1,0:T(8,128)S(1)} %get-tuple-element.12), channel_id=1, source_target_pairs={{3,0},{0,1},{1,2},{2,3},{7,4},{4,5},{5,6},{6,7},{11,8},{8,9},{9,10... | collective-permute-start | bytes 147464 | tf_op jit(solution)/shard_map/ppermute | solution.py:288

commit v11 on v10

--- a/solution.py
+++ b/solution.py
@@ -22,7 +22,8 @@
 SENT = VARS * FLAT
 STEP = 192
 TAG_FACE = SENT
-TAG_ROW = SENT + 1
+ROWS_PAD = 1152
+TAG_SLOT = VARS * ROW
 CELL_PAD = 384
 FACE_PAD = 40
 FACES_PAD = 256
@@ -110,6 +111,18 @@
     return rank % size_x * size_y + rank // size_x
 
 
+def pairwise():
+    size_y = lax.axis_size("gy")
+    return lax.axis_size("gx") == 2 and size_y <= 4 and size_y & (size_y - 1) == 0
+
+
+def trace_device_of(shape):
+    if not pairwise():
+        return device_of(shape)
+    size_y = lax.axis_size("gy")
+    return iota(shape, 0) ^ (lax.axis_index("gx") * size_y + lax.axis_index("gy"))
+
+
 def owner_of(crow, peers, elements):
     first = device_of((peers, crow.shape[1])) * elements
     return ((crow >= first) & (crow < first + elements)).astype(jnp.float32)
@@ -137,53 +150,53 @@
     return jnp.concatenate([x, jnp.zeros((x.shape[0], lanes - x.shape[1]), x.dtype)], axis=1)
 
 
-def pack_kernel(peers, cap, row_cap, elements, get, out, conf_out, message, sent):
-    dest, sub, elem, face, crow = [get(i) for i in range(5)]
+def pack_kernel(peers, cap, row_cap, elements, get, conf_out, *outs):
+    dest, sub, elem, face = [get(i) for i in range(4)]
     count = dest.shape[1]
     groups, slots = -(-cap // row_cap), peers * row_cap
-    member = (device_of((peers, count)) == dest).astype(jnp.float32)
+    member = (trace_device_of((peers, count)) == dest).astype(jnp.float32)
     block = jnp.sum(member * iota(member.shape, 0).astype(jnp.float32), axis=0, keepdims=True)
     rank = jnp.sum(member * earlier(member), axis=0, keepdims=True)
     group = sum([(rank >= float(g * row_cap)).astype(jnp.float32) for g in range(1, groups)], jnp.zeros_like(rank))
     place = group * float(slots - row_cap) + block * float(row_cap) + rank
     put = onehot_rows(place, groups * slots)
     code_col = column(put, (face * elements + elem + 1).astype(jnp.float32))
-    row_place, row_slot = row_places(crow, peers, elements, row_cap)
-    row_col = column(onehot_rows(row_place, slots), row_slot + 1.0)
     eye = (iota((count, count), 0) == iota((count, count), 1)).astype(jnp.float32)
     sub_col = column(eye, sub.astype(jnp.float32))
-    x = pad_lanes(get(5), TRACE_PAD)
+    x = pad_lanes(get(4), TRACE_PAD)
     wide = jnp.concatenate([jnp.where(sub_col == float(s), x, 0.0) for s in range(4)], axis=1)
-    lifted_high, lifted_low = halves(dot3(*halves(wide), get(6), get(7)))
+    lifted_high, lifted_low = halves(dot3(*halves(wide), get(5), get(6)))
     put = put.astype(jnp.bfloat16)
     packed = dot(put, lifted_high) + dot(put, lifted_low)
     packed = jnp.where(iota(packed.shape, 1) == TAG_FACE, code_col, packed)
     for g in range(groups):
-        part = packed[g * slots : (g + 1) * slots]
-        if g == 0:
-            part = jnp.where(iota(part.shape, 1) == TAG_ROW, row_col, part)
-        message[:, :, g * STEP : (g + 1) * STEP] = part.reshape(peers, row_cap, STEP)
-    send = pltpu.make_async_copy(message, out, sent.at[0])
-    send.start()
-    cface, celem = get(8), get(9)
+        for out, part in zip(outs, jnp.split(packed[g * slots : (g + 1) * slots], len(outs))):
+            out[:, :, g * STEP : (g + 1) * STEP] = part.reshape(-1, row_cap, STEP)
+    cface, celem = get(7), get(8)
     confs = cface.shape[1]
     eye = (iota((confs, confs), 0) == iota((confs, confs), 1)).astype(jnp.float32)
     conf_col = column(eye, (cface * elements + celem + 1).astype(jnp.float32))
-    conf = dot3(*halves(pad_lanes(get(10), TRACE_PAD)), get(11), get(12))
+    conf = dot3(*halves(pad_lanes(get(9), TRACE_PAD)), get(10), get(11))
     conf_out[...] = jnp.where(iota(conf.shape, 1) == TAG_FACE, conf_col, conf)
-    send.wait()
+
+
+def pair_kernel(get, near, far, *outs):
+    for k, out in enumerate(outs):
+        out[0] = near[k]
+        out[1] = far[k]
 
 
 def cell_kernel(peers, row_cap, get, y_out, col_out, spread):
     order, crow = get(0), get(1)
     elements = order.shape[1]
     slots = peers * row_cap
-    place, _ = row_places(crow, peers, elements, row_cap)
+    place, slot = row_places(crow, peers, elements, row_cap)
     take = onehot_rows(place, slots)
     order_col = column(take, order.astype(jnp.float32))
     elem_col = column(take, iota((1, elements), 1).astype(jnp.float32) + 1.0)
     lane = iota((slots, 128), 1)
-    col_out[...] = jnp.where(lane == 0, order_col, jnp.where(lane == 1, elem_col, 0.0))
+    slot_col = column(take, slot + 1.0)
+    col_out[...] = jnp.where(lane == 0, order_col, jnp.where(lane == 1, elem_col, slot_col))
     take = take.astype(jnp.bfloat16)
     spread[...] = jnp.zeros_like(spread)
     for half, part in enumerate(halves(get(2))):
@@ -197,9 +210,10 @@
     y_out[...] = dot3(wide_high, wide_low, get(3), get(4))
 
 
-def face_kernel(peers, row_cap, elements, groups, get, incoming, conf, y, cols, table_high, table_low, out, spread):
+def face_kernel(peers, row_cap, elements, groups, blocks, get, *refs):
+    incoming, (conf, y, cols, table_high, table_low, out, spread) = refs[:blocks], refs[blocks:]
     slots = peers * row_cap
-    message = incoming[...].reshape(slots, incoming.shape[2])
+    message = jnp.concatenate([ref[...].reshape(-1, ref.shape[2]) for ref in incoming], axis=0)
     x = jnp.concatenate([*[message[:, g * STEP : (g + 1) * STEP] for g in range(groups)], conf[...]], axis=0)
     code_col = x[:, TAG_FACE : TAG_FACE + 1]
     count = x.shape[0]
@@ -222,13 +236,14 @@
     total = y[...] + dot3(high, low, table_high[...], table_low[...])
     for v in range(VARS):
         out[:, :, v * ROW : (v + 1) * ROW] = total[v * slots : (v + 1) * slots].reshape(peers, row_cap, ROW)
-
-
-def place_kernel(peers, row_cap, get, arrived, message, out):
+    out[:, :, TAG_SLOT : TAG_SLOT + 1] = cols[:, 2:3].reshape(peers, row_cap, 1)
+
+
+def place_kernel(peers, row_cap, get, arrived, out):
     elements = out.shape[0]
     rows = peers * row_cap
-    x = arrived[...].reshape(rows, arrived.shape[2])
-    slot_col = message[:, :, TAG_ROW : TAG_ROW + 1].reshape(rows, 1)
+    message = arrived[...].reshape(rows, arrived.shape[2])
+    x, slot_col = message[:, :TAG_SLOT], message[:, TAG_SLOT : TAG_SLOT + 1]
     slot_row = jnp.sum(jnp.where(iota((rows, rows), 0) == iota((rows, rows), 1), slot_col, 0.0), axis=0, keepdims=True)
     put = (iota((elements, rows), 0).astype(jnp.float32) + 1.0 == slot_row).astype(jnp.bfloat16)
     high, low = halves(x)
@@ -259,10 +274,8 @@
     return jax.ShapeDtypeStruct(a.shape, a.dtype)
 
 
-def call(kernel, outs, far, near=(), scratch=(), hand_on=(), out_far=(), flops=0):
+def call(kernel, outs, far, near=(), scratch=(), hand_on=(), flops=0):
     outs = [*outs, *[like(a) for a in hand_on]]
-    out_specs = [pl.BlockSpec(memory_space=pltpu.HBM if i in out_far else pltpu.VMEM) for i in range(len(outs))]
-    outs = [pltpu.HBM(a.shape, a.dtype) if i in out_far else a for i, a in enumerate(outs)]
     sizes = [np.prod(a.shape) * a.dtype.itemsize for a in (*far, *near, *outs)]
     held = [pltpu.VMEM(a.shape, a.dtype) for a in far]
     far = (*far, *hand_on)
@@ -270,7 +283,6 @@
     return pl.pallas_call(
         functools.partial(fetched, kernel, len(far), len(hand_on), len(near), len(outs)),
         in_specs=in_specs,
-        out_specs=out_specs,
         out_shape=outs,
         scratch_shapes=[*held, pltpu.SemaphoreType.DMA((max(1, len(far)),)), *scratch],
         compiler_params=pltpu.CompilerParams(vmem_limit_bytes=48 * 1024 * 1024),
@@ -280,6 +292,18 @@
 
 def exchange(block):
     return lax.all_to_all(block, ("gy", "gx"), split_axis=0, concat_axis=0, tiled=True)
+
+
+def exchange_traces(blocks):
+    if len(blocks) == 1:
+        return [exchange(blocks[0])]
+    near, far = blocks
+    far = lax.ppermute(far, "gx", [(0, 1), (1, 0)])
+    size_y = near.shape[0]
+    pair = jax.ShapeDtypeStruct((2, *near.shape[1:]), near.dtype)
+    own, *others = call(pair_kernel, [pair] * size_y, (), (near, far))
+    hops = [[(i, i ^ k) for i in range(size_y)] for k in range(1, size_y)]
+    return [own, *[lax.ppermute(other, "gy", hop) for other, hop in zip(others, hops)]]
 
 
 def from_behind(block, axis, distance):
@@ -314,15 +338,18 @@
     f32 = jnp.float32
     line = lambda a: a.reshape(1, -1)
     order, coarse_row = line(order), line(coarse_row)
-    outgoing, conf = call(
+    blocks = 2 if pairwise() else 1
+    conf, *outgoing = call(
         functools.partial(pack_kernel, peers, cap, row_cap, elements),
-        [jax.ShapeDtypeStruct((peers, row_cap, lanes), f32), jax.ShapeDtypeStruct((confs, STEP), f32)],
+        [
+            jax.ShapeDtypeStruct((confs, STEP), f32),
+            *[jax.ShapeDtypeStruct((peers // blocks, row_cap, lanes), f32)] * blocks,
+        ],
         (
             line(mortar_dest),
             line(mortar_sub),
             line(mortar_elem),
             line(mortar_face),
-            coarse_row,
             mortar_trace,
             *lift,
             line(conf_face),
@@ -330,10 +357,8 @@
             conf_trace,
             *conf_lift,
         ),
-        scratch=[pltpu.VMEM((peers, row_cap, lanes), f32), pltpu.SemaphoreType.DMA((1,))],
-        out_far=(0,),
-    )
-    incoming = exchange(outgoing)
+    )
+    incoming = exchange_traces(outgoing)
     conf = from_behind(conf, "gz", 1)
     y, cols, *face = call(
         functools.partial(cell_kernel, peers, row_cap),
@@ -343,17 +368,17 @@
         hand_on=face,
     )
     (rows,) = call(
-        functools.partial(face_kernel, peers, row_cap, elements, groups),
-        [jax.ShapeDtypeStruct((peers, row_cap, VARS * ROW), f32)],
+        functools.partial(face_kernel, peers, row_cap, elements, groups, len(incoming)),
+        [jax.ShapeDtypeStruct((peers, row_cap, ROWS_PAD), f32)],
         (),
-        (incoming, conf, y, cols, *face),
+        (*incoming, conf, y, cols, *face),
         scratch=[pltpu.VMEM((VARS * slots, FACES_PAD), f32)],
     )
     (out,) = call(
         functools.partial(place_kernel, peers, row_cap),
         [jax.ShapeDtypeStruct((elements, VARS * ROW), f32)],
         (),
-        (exchange(rows), incoming),
+        (exchange(rows),),
     )
     return out
 

time: 29.8 us -> 30.7 us (1.030)
  waiting for transfers between devices: 5.05 us -> 5.68 us
  starting transfers between devices: 7.3 us -> 7.77 us
  Pallas kernels: 7.28 us -> 6.96 us
    ppermute x0 -> x4, starting transfers between devices: none -> 7.77 us  [the longest x3 4.73 us: exchange_traces(): lax.ppermute(other, 'gy', hop)]
    all_to_all x1 -> x0, starting transfers between devices: 7.29 us -> none  [exchange(): lax.all_to_all(block, ('gy', 'gx'), split_axis=0, concat_axis=0, tiled=True)]
    ppermute x0 -> x4, waiting for transfers between devices: none -> 5.68 us  [the longest x3 3.35 us: exchange_traces(): lax.ppermute(other, 'gy', hop)]
    all_to_all x1 -> x0, waiting for transfers between devices: 3.76 us -> none  [exchange(): lax.all_to_all(block, ('gy', 'gx'), split_axis=0, concat_axis=0, tiled=True)]
    ppermute x1, waiting for transfers between devices: 1.29 us -> 0.01 us  [from_behind(): return lax.ppermute(block, axis, route)]
    pallas_call x4 -> x5, Pallas kernels: 7.28 us -> 6.96 us  [call(): pl.pallas_call(functools.partial(fetched, kernel, len(far), len(hand_on),...]
  transfers between devices with their start and end apart: 2 -> 5, of which waited for: 2 -> 3; matrix products, arithmetic and copies ran while one was open for 0% -> 0% of each run, Pallas kernels for 8% -> 8%
where the time goes in v11:
time: 30.7 us; the launch traced here: 30.5 us
  blocking collectives  10 us (33%)
  starting transfers between devices  7.77 us (25%)
  Pallas kernels  6.96 us (23%)
  waiting for transfers between devices  5.68 us (19%)
    all_to_all x1, blocking collectives, exchange(): lax.all_to_all(block, ('gy', 'gx'), split_axis=0, concat_axis=0, tiled=True)  10 us
    pallas_call x5, Pallas kernels, call(): pl.pallas_call(functools.partial(fetched, kernel, len(far), len(hand_on),...  6.96 us
    ppermute x3, starting transfers between devices, exchange_traces(): lax.ppermute(other, 'gy', hop)  4.73 us
    ppermute x3, waiting for transfers between devices, exchange_traces(): lax.ppermute(other, 'gy', hop)  3.35 us
    ppermute x1, starting transfers between devices, exchange_traces(): far = lax.ppermute(far, 'gx', [(0, 1), (1, 0)])  3.03 us
    ppermute x1, waiting for transfers between devices, exchange_traces(): far = lax.ppermute(far, 'gx', [(0, 1), (1, 0)])  2.33 us
  transfers between devices with their start and end apart: 5, of which 3 were waited for; matrix products, arithmetic and copies ran while one was open for 0% of the time, Pallas kernels for 8%

profile of v11, /device:TPU:0, one launch (start us, length us, event | category | flops | bytes accessed | tf_op | source)
XLA Modules:
  0.0 30.5 jit_solution(8636100958164839300)
XLA Ops:
  0.0 2.5 %shard_map.181 = (f32[64,192]{1,0:T(8,128)S(1)}, f32[4,4,1152]{2,1,0:T(4,128)S(1)}, f32[4,4,1152]{2,1,0:T(4,128)S(1)}) custom-call(s32[1,96]{1,0:T(1,128)} %bitcast.8, s32[1,96]{1,0:T(1,128)} %bitcast.9, s32[1,96]{1,0:T(1,128)} %bitcast.10, s32[1,96]{1,0:T(1,128)} %bitcast.11, f32[96,245]{1,0:T(8,128)} %refs_4_.2, bf16[1024,192]{1,0:T(8,128)(2,1)} %constant.16.clone.refs_5_, ...), custom_call_target="tpu_custom_call" | custom-call | bytes 1338496 | tf_op jit(solution)/shard_map/pallas_call | solution.py:283
  2.5 3.0 %collective-permute-start = (f32[4,4,1152]{2,1,0:T(4,128)S(1)}, f32[4,4,1152]{2,1,0:T(4,128)S(1)}, u32[]{:S(2)}, u32[]{:S(2)}) collective-permute-start(f32[4,4,1152]{2,1,0:T(4,128)S(1)} %get-tuple-element.17), channel_id=1, source_target_pairs={{0,16},{16,0},{1,17},{17,1},{2,18},{18,2},{3,19},{19,3},{4,20},{20... | collective-permute-start | bytes 221192 | tf_op jit(solution)/shard_map/ppermute | solution.py:301
  5.6 0.0 collective-permute-start.4
  5.6 2.3 %collective-permute-done.refs_1_ = f32[4,4,1152]{2,1,0:T(4,128)S(1)} collective-permute-done((f32[4,4,1152]{2,1,0:T(4,128)S(1)}, f32[4,4,1152]{2,1,0:T(4,128)S(1)}, u32[]{:S(2)}, u32[]{:S(2)}) %collective-permute-start) | collective-permute-done | bytes 73760 | tf_op jit(solution)/shard_map/ppermute | solution.py:301
  7.9 2.1 %collective-permute-start.1 = (f32[2,4,1152]{2,1,0:T(4,128)S(1)}, f32[2,4,1152]{2,1,0:T(4,128)S(1)}, u32[]{:S(2)}, u32[]{:S(2)}) collective-permute-start(f32[2,4,1152]{2,1,0:T(4,128)S(1)} %get-tuple-element.19), channel_id=1, source_target_pairs={{0,4},{4,0},{8,12},{12,8},{1,5},{5,1},{9,13},{13,9},{2,6},{6,2},{1... | collective-permute-start | bytes 110600 | tf_op jit(solution)/shard_map/ppermute | solution.py:306
  10.1 2.6 %collective-permute-start.2 = (f32[2,4,1152]{2,1,0:T(4,128)S(1)}, f32[2,4,1152]{2,1,0:T(4,128)S(1)}, u32[]{:S(2)}, u32[]{:S(2)}) collective-permute-start(f32[2,4,1152]{2,1,0:T(4,128)S(1)} %get-tuple-element.20), channel_id=1, source_target_pairs={{0,8},{4,12},{8,0},{12,4},{1,9},{5,13},{9,1},{13,5},{2,10},{6,14},... | collective-permute-start | bytes 110600 | tf_op jit(solution)/shard_map/ppermute | solution.py:306
  12.7 0.0 collective-permute-start.3
  12.7 2.4 %shard_map.183 = (f32[160,216]{1,0:T(8,128)S(1)}, f32[32,128]{1,0:T(8,128)S(1)}, bf16[1280,216]{1,0:T(8,128)(2,1)S(1)}, bf16[1280,216]{1,0:T(8,128)(2,1)S(1)}) custom-call(s32[1,32]{1,0:T(1,128)} %bitcast.14, s32[1,32]{1,0:T(1,128)} %bitcast.15, f32[32,1715]{1,0:T(8,128)} %refs_2_.1, bf16[1920,216]{1,0:T(8,128)(2,1)} %constant.20.clone.refs_3_, ...), custom_call_target="tpu_custom_call" | custom-call | bytes 3139200 | tf_op jit(solution)/shard_map/pallas_call | solution.py:283
  15.0 0.0 collective-permute-done.4.refs_4_
  15.1 0.0 collective-permute-done.1.refs_1_
  15.1 0.2 collective-permute-done.2.refs_2_
  15.3 3.1 %collective-permute-done.3.refs_3_ = f32[2,4,1152]{2,1,0:T(4,128)S(1)} collective-permute-done((f32[2,4,1152]{2,1,0:T(4,128)S(1)}, f32[2,4,1152]{2,1,0:T(4,128)S(1)}, u32[]{:S(2)}, u32[]{:S(2)}) %collective-permute-start.3) | collective-permute-done | bytes 36896 | tf_op jit(solution)/shard_map/ppermute | solution.py:306
  18.4 1.1 %shard_map.184 = f32[8,4,1152]{2,1,0:T(4,128)S(1)} custom-call(f32[2,4,1152]{2,1,0:T(4,128)S(1)} %get-tuple-element.18.refs_0_, f32[2,4,1152]{2,1,0:T(4,128)S(1)} %collective-permute-done.1.refs_1_, f32[2,4,1152]{2,1,0:T(4,128)S(1)} %collective-permute-done.2.refs_2_, f32[2,4,1152]{2,1,0:T(4,128)S(1)} %collective-permute-done.3.refs_3_, ...), custom_call_target="tpu_custom_call" | custom-call | bytes 1604608 | tf_op jit(solution)/shard_map/pallas_call | solution.py:283
  19.5 10.0 %all_to_all.5.refs_0_ = f32[8,4,1152]{2,1,0:T(4,128)S(1)} all-to-all(f32[8,4,1152]{2,1,0:T(4,128)S(1)} %shard_map.184), channel_id=1, replica_groups=mesh['gx'=2,'gy'=4,'gz'=4] {'gy','gx'}, dimensions={0} | all-to-all | bytes 294912 | tf_op jit(solution)/shard_map/all_to_all | solution.py:294
  29.6 0.9 %shard_map.185 = f32[32,1080]{1,0:T(8,128)} custom-call(f32[8,4,1152]{2,1,0:T(4,128)S(1)} %all_to_all.5.refs_0_), custom_call_target="tpu_custom_call" | custom-call | bytes 285696 | tf_op jit(solution)/shard_map/pallas_call | solution.py:283
  (1 shorter events, 0.0 us)
Async XLA Ops:
  2.5 5.4 %collective-permute-start = (f32[4,4,1152]{2,1,0:T(4,128)S(1)}, f32[4,4,1152]{2,1,0:T(4,128)S(1)}, u32[]{:S(2)}, u32[]{:S(2)}) collective-permute-start(f32[4,4,1152]{2,1,0:T(4,128)S(1)} %get-tuple-element.17), channel_id=1, source_target_pairs={{0,16},{16,0},{1,17},{17,1},{2,18},{18,2},{3,19},{19,3},{4,20},{20... | collective-permute-start | bytes 221192 | tf_op jit(solution)/shard_map/ppermute | solution.py:301
  5.6 9.5 %collective-permute-start.4 = (f32[64,192]{1,0:T(8,128)S(1)}, f32[64,192]{1,0:T(8,128)S(1)}, u32[]{:S(2)}, u32[]{:S(2)}) collective-permute-start(f32[64,192]{1,0:T(8,128)S(1)} %get-tuple-element.22), channel_id=1, source_target_pairs={{3,0},{0,1},{1,2},{2,3},{7,4},{4,5},{5,6},{6,7},{11,8},{8,9},{9,10... | collective-permute-start | bytes 147464 | tf_op jit(solution)/shard_map/ppermute | solution.py:312
  7.9 7.1 %collective-permute-start.1 = (f32[2,4,1152]{2,1,0:T(4,128)S(1)}, f32[2,4,1152]{2,1,0:T(4,128)S(1)}, u32[]{:S(2)}, u32[]{:S(2)}) collective-permute-start(f32[2,4,1152]{2,1,0:T(4,128)S(1)} %get-tuple-element.19), channel_id=1, source_target_pairs={{0,4},{4,0},{8,12},{12,8},{1,5},{5,1},{9,13},{13,9},{2,6},{6,2},{1... | collective-permute-start | bytes 110600 | tf_op jit(solution)/shard_map/ppermute | solution.py:306
  10.1 5.2 %collective-permute-start.2 = (f32[2,4,1152]{2,1,0:T(4,128)S(1)}, f32[2,4,1152]{2,1,0:T(4,128)S(1)}, u32[]{:S(2)}, u32[]{:S(2)}) collective-permute-start(f32[2,4,1152]{2,1,0:T(4,128)S(1)} %get-tuple-element.20), channel_id=1, source_target_pairs={{0,8},{4,12},{8,0},{12,4},{1,9},{5,13},{9,1},{13,5},{2,10},{6,14},... | collective-permute-start | bytes 110600 | tf_op jit(solution)/shard_map/ppermute | solution.py:306
  12.7 5.8 %collective-permute-start.3 = (f32[2,4,1152]{2,1,0:T(4,128)S(1)}, f32[2,4,1152]{2,1,0:T(4,128)S(1)}, u32[]{:S(2)}, u32[]{:S(2)}) collective-permute-start(f32[2,4,1152]{2,1,0:T(4,128)S(1)} %get-tuple-element.21), channel_id=1, source_target_pairs={{0,12},{4,8},{8,4},{12,0},{1,13},{5,9},{9,5},{13,1},{2,14},{6,10},... | collective-permute-start | bytes 110600 | tf_op jit(solution)/shard_map/ppermute | solution.py:306

commit v12 on v10

--- a/solution.py
+++ b/solution.py
@@ -20,9 +20,10 @@
 TRACE_PAD = 256
 FLAT = 36
 SENT = VARS * FLAT
-STEP = 192
+STEP = SENT + 1
 TAG_FACE = SENT
-TAG_ROW = SENT + 1
+TAG_SLOT = VARS * ROW
+ROW_STEP = TAG_SLOT + 1
 CELL_PAD = 384
 FACE_PAD = 40
 FACES_PAD = 256
@@ -73,7 +74,7 @@
                 first = (2 * axis + side) * FACE_PAD
                 face[index, first : first + FLAT] = np.einsum(spec, edge, lower, lower).reshape(FLAT, ROW)
     return (
-        split_table(lift[:4].reshape(-1, STEP)),
+        split_table(lift[:2].reshape(-1, STEP)) + split_table(lift[2:4].reshape(-1, STEP)),
         split_table(lift[4]),
         split_table(cell.reshape(-1, ROW)),
         split_table(face.reshape(-1, ROW)),
@@ -110,19 +111,30 @@
     return rank % size_x * size_y + rank // size_x
 
 
+def sublanes(row_cap):
+    return 2 if row_cap % 2 == 0 else 1
+
+
+def place_of(member, per_group):
+    peers, count = member.shape
+    block = jnp.sum(member * iota(member.shape, 0).astype(jnp.float32), axis=0, keepdims=True)
+    rank = jnp.sum(member * earlier(member), axis=0, keepdims=True)
+    group = jnp.zeros_like(rank)
+    for first in range(per_group, count, per_group):
+        group = group + (rank >= float(first)).astype(jnp.float32)
+    return group * float((peers - 1) * per_group) + block * float(per_group) + rank
+
+
 def owner_of(crow, peers, elements):
     first = device_of((peers, crow.shape[1])) * elements
     return ((crow >= first) & (crow < first + elements)).astype(jnp.float32)
 
 
-def row_places(crow, peers, elements, stride):
+def row_places(crow, peers, row_cap, elements):
     member = owner_of(crow, peers, elements)
-    rank = earlier(member)
-    block = iota(member.shape, 0).astype(jnp.float32)
-    place = jnp.sum(member * (block * stride + rank), axis=0, keepdims=True)
     owned = (device_of(member.shape) * elements).astype(jnp.float32)
     slot = crow.astype(jnp.float32) - jnp.sum(member * owned, axis=0, keepdims=True)
-    return place, slot
+    return place_of(member, sublanes(row_cap)), slot
 
 
 def onehot_rows(place, rows):
@@ -137,39 +149,32 @@
     return jnp.concatenate([x, jnp.zeros((x.shape[0], lanes - x.shape[1]), x.dtype)], axis=1)
 
 
-def pack_kernel(peers, cap, row_cap, elements, get, out, conf_out, message, sent):
-    dest, sub, elem, face, crow = [get(i) for i in range(5)]
-    count = dest.shape[1]
-    groups, slots = -(-cap // row_cap), peers * row_cap
-    member = (device_of((peers, count)) == dest).astype(jnp.float32)
-    block = jnp.sum(member * iota(member.shape, 0).astype(jnp.float32), axis=0, keepdims=True)
-    rank = jnp.sum(member * earlier(member), axis=0, keepdims=True)
-    group = sum([(rank >= float(g * row_cap)).astype(jnp.float32) for g in range(1, groups)], jnp.zeros_like(rank))
-    place = group * float(slots - row_cap) + block * float(row_cap) + rank
-    put = onehot_rows(place, groups * slots)
-    code_col = column(put, (face * elements + elem + 1).astype(jnp.float32))
-    row_place, row_slot = row_places(crow, peers, elements, row_cap)
-    row_col = column(onehot_rows(row_place, slots), row_slot + 1.0)
-    eye = (iota((count, count), 0) == iota((count, count), 1)).astype(jnp.float32)
-    sub_col = column(eye, sub.astype(jnp.float32))
-    x = pad_lanes(get(5), TRACE_PAD)
-    wide = jnp.concatenate([jnp.where(sub_col == float(s), x, 0.0) for s in range(4)], axis=1)
-    lifted_high, lifted_low = halves(dot3(*halves(wide), get(6), get(7)))
-    put = put.astype(jnp.bfloat16)
-    packed = dot(put, lifted_high) + dot(put, lifted_low)
+def pack_kernel(peers, cap, per_group, elements, get, out, conf_out, message, sent):
+    dest, sub, trace = [get(i) for i in range(3)]
+    groups, rows = -(-cap // per_group), peers * per_group
+    member = (device_of((peers, dest.shape[1])) == dest).astype(jnp.float32)
+    put = onehot_rows(place_of(member, per_group), groups * rows)
+    sub_col = column(put, sub.astype(jnp.float32))
+    move = put.astype(jnp.bfloat16)
+    high, low = [dot(move, half) for half in halves(pad_lanes(trace, TRACE_PAD))]
+    packed = jnp.zeros((groups * rows, STEP), jnp.float32)
+    for first in (0, 2):
+        wide = [
+            jnp.concatenate([jnp.where(sub_col == float(s), x, 0.0).astype(jnp.bfloat16) for s in (first, first + 1)], axis=1)
+            for x in (high, low)
+        ]
+        packed = packed + dot3(*wide, get(3 + first), get(4 + first))
+    code_col = column(put, (get(8) * elements + get(7) + 1).astype(jnp.float32))
     packed = jnp.where(iota(packed.shape, 1) == TAG_FACE, code_col, packed)
     for g in range(groups):
-        part = packed[g * slots : (g + 1) * slots]
-        if g == 0:
-            part = jnp.where(iota(part.shape, 1) == TAG_ROW, row_col, part)
-        message[:, :, g * STEP : (g + 1) * STEP] = part.reshape(peers, row_cap, STEP)
+        message[:, :, g * STEP : (g + 1) * STEP] = packed[g * rows : (g + 1) * rows].reshape(peers, per_group, STEP)
     send = pltpu.make_async_copy(message, out, sent.at[0])
     send.start()
-    cface, celem = get(8), get(9)
+    cface, celem = get(9), get(10)
     confs = cface.shape[1]
     eye = (iota((confs, confs), 0) == iota((confs, confs), 1)).astype(jnp.float32)
     conf_col = column(eye, (cface * elements + celem + 1).astype(jnp.float32))
-    conf = dot3(*halves(pad_lanes(get(10), TRACE_PAD)), get(11), get(12))
+    conf = dot3(*halves(pad_lanes(get(11), TRACE_PAD)), get(12), get(13))
     conf_out[...] = jnp.where(iota(conf.shape, 1) == TAG_FACE, conf_col, conf)
     send.wait()
 
@@ -178,12 +183,13 @@
     order, crow = get(0), get(1)
     elements = order.shape[1]
     slots = peers * row_cap
-    place, _ = row_places(crow, peers, elements, row_cap)
+    place, slot = row_places(crow, peers, row_cap, elements)
     take = onehot_rows(place, slots)
     order_col = column(take, order.astype(jnp.float32))
     elem_col = column(take, iota((1, elements), 1).astype(jnp.float32) + 1.0)
     lane = iota((slots, 128), 1)
-    col_out[...] = jnp.where(lane == 0, order_col, jnp.where(lane == 1, elem_col, 0.0))
+    slot_col = column(take, slot + 1.0)
+    col_out[...] = jnp.where(lane == 0, order_col, jnp.where(lane == 1, elem_col, slot_col))
     take = take.astype(jnp.bfloat16)
     spread[...] = jnp.zeros_like(spread)
     for half, part in enumerate(halves(get(2))):
@@ -198,8 +204,8 @@
 
 
 def face_kernel(peers, row_cap, elements, groups, get, incoming, conf, y, cols, table_high, table_low, out, spread):
-    slots = peers * row_cap
-    message = incoming[...].reshape(slots, incoming.shape[2])
+    slots, per_group = peers * row_cap, sublanes(row_cap)
+    message = incoming[...].reshape(peers * per_group, incoming.shape[2])
     x = jnp.concatenate([*[message[:, g * STEP : (g + 1) * STEP] for g in range(groups)], conf[...]], axis=0)
     code_col = x[:, TAG_FACE : TAG_FACE + 1]
     count = x.shape[0]
@@ -220,15 +226,23 @@
     wide = jnp.concatenate([jnp.where(order_rows == float(p), z, 0.0) for p in ORDERS], axis=1)
     high, low = halves(wide)
     total = y[...] + dot3(high, low, table_high[...], table_low[...])
-    for v in range(VARS):
-        out[:, :, v * ROW : (v + 1) * ROW] = total[v * slots : (v + 1) * slots].reshape(peers, row_cap, ROW)
-
-
-def place_kernel(peers, row_cap, get, arrived, message, out):
-    elements = out.shape[0]
-    rows = peers * row_cap
-    x = arrived[...].reshape(rows, arrived.shape[2])
-    slot_col = message[:, :, TAG_ROW : TAG_ROW + 1].reshape(rows, 1)
+    rows = peers * per_group
+    for j in range(row_cap // per_group):
+        for v in range(VARS):
+            part = total[v * slots + j * rows : v * slots + (j + 1) * rows]
+            first = j * ROW_STEP + v * ROW
+            out[:, :, first : first + ROW] = part.reshape(peers, per_group, ROW)
+        tag = cols[j * rows : (j + 1) * rows, 2:3]
+        first = j * ROW_STEP + TAG_SLOT
+        out[:, :, first : first + 1] = tag.reshape(peers, per_group, 1)
+
+
+def place_kernel(peers, row_cap, get, arrived, out):
+    elements, rows, per_group = out.shape[0], peers * row_cap, sublanes(row_cap)
+    message = arrived[...].reshape(peers * per_group, arrived.shape[2])
+    parts = [message[:, j * ROW_STEP : (j + 1) * ROW_STEP] for j in range(row_cap // per_group)]
+    x = jnp.concatenate([part[:, :TAG_SLOT] for part in parts], axis=0)
+    slot_col = jnp.concatenate([part[:, TAG_SLOT:] for part in parts], axis=0)
     slot_row = jnp.sum(jnp.where(iota((rows, rows), 0) == iota((rows, rows), 1), slot_col, 0.0), axis=0, keepdims=True)
     put = (iota((elements, rows), 0).astype(jnp.float32) + 1.0 == slot_row).astype(jnp.bfloat16)
     high, low = halves(x)
@@ -259,10 +273,9 @@
     return jax.ShapeDtypeStruct(a.shape, a.dtype)
 
 
-def call(kernel, outs, far, near=(), scratch=(), hand_on=(), out_far=(), flops=0):
+def call(kernel, outs, far, near=(), scratch=(), hand_on=(), flops=0):
     outs = [*outs, *[like(a) for a in hand_on]]
-    out_specs = [pl.BlockSpec(memory_space=pltpu.HBM if i in out_far else pltpu.VMEM) for i in range(len(outs))]
-    outs = [pltpu.HBM(a.shape, a.dtype) if i in out_far else a for i, a in enumerate(outs)]
+    out_specs = [pl.BlockSpec(memory_space=getattr(a, "memory_space", None) or pltpu.VMEM) for a in outs]
     sizes = [np.prod(a.shape) * a.dtype.itemsize for a in (*far, *near, *outs)]
     held = [pltpu.VMEM(a.shape, a.dtype) for a in far]
     far = (*far, *hand_on)
@@ -308,30 +321,29 @@
     cap = max(2, 2 * count // peers)
     row_cap = max(2, elements // peers)
     slots = peers * row_cap
-    groups = -(-cap // row_cap)
-    lanes = groups * STEP
+    per_group = sublanes(row_cap)
+    groups = -(-cap // per_group)
     lift, conf_lift, cell, face = [tuple(jnp.asarray(t) for t in pair) for pair in basis_tables()]
     f32 = jnp.float32
     line = lambda a: a.reshape(1, -1)
     order, coarse_row = line(order), line(coarse_row)
+    message = (peers, per_group, groups * STEP)
     outgoing, conf = call(
-        functools.partial(pack_kernel, peers, cap, row_cap, elements),
-        [jax.ShapeDtypeStruct((peers, row_cap, lanes), f32), jax.ShapeDtypeStruct((confs, STEP), f32)],
+        functools.partial(pack_kernel, peers, cap, per_group, elements),
+        [pltpu.HBM(message, f32), jax.ShapeDtypeStruct((confs, STEP), f32)],
         (
             line(mortar_dest),
             line(mortar_sub),
+            mortar_trace,
+            *lift,
             line(mortar_elem),
             line(mortar_face),
-            coarse_row,
-            mortar_trace,
-            *lift,
             line(conf_face),
             line(conf_elem),
             conf_trace,
             *conf_lift,
         ),
-        scratch=[pltpu.VMEM((peers, row_cap, lanes), f32), pltpu.SemaphoreType.DMA((1,))],
-        out_far=(0,),
+        scratch=[pltpu.VMEM(message, f32), pltpu.SemaphoreType.DMA((1,))],
     )
     incoming = exchange(outgoing)
     conf = from_behind(conf, "gz", 1)
@@ -344,7 +356,7 @@
     )
     (rows,) = call(
         functools.partial(face_kernel, peers, row_cap, elements, groups),
-        [jax.ShapeDtypeStruct((peers, row_cap, VARS * ROW), f32)],
+        [jax.ShapeDtypeStruct((peers, per_group, row_cap // per_group * ROW_STEP), f32)],
         (),
         (incoming, conf, y, cols, *face),
         scratch=[pltpu.VMEM((VARS * slots, FACES_PAD), f32)],
@@ -353,7 +365,7 @@
         functools.partial(place_kernel, peers, row_cap),
         [jax.ShapeDtypeStruct((elements, VARS * ROW), f32)],
         (),
-        (exchange(rows), incoming),
+        (exchange(rows),),
     )
     return out
 

time: 29.8 us -> 30.2 us (1.013)
  Pallas kernels: 7.28 us -> 7.8 us
    pallas_call x4, Pallas kernels: 7.28 us -> 7.8 us  [call(): pl.pallas_call(functools.partial(fetched, kernel, len(far), len(hand_on),...]
where the time goes in v12:
time: 30.2 us; the launch traced here: 29.9 us
  blocking collectives  9.8 us (32%)
  Pallas kernels  7.8 us (26%)
  starting transfers between devices  7.3 us (24%)
  waiting for transfers between devices  4.99 us (17%)
    all_to_all x1, blocking collectives, exchange(): lax.all_to_all(block, ('gy', 'gx'), split_axis=0, concat_axis=0, tiled=True)  9.8 us
    pallas_call x4, Pallas kernels, call(): pl.pallas_call(functools.partial(fetched, kernel, len(far), len(hand_on),...  7.8 us
    all_to_all x1, starting transfers between devices, exchange(): lax.all_to_all(block, ('gy', 'gx'), split_axis=0, concat_axis=0, tiled=True)  7.3 us
    all_to_all x1, waiting for transfers between devices, exchange(): lax.all_to_all(block, ('gy', 'gx'), split_axis=0, concat_axis=0, tiled=True)  3.71 us
    ppermute x1, waiting for transfers between devices, from_behind(): return lax.ppermute(block, axis, route)  1.29 us
  transfers between devices with their start and end apart: 2, of which 2 were waited for; matrix products, arithmetic and copies ran while one was open for 0% of the time, Pallas kernels for 8%

profile of v12, /device:TPU:0, one launch (start us, length us, event | category | flops | bytes accessed | tf_op | source)
XLA Modules:
  0.0 29.9 jit_solution(7651194383360055534)
XLA Ops:
  0.0 3.2 %shard_map.199 = (f32[8,2,2172]{2,1,0:T(2,128)}, f32[64,181]{1,0:T(8,128)S(1)}) custom-call(s32[1,96]{1,0:T(1,128)} %bitcast.8, s32[1,96]{1,0:T(1,128)} %bitcast.9, f32[96,245]{1,0:T(8,128)} %refs_2_.2, bf16[512,181]{1,0:T(8,128)(2,1)} %constant.20.clone.refs_3_, bf16[512,181]{1,0:T(8,128)(2,1)} %constant.21.clone.refs_4_, ...), custom_call_target="tpu_custom_call" | custom-call | bytes 1270912 | tf_op jit(solution)/shard_map/pallas_call | solution.py:283
  3.2 7.3 %all-to-all-start = ((f32[8,2,2172]{2,1,0:T(2,128)}), f32[8,2,2172]{2,1,0:T(2,128)S(1)}, u32[]{:S(2)}, u32[]{:S(2)}) async-start(f32[8,2,2172]{2,1,0:T(2,128)} %get-tuple-element.11), calls=%async_computation | async-start | bytes 278528 | tf_op jit(solution)/shard_map/all_to_all | solution.py:295
  10.5 0.0 collective-permute-start
  10.5 2.4 %shard_map.200 = (f32[160,216]{1,0:T(8,128)S(1)}, f32[32,128]{1,0:T(8,128)S(1)}, bf16[1280,216]{1,0:T(8,128)(2,1)S(1)}, bf16[1280,216]{1,0:T(8,128)(2,1)S(1)}) custom-call(s32[1,32]{1,0:T(1,128)} %bitcast.14, s32[1,32]{1,0:T(1,128)} %bitcast.15, f32[32,1715]{1,0:T(8,128)} %refs_2_.3, bf16[1920,216]{1,0:T(8,128)(2,1)} %constant.26.clone.refs_3_, ...), custom_call_target="tpu_custom_call" | custom-call | bytes 3139200 | tf_op jit(solution)/shard_map/pallas_call | solution.py:283
  12.9 1.3 %collective-permute-done.refs_1_ = f32[64,181]{1,0:T(8,128)S(1)} collective-permute-done((f32[64,181]{1,0:T(8,128)S(1)}, f32[64,181]{1,0:T(8,128)S(1)}, u32[]{:S(2)}, u32[]{:S(2)}) %collective-permute-start) | collective-permute-done | bytes 46368 | tf_op jit(solution)/shard_map/ppermute | solution.py:301
  14.2 3.7 %all-to-all-done.refs_0_ = f32[8,2,2172]{2,1,0:T(2,128)S(1)} async-done(((f32[8,2,2172]{2,1,0:T(2,128)}), f32[8,2,2172]{2,1,0:T(2,128)S(1)}, u32[]{:S(2)}, u32[]{:S(2)}) %all-to-all-start) | async-done | bytes 139040 | tf_op jit(solution)/shard_map/all_to_all | solution.py:295
  17.9 1.2 %shard_map.201 = f32[8,2,2162]{2,1,0:T(2,128)S(1)} custom-call(f32[8,2,2172]{2,1,0:T(2,128)S(1)} %all-to-all-done.refs_0_, f32[64,181]{1,0:T(8,128)S(1)} %collective-permute-done.refs_1_, f32[160,216]{1,0:T(8,128)S(1)} %get-tuple-element.13.refs_2_, f32[32,128]{1,0:T(8,128)S(1)} %get-tuple-element.14.refs_3_, ...), custom_call_target="tpu_custom_call" | custom-call | bytes 1584256 | tf_op jit(solution)/shard_map/pallas_call | solution.py:283
  19.1 9.8 %all_to_all.10.refs_0_ = f32[8,2,2162]{2,1,0:T(2,128)S(1)} all-to-all(f32[8,2,2162]{2,1,0:T(2,128)S(1)} %shard_map.201), channel_id=1, replica_groups=mesh['gx'=2,'gy'=4,'gz'=4] {'gy','gx'}, dimensions={0} | all-to-all | bytes 276736 | tf_op jit(solution)/shard_map/all_to_all | solution.py:295
  28.9 1.0 %shard_map.202 = f32[32,1080]{1,0:T(8,128)} custom-call(f32[8,2,2162]{2,1,0:T(2,128)S(1)} %all_to_all.10.refs_0_), custom_call_target="tpu_custom_call" | custom-call | bytes 276608 | tf_op jit(solution)/shard_map/pallas_call | solution.py:283
Async XLA Ops:
  3.2 14.7 %all-to-all-start = ((f32[8,2,2172]{2,1,0:T(2,128)}), f32[8,2,2172]{2,1,0:T(2,128)S(1)}, u32[]{:S(2)}, u32[]{:S(2)}) async-start(f32[8,2,2172]{2,1,0:T(2,128)} %get-tuple-element.11), calls=%async_computation | async-start | bytes 278528 | tf_op jit(solution)/shard_map/all_to_all | solution.py:295
  10.5 3.7 %collective-permute-start = (f32[64,181]{1,0:T(8,128)S(1)}, f32[64,181]{1,0:T(8,128)S(1)}, u32[]{:S(2)}, u32[]{:S(2)}) collective-permute-start(f32[64,181]{1,0:T(8,128)S(1)} %get-tuple-element.12), channel_id=1, source_target_pairs={{3,0},{0,1},{1,2},{2,3},{7,4},{4,5},{5,6},{6,7},{11,8},{8,9},{9,10... | collective-permute-start | bytes 139016 | tf_op jit(solution)/shard_map/ppermute | solution.py:301

commit v13 on v10

--- a/solution.py
+++ b/solution.py
@@ -22,7 +22,8 @@
 SENT = VARS * FLAT
 STEP = 192
 TAG_FACE = SENT
-TAG_ROW = SENT + 1
+ROWS_PAD = 1152
+TAG_SLOT = VARS * ROW
 CELL_PAD = 384
 FACE_PAD = 40
 FACES_PAD = 256
@@ -73,7 +74,7 @@
                 first = (2 * axis + side) * FACE_PAD
                 face[index, first : first + FLAT] = np.einsum(spec, edge, lower, lower).reshape(FLAT, ROW)
     return (
-        split_table(lift[:4].reshape(-1, STEP)),
+        split_table(lift[:4].transpose(1, 0, 2).reshape(TRACE_PAD, -1)),
         split_table(lift[4]),
         split_table(cell.reshape(-1, ROW)),
         split_table(face.reshape(-1, ROW)),
@@ -138,7 +139,7 @@
 
 
 def pack_kernel(peers, cap, row_cap, elements, get, out, conf_out, message, sent):
-    dest, sub, elem, face, crow = [get(i) for i in range(5)]
+    dest, elem, face, sub = [get(i) for i in range(4)]
     count = dest.shape[1]
     groups, slots = -(-cap // row_cap), peers * row_cap
     member = (device_of((peers, count)) == dest).astype(jnp.float32)
@@ -148,28 +149,25 @@
     place = group * float(slots - row_cap) + block * float(row_cap) + rank
     put = onehot_rows(place, groups * slots)
     code_col = column(put, (face * elements + elem + 1).astype(jnp.float32))
-    row_place, row_slot = row_places(crow, peers, elements, row_cap)
-    row_col = column(onehot_rows(row_place, slots), row_slot + 1.0)
     eye = (iota((count, count), 0) == iota((count, count), 1)).astype(jnp.float32)
     sub_col = column(eye, sub.astype(jnp.float32))
-    x = pad_lanes(get(5), TRACE_PAD)
-    wide = jnp.concatenate([jnp.where(sub_col == float(s), x, 0.0) for s in range(4)], axis=1)
-    lifted_high, lifted_low = halves(dot3(*halves(wide), get(6), get(7)))
+    lifts = dot3(*halves(pad_lanes(get(4), TRACE_PAD)), get(5), get(6))
+    lifted = lifts[:, :STEP]
+    for s in range(1, 4):
+        lifted = jnp.where(sub_col == float(s), lifts[:, s * STEP : (s + 1) * STEP], lifted)
+    lifted_high, lifted_low = halves(lifted)
     put = put.astype(jnp.bfloat16)
     packed = dot(put, lifted_high) + dot(put, lifted_low)
     packed = jnp.where(iota(packed.shape, 1) == TAG_FACE, code_col, packed)
     for g in range(groups):
-        part = packed[g * slots : (g + 1) * slots]
-        if g == 0:
-            part = jnp.where(iota(part.shape, 1) == TAG_ROW, row_col, part)
-        message[:, :, g * STEP : (g + 1) * STEP] = part.reshape(peers, row_cap, STEP)
+        message[:, :, g * STEP : (g + 1) * STEP] = packed[g * slots : (g + 1) * slots].reshape(peers, row_cap, STEP)
     send = pltpu.make_async_copy(message, out, sent.at[0])
     send.start()
-    cface, celem = get(8), get(9)
+    cface, celem = get(7), get(8)
     confs = cface.shape[1]
     eye = (iota((confs, confs), 0) == iota((confs, confs), 1)).astype(jnp.float32)
     conf_col = column(eye, (cface * elements + celem + 1).astype(jnp.float32))
-    conf = dot3(*halves(pad_lanes(get(10), TRACE_PAD)), get(11), get(12))
+    conf = dot3(*halves(pad_lanes(get(9), TRACE_PAD)), get(10), get(11))
     conf_out[...] = jnp.where(iota(conf.shape, 1) == TAG_FACE, conf_col, conf)
     send.wait()
 
@@ -178,12 +176,13 @@
     order, crow = get(0), get(1)
     elements = order.shape[1]
     slots = peers * row_cap
-    place, _ = row_places(crow, peers, elements, row_cap)
+    place, slot = row_places(crow, peers, elements, row_cap)
     take = onehot_rows(place, slots)
     order_col = column(take, order.astype(jnp.float32))
     elem_col = column(take, iota((1, elements), 1).astype(jnp.float32) + 1.0)
     lane = iota((slots, 128), 1)
-    col_out[...] = jnp.where(lane == 0, order_col, jnp.where(lane == 1, elem_col, 0.0))
+    slot_col = column(take, slot + 1.0)
+    col_out[...] = jnp.where(lane == 0, order_col, jnp.where(lane == 1, elem_col, slot_col))
     take = take.astype(jnp.bfloat16)
     spread[...] = jnp.zeros_like(spread)
     for half, part in enumerate(halves(get(2))):
@@ -216,24 +215,23 @@
                 f * slots : (f + 1) * slots, v * FLAT : (v + 1) * FLAT
             ]
     order_rows = jnp.concatenate([order_col] * VARS, axis=0)
-    z = spread[...]
-    wide = jnp.concatenate([jnp.where(order_rows == float(p), z, 0.0) for p in ORDERS], axis=1)
-    high, low = halves(wide)
+    masks = [(order_rows == float(p)).astype(jnp.bfloat16) for p in ORDERS]
+    high, low = [jnp.concatenate([half * mask for mask in masks], axis=1) for half in halves(spread[...])]
     total = y[...] + dot3(high, low, table_high[...], table_low[...])
     for v in range(VARS):
         out[:, :, v * ROW : (v + 1) * ROW] = total[v * slots : (v + 1) * slots].reshape(peers, row_cap, ROW)
-
-
-def place_kernel(peers, row_cap, get, arrived, message, out):
+    out[:, :, TAG_SLOT : TAG_SLOT + 1] = cols[:, 2:3].reshape(peers, row_cap, 1)
+
+
+def place_kernel(peers, row_cap, get, arrived, out):
     elements = out.shape[0]
     rows = peers * row_cap
-    x = arrived[...].reshape(rows, arrived.shape[2])
-    slot_col = message[:, :, TAG_ROW : TAG_ROW + 1].reshape(rows, 1)
+    message = arrived[...].reshape(rows, arrived.shape[2])
+    x, slot_col = message[:, :TAG_SLOT], message[:, TAG_SLOT : TAG_SLOT + 1]
     slot_row = jnp.sum(jnp.where(iota((rows, rows), 0) == iota((rows, rows), 1), slot_col, 0.0), axis=0, keepdims=True)
     put = (iota((elements, rows), 0).astype(jnp.float32) + 1.0 == slot_row).astype(jnp.bfloat16)
     high, low = halves(x)
-    rest = (x - high.astype(jnp.float32) - low.astype(jnp.float32)).astype(jnp.bfloat16)
-    out[...] = dot(put, high) + dot(put, low) + dot(put, rest)
+    out[...] = dot(put, high) + dot(put, low)
 
 
 def fetched(kernel, n_far, n_pass, n_near, n_out, *refs):
@@ -259,10 +257,9 @@
     return jax.ShapeDtypeStruct(a.shape, a.dtype)
 
 
-def call(kernel, outs, far, near=(), scratch=(), hand_on=(), out_far=(), flops=0):
+def call(kernel, outs, far, near=(), scratch=(), hand_on=(), flops=0):
     outs = [*outs, *[like(a) for a in hand_on]]
-    out_specs = [pl.BlockSpec(memory_space=pltpu.HBM if i in out_far else pltpu.VMEM) for i in range(len(outs))]
-    outs = [pltpu.HBM(a.shape, a.dtype) if i in out_far else a for i, a in enumerate(outs)]
+    out_specs = [pl.BlockSpec(memory_space=getattr(a, "memory_space", None) or pltpu.VMEM) for a in outs]
     sizes = [np.prod(a.shape) * a.dtype.itemsize for a in (*far, *near, *outs)]
     held = [pltpu.VMEM(a.shape, a.dtype) for a in far]
     far = (*far, *hand_on)
@@ -314,15 +311,15 @@
     f32 = jnp.float32
     line = lambda a: a.reshape(1, -1)
     order, coarse_row = line(order), line(coarse_row)
+    message = (peers, row_cap, lanes)
     outgoing, conf = call(
         functools.partial(pack_kernel, peers, cap, row_cap, elements),
-        [jax.ShapeDtypeStruct((peers, row_cap, lanes), f32), jax.ShapeDtypeStruct((confs, STEP), f32)],
+        [pltpu.HBM(message, f32), jax.ShapeDtypeStruct((confs, STEP), f32)],
         (
             line(mortar_dest),
-            line(mortar_sub),
             line(mortar_elem),
             line(mortar_face),
-            coarse_row,
+            line(mortar_sub),
             mortar_trace,
             *lift,
             line(conf_face),
@@ -330,8 +327,7 @@
             conf_trace,
             *conf_lift,
         ),
-        scratch=[pltpu.VMEM((peers, row_cap, lanes), f32), pltpu.SemaphoreType.DMA((1,))],
-        out_far=(0,),
+        scratch=[pltpu.VMEM(message, f32), pltpu.SemaphoreType.DMA((1,))],
     )
     incoming = exchange(outgoing)
     conf = from_behind(conf, "gz", 1)
@@ -344,7 +340,7 @@
     )
     (rows,) = call(
         functools.partial(face_kernel, peers, row_cap, elements, groups),
-        [jax.ShapeDtypeStruct((peers, row_cap, VARS * ROW), f32)],
+        [jax.ShapeDtypeStruct((peers, row_cap, ROWS_PAD), f32)],
         (),
         (incoming, conf, y, cols, *face),
         scratch=[pltpu.VMEM((VARS * slots, FACES_PAD), f32)],
@@ -353,7 +349,7 @@
         functools.partial(place_kernel, peers, row_cap),
         [jax.ShapeDtypeStruct((elements, VARS * ROW), f32)],
         (),
-        (exchange(rows), incoming),
+        (exchange(rows),),
     )
     return out
 

time: 29.8 us -> 29.8 us (level)
  no operation moved by 1% of the time
where the time goes in v13:
time: 29.8 us; the launch traced here: 29.5 us
  blocking collectives  9.85 us (33%)
  Pallas kernels  7.29 us (24%)
  starting transfers between devices  7.29 us (24%)
  waiting for transfers between devices  5.05 us (17%)
    all_to_all x1, blocking collectives, exchange(): lax.all_to_all(block, ('gy', 'gx'), split_axis=0, concat_axis=0, tiled=True)  9.85 us
    all_to_all x1, starting transfers between devices, exchange(): lax.all_to_all(block, ('gy', 'gx'), split_axis=0, concat_axis=0, tiled=True)  7.29 us
    pallas_call x4, Pallas kernels, call(): pl.pallas_call(functools.partial(fetched, kernel, len(far), len(hand_on),...  7.29 us
    all_to_all x1, waiting for transfers between devices, exchange(): lax.all_to_all(block, ('gy', 'gx'), split_axis=0, concat_axis=0, tiled=True)  3.76 us
    ppermute x1, waiting for transfers between devices, from_behind(): return lax.ppermute(block, axis, route)  1.29 us
  transfers between devices with their start and end apart: 2, of which 2 were waited for; matrix products, arithmetic and copies ran while one was open for 0% of the time, Pallas kernels for 8%

profile of v13, /device:TPU:0, one launch (start us, length us, event | category | flops | bytes accessed | tf_op | source)
XLA Modules:
  0.0 29.5 jit_solution(15035910875194727204)
XLA Ops:
  0.0 2.9 %shard_map.181 = (f32[8,4,1152]{2,1,0:T(4,128)}, f32[64,192]{1,0:T(8,128)S(1)}) custom-call(s32[1,96]{1,0:T(1,128)} %bitcast.8, s32[1,96]{1,0:T(1,128)} %bitcast.9, s32[1,96]{1,0:T(1,128)} %bitcast.10, s32[1,96]{1,0:T(1,128)} %bitcast.11, f32[96,245]{1,0:T(8,128)} %refs_4_.2, bf16[256,768]{1,0:T(8,128)(2,1)} %constant.16.clone.refs_5_, ...), custom_call_target="tpu_custom_call" | custom-call | bytes 1338496 | tf_op jit(solution)/shard_map/pallas_call | solution.py:267
  2.9 7.3 %all-to-all-start = ((f32[8,4,1152]{2,1,0:T(4,128)}), f32[8,4,1152]{2,1,0:T(4,128)S(1)}, u32[]{:S(2)}, u32[]{:S(2)}) async-start(f32[8,4,1152]{2,1,0:T(4,128)} %get-tuple-element.11), calls=%async_computation | async-start | bytes 294912 | tf_op jit(solution)/shard_map/all_to_all | solution.py:279
  10.2 0.0 collective-permute-start
  10.2 2.4 %shard_map.182 = (f32[160,216]{1,0:T(8,128)S(1)}, f32[32,128]{1,0:T(8,128)S(1)}, bf16[1280,216]{1,0:T(8,128)(2,1)S(1)}, bf16[1280,216]{1,0:T(8,128)(2,1)S(1)}) custom-call(s32[1,32]{1,0:T(1,128)} %bitcast.14, s32[1,32]{1,0:T(1,128)} %bitcast.15, f32[32,1715]{1,0:T(8,128)} %refs_2_.1, bf16[1920,216]{1,0:T(8,128)(2,1)} %constant.20.clone.refs_3_, ...), custom_call_target="tpu_custom_call" | custom-call | bytes 3139200 | tf_op jit(solution)/shard_map/pallas_call | solution.py:267
  12.6 1.3 %collective-permute-done.refs_1_ = f32[64,192]{1,0:T(8,128)S(1)} collective-permute-done((f32[64,192]{1,0:T(8,128)S(1)}, f32[64,192]{1,0:T(8,128)S(1)}, u32[]{:S(2)}, u32[]{:S(2)}) %collective-permute-start) | collective-permute-done | bytes 49184 | tf_op jit(solution)/shard_map/ppermute | solution.py:285
  13.9 3.8 %all-to-all-done.refs_0_ = f32[8,4,1152]{2,1,0:T(4,128)S(1)} async-done(((f32[8,4,1152]{2,1,0:T(4,128)}), f32[8,4,1152]{2,1,0:T(4,128)S(1)}, u32[]{:S(2)}, u32[]{:S(2)}) %all-to-all-start) | async-done | bytes 147488 | tf_op jit(solution)/shard_map/all_to_all | solution.py:279
  17.6 1.1 %shard_map.183 = f32[8,4,1152]{2,1,0:T(4,128)S(1)} custom-call(f32[8,4,1152]{2,1,0:T(4,128)S(1)} %all-to-all-done.refs_0_, f32[64,192]{1,0:T(8,128)S(1)} %collective-permute-done.refs_1_, f32[160,216]{1,0:T(8,128)S(1)} %get-tuple-element.13.refs_2_, f32[32,128]{1,0:T(8,128)S(1)} %get-tuple-element.14.refs_3_, ...), custom_call_target="tpu_custom_call" | custom-call | bytes 1604608 | tf_op jit(solution)/shard_map/pallas_call | solution.py:267
  18.7 9.9 %all_to_all.10.refs_0_ = f32[8,4,1152]{2,1,0:T(4,128)S(1)} all-to-all(f32[8,4,1152]{2,1,0:T(4,128)S(1)} %shard_map.183), channel_id=1, replica_groups=mesh['gx'=2,'gy'=4,'gz'=4] {'gy','gx'}, dimensions={0} | all-to-all | bytes 294912 | tf_op jit(solution)/shard_map/all_to_all | solution.py:279
  28.6 0.9 %shard_map.184 = f32[32,1080]{1,0:T(8,128)} custom-call(f32[8,4,1152]{2,1,0:T(4,128)S(1)} %all_to_all.10.refs_0_), custom_call_target="tpu_custom_call" | custom-call | bytes 285696 | tf_op jit(solution)/shard_map/pallas_call | solution.py:267
Async XLA Ops:
  2.9 14.7 %all-to-all-start = ((f32[8,4,1152]{2,1,0:T(4,128)}), f32[8,4,1152]{2,1,0:T(4,128)S(1)}, u32[]{:S(2)}, u32[]{:S(2)}) async-start(f32[8,4,1152]{2,1,0:T(4,128)} %get-tuple-element.11), calls=%async_computation | async-start | bytes 294912 | tf_op jit(solution)/shard_map/all_to_all | solution.py:279
  10.2 3.7 %collective-permute-start = (f32[64,192]{1,0:T(8,128)S(1)}, f32[64,192]{1,0:T(8,128)S(1)}, u32[]{:S(2)}, u32[]{:S(2)}) collective-permute-start(f32[64,192]{1,0:T(8,128)S(1)} %get-tuple-element.12), channel_id=1, source_target_pairs={{3,0},{0,1},{1,2},{2,3},{7,4},{4,5},{5,6},{6,7},{11,8},{8,9},{9,10... | collective-permute-start | bytes 147464 | tf_op jit(solution)/shard_map/ppermute | solution.py:285

commit v14 on v13

--- a/solution.py
+++ b/solution.py
@@ -74,7 +74,7 @@
                 first = (2 * axis + side) * FACE_PAD
                 face[index, first : first + FLAT] = np.einsum(spec, edge, lower, lower).reshape(FLAT, ROW)
     return (
-        split_table(lift[:4].transpose(1, 0, 2).reshape(TRACE_PAD, -1)),
+        split_table(lift[:2].reshape(-1, STEP)) + split_table(lift[2:4].reshape(-1, STEP)),
         split_table(lift[4]),
         split_table(cell.reshape(-1, ROW)),
         split_table(face.reshape(-1, ROW)),
@@ -139,7 +139,7 @@
 
 
 def pack_kernel(peers, cap, row_cap, elements, get, out, conf_out, message, sent):
-    dest, elem, face, sub = [get(i) for i in range(4)]
+    dest, sub = get(0), get(1)
     count = dest.shape[1]
     groups, slots = -(-cap // row_cap), peers * row_cap
     member = (device_of((peers, count)) == dest).astype(jnp.float32)
@@ -148,28 +148,38 @@
     group = sum([(rank >= float(g * row_cap)).astype(jnp.float32) for g in range(1, groups)], jnp.zeros_like(rank))
     place = group * float(slots - row_cap) + block * float(row_cap) + rank
     put = onehot_rows(place, groups * slots)
-    code_col = column(put, (face * elements + elem + 1).astype(jnp.float32))
     eye = (iota((count, count), 0) == iota((count, count), 1)).astype(jnp.float32)
     sub_col = column(eye, sub.astype(jnp.float32))
-    lifts = dot3(*halves(pad_lanes(get(4), TRACE_PAD)), get(5), get(6))
-    lifted = lifts[:, :STEP]
-    for s in range(1, 4):
-        lifted = jnp.where(sub_col == float(s), lifts[:, s * STEP : (s + 1) * STEP], lifted)
+    high, low = halves(pad_lanes(get(2), TRACE_PAD))
+    masks = [(sub_col == float(s)).astype(jnp.bfloat16) for s in range(4)]
+    lifted = jnp.zeros((count, STEP), jnp.float32)
+    for first in (0, 2):
+        wide = [jnp.concatenate([half * mask for mask in masks[first : first + 2]], axis=1) for half in (high, low)]
+        lifted = lifted + dot3(*wide, get(3 + first), get(4 + first))
     lifted_high, lifted_low = halves(lifted)
+    code_col = column(put, (get(8) * elements + get(7) + 1).astype(jnp.float32))
     put = put.astype(jnp.bfloat16)
     packed = dot(put, lifted_high) + dot(put, lifted_low)
     packed = jnp.where(iota(packed.shape, 1) == TAG_FACE, code_col, packed)
-    for g in range(groups):
-        message[:, :, g * STEP : (g + 1) * STEP] = packed[g * slots : (g + 1) * slots].reshape(peers, row_cap, STEP)
-    send = pltpu.make_async_copy(message, out, sent.at[0])
-    send.start()
-    cface, celem = get(7), get(8)
+    bounds = (0, groups // 2 // 2 * 2, groups)
+    sends = []
+    for half, (first, last) in enumerate(zip(bounds[:-1], bounds[1:])):
+        if first == last:
+            continue
+        for g in range(first, last):
+            message[:, :, g * STEP : (g + 1) * STEP] = packed[g * slots : (g + 1) * slots].reshape(peers, row_cap, STEP)
+        lanes = pl.ds(first * STEP, (last - first) * STEP)
+        send = pltpu.make_async_copy(message.at[:, :, lanes], out.at[:, :, lanes], sent.at[half])
+        send.start()
+        sends.append(send)
+    cface, celem = get(9), get(10)
     confs = cface.shape[1]
     eye = (iota((confs, confs), 0) == iota((confs, confs), 1)).astype(jnp.float32)
     conf_col = column(eye, (cface * elements + celem + 1).astype(jnp.float32))
-    conf = dot3(*halves(pad_lanes(get(9), TRACE_PAD)), get(10), get(11))
+    conf = dot3(*halves(pad_lanes(get(11), TRACE_PAD)), get(12), get(13))
     conf_out[...] = jnp.where(iota(conf.shape, 1) == TAG_FACE, conf_col, conf)
-    send.wait()
+    for send in sends:
+        send.wait()
 
 
 def cell_kernel(peers, row_cap, get, y_out, col_out, spread):
@@ -215,8 +225,9 @@
                 f * slots : (f + 1) * slots, v * FLAT : (v + 1) * FLAT
             ]
     order_rows = jnp.concatenate([order_col] * VARS, axis=0)
-    masks = [(order_rows == float(p)).astype(jnp.bfloat16) for p in ORDERS]
-    high, low = [jnp.concatenate([half * mask for mask in masks], axis=1) for half in halves(spread[...])]
+    z = spread[...]
+    wide = jnp.concatenate([jnp.where(order_rows == float(p), z, 0.0) for p in ORDERS], axis=1)
+    high, low = halves(wide)
     total = y[...] + dot3(high, low, table_high[...], table_low[...])
     for v in range(VARS):
         out[:, :, v * ROW : (v + 1) * ROW] = total[v * slots : (v + 1) * slots].reshape(peers, row_cap, ROW)
@@ -317,17 +328,17 @@
         [pltpu.HBM(message, f32), jax.ShapeDtypeStruct((confs, STEP), f32)],
         (
             line(mortar_dest),
-            line(mortar_elem),
-            line(mortar_face),
             line(mortar_sub),
             mortar_trace,
             *lift,
+            line(mortar_elem),
+            line(mortar_face),
             line(conf_face),
             line(conf_elem),
             conf_trace,
             *conf_lift,
         ),
-        scratch=[pltpu.VMEM(message, f32), pltpu.SemaphoreType.DMA((1,))],
+        scratch=[pltpu.VMEM(message, f32), pltpu.SemaphoreType.DMA((2,))],
     )
     incoming = exchange(outgoing)
     conf = from_behind(conf, "gz", 1)

time: 29.8 us -> 29.7 us (level)
  no operation moved by 1% of the time
where the time goes in v14:
time: 29.7 us; the launch traced here: 29.4 us
  blocking collectives  9.85 us (33%)
  starting transfers between devices  7.3 us (25%)
  Pallas kernels  7.19 us (24%)
  waiting for transfers between devices  5.05 us (17%)
    all_to_all x1, blocking collectives, exchange(): lax.all_to_all(block, ('gy', 'gx'), split_axis=0, concat_axis=0, tiled=True)  9.85 us
    all_to_all x1, starting transfers between devices, exchange(): lax.all_to_all(block, ('gy', 'gx'), split_axis=0, concat_axis=0, tiled=True)  7.3 us
    pallas_call x4, Pallas kernels, call(): pl.pallas_call(functools.partial(fetched, kernel, len(far), len(hand_on),...  7.19 us
    all_to_all x1, waiting for transfers between devices, exchange(): lax.all_to_all(block, ('gy', 'gx'), split_axis=0, concat_axis=0, tiled=True)  3.76 us
    ppermute x1, waiting for transfers between devices, from_behind(): return lax.ppermute(block, axis, route)  1.29 us
  transfers between devices with their start and end apart: 2, of which 2 were waited for; matrix products, arithmetic and copies ran while one was open for 0% of the time, Pallas kernels for 8%

profile of v14, /device:TPU:0, one launch (start us, length us, event | category | flops | bytes accessed | tf_op | source)
XLA Modules:
  0.0 29.4 jit_solution(10980684494736988234)
XLA Ops:
  0.0 2.8 %shard_map.199 = (f32[8,4,1152]{2,1,0:T(4,128)}, f32[64,192]{1,0:T(8,128)S(1)}) custom-call(s32[1,96]{1,0:T(1,128)} %bitcast.8, s32[1,96]{1,0:T(1,128)} %bitcast.9, f32[96,245]{1,0:T(8,128)} %refs_2_.2, bf16[512,192]{1,0:T(8,128)(2,1)} %constant.20.clone.refs_3_, bf16[512,192]{1,0:T(8,128)(2,1)} %constant.21.clone.refs_4_, ...), custom_call_target="tpu_custom_call" | custom-call | bytes 1338496 | tf_op jit(solution)/shard_map/pallas_call | solution.py:278
  2.8 7.3 %all-to-all-start = ((f32[8,4,1152]{2,1,0:T(4,128)}), f32[8,4,1152]{2,1,0:T(4,128)S(1)}, u32[]{:S(2)}, u32[]{:S(2)}) async-start(f32[8,4,1152]{2,1,0:T(4,128)} %get-tuple-element.11), calls=%async_computation | async-start | bytes 294912 | tf_op jit(solution)/shard_map/all_to_all | solution.py:290
  10.1 0.0 collective-permute-start
  10.1 2.4 %shard_map.200 = (f32[160,216]{1,0:T(8,128)S(1)}, f32[32,128]{1,0:T(8,128)S(1)}, bf16[1280,216]{1,0:T(8,128)(2,1)S(1)}, bf16[1280,216]{1,0:T(8,128)(2,1)S(1)}) custom-call(s32[1,32]{1,0:T(1,128)} %bitcast.14, s32[1,32]{1,0:T(1,128)} %bitcast.15, f32[32,1715]{1,0:T(8,128)} %refs_2_.3, bf16[1920,216]{1,0:T(8,128)(2,1)} %constant.26.clone.refs_3_, ...), custom_call_target="tpu_custom_call" | custom-call | bytes 3139200 | tf_op jit(solution)/shard_map/pallas_call | solution.py:278
  12.5 1.3 %collective-permute-done.refs_1_ = f32[64,192]{1,0:T(8,128)S(1)} collective-permute-done((f32[64,192]{1,0:T(8,128)S(1)}, f32[64,192]{1,0:T(8,128)S(1)}, u32[]{:S(2)}, u32[]{:S(2)}) %collective-permute-start) | collective-permute-done | bytes 49184 | tf_op jit(solution)/shard_map/ppermute | solution.py:296
  13.8 3.8 %all-to-all-done.refs_0_ = f32[8,4,1152]{2,1,0:T(4,128)S(1)} async-done(((f32[8,4,1152]{2,1,0:T(4,128)}), f32[8,4,1152]{2,1,0:T(4,128)S(1)}, u32[]{:S(2)}, u32[]{:S(2)}) %all-to-all-start) | async-done | bytes 147488 | tf_op jit(solution)/shard_map/all_to_all | solution.py:290
  17.6 1.1 %shard_map.201 = f32[8,4,1152]{2,1,0:T(4,128)S(1)} custom-call(f32[8,4,1152]{2,1,0:T(4,128)S(1)} %all-to-all-done.refs_0_, f32[64,192]{1,0:T(8,128)S(1)} %collective-permute-done.refs_1_, f32[160,216]{1,0:T(8,128)S(1)} %get-tuple-element.13.refs_2_, f32[32,128]{1,0:T(8,128)S(1)} %get-tuple-element.14.refs_3_, ...), custom_call_target="tpu_custom_call" | custom-call | bytes 1604608 | tf_op jit(solution)/shard_map/pallas_call | solution.py:278
  18.6 9.8 %all_to_all.10.refs_0_ = f32[8,4,1152]{2,1,0:T(4,128)S(1)} all-to-all(f32[8,4,1152]{2,1,0:T(4,128)S(1)} %shard_map.201), channel_id=1, replica_groups=mesh['gx'=2,'gy'=4,'gz'=4] {'gy','gx'}, dimensions={0} | all-to-all | bytes 294912 | tf_op jit(solution)/shard_map/all_to_all | solution.py:290
  28.5 0.9 %shard_map.202 = f32[32,1080]{1,0:T(8,128)} custom-call(f32[8,4,1152]{2,1,0:T(4,128)S(1)} %all_to_all.10.refs_0_), custom_call_target="tpu_custom_call" | custom-call | bytes 285696 | tf_op jit(solution)/shard_map/pallas_call | solution.py:278
Async XLA Ops:
  2.8 14.7 %all-to-all-start = ((f32[8,4,1152]{2,1,0:T(4,128)}), f32[8,4,1152]{2,1,0:T(4,128)S(1)}, u32[]{:S(2)}, u32[]{:S(2)}) async-start(f32[8,4,1152]{2,1,0:T(4,128)} %get-tuple-element.11), calls=%async_computation | async-start | bytes 294912 | tf_op jit(solution)/shard_map/all_to_all | solution.py:290
  10.1 3.7 %collective-permute-start = (f32[64,192]{1,0:T(8,128)S(1)}, f32[64,192]{1,0:T(8,128)S(1)}, u32[]{:S(2)}, u32[]{:S(2)}) collective-permute-start(f32[64,192]{1,0:T(8,128)S(1)} %get-tuple-element.12), channel_id=1, source_target_pairs={{3,0},{0,1},{1,2},{2,3},{7,4},{4,5},{5,6},{6,7},{11,8},{8,9},{9,10... | collective-permute-start | bytes 147464 | tf_op jit(solution)/shard_map/ppermute | solution.py:296

commit v15 on v14

--- a/solution.py
+++ b/solution.py
@@ -105,10 +105,13 @@
     return dot(member.astype(jnp.bfloat16), before.astype(jnp.bfloat16))
 
 
+def ranked(rank, size_y, where):
+    x, y = rank // size_y, rank % size_y
+    return x * size_y + where(x % 2 == 0, y, size_y - 1 - y)
+
+
 def device_of(shape):
-    size_x, size_y = lax.axis_size("gx"), lax.axis_size("gy")
-    rank = iota(shape, 0)
-    return rank % size_x * size_y + rank // size_x
+    return ranked(iota(shape, 0), lax.axis_size("gy"), jnp.where)
 
 
 def owner_of(crow, peers, elements):
@@ -287,7 +290,8 @@
 
 
 def exchange(block):
-    return lax.all_to_all(block, ("gy", "gx"), split_axis=0, concat_axis=0, tiled=True)
+    order = ranked(np.arange(block.shape[0]), lax.axis_size("gy"), np.where).tolist()
+    return lax.all_to_all(block, ("gx", "gy"), split_axis=0, concat_axis=0, tiled=True, axis_index_groups=[order])
 
 
 def from_behind(block, axis, distance):

time: 29.7 us -> 30.1 us (1.013)
  no operation moved by 1% of the time
where the time goes in v15:
time: 30.1 us; the launch traced here: 29.8 us
  blocking collectives  10 us (33%)
  starting transfers between devices  7.3 us (24%)
  Pallas kernels  7.19 us (24%)
  waiting for transfers between devices  5.25 us (17%)
    all_to_all x1, blocking collectives, exchange(): lax.all_to_all(block, ('gx', 'gy'), split_axis=0, concat_axis=0, tiled=Tr...  10 us
    all_to_all x1, starting transfers between devices, exchange(): lax.all_to_all(block, ('gx', 'gy'), split_axis=0, concat_axis=0, tiled=Tr...  7.3 us
    pallas_call x4, Pallas kernels, call(): pl.pallas_call(functools.partial(fetched, kernel, len(far), len(hand_on),...  7.19 us
    all_to_all x1, waiting for transfers between devices, exchange(): lax.all_to_all(block, ('gx', 'gy'), split_axis=0, concat_axis=0, tiled=Tr...  3.96 us
    ppermute x1, waiting for transfers between devices, from_behind(): return lax.ppermute(block, axis, route)  1.29 us
  transfers between devices with their start and end apart: 2, of which 2 were waited for; matrix products, arithmetic and copies ran while one was open for 0% of the time, Pallas kernels for 8%

profile of v15, /device:TPU:0, one launch (start us, length us, event | category | flops | bytes accessed | tf_op | source)
XLA Modules:
  0.0 29.8 jit_solution(5924147571255654909)
XLA Ops:
  0.0 2.8 %shard_map.199 = (f32[8,4,1152]{2,1,0:T(4,128)}, f32[64,192]{1,0:T(8,128)S(1)}) custom-call(s32[1,96]{1,0:T(1,128)} %bitcast.8, s32[1,96]{1,0:T(1,128)} %bitcast.9, f32[96,245]{1,0:T(8,128)} %refs_2_.2, bf16[512,192]{1,0:T(8,128)(2,1)} %constant.20.clone.refs_3_, bf16[512,192]{1,0:T(8,128)(2,1)} %constant.21.clone.refs_4_, ...), custom_call_target="tpu_custom_call" | custom-call | bytes 1338496 | tf_op jit(solution)/shard_map/pallas_call | solution.py:281
  2.8 7.3 %all-to-all-start = ((f32[8,4,1152]{2,1,0:T(4,128)}), f32[8,4,1152]{2,1,0:T(4,128)S(1)}, u32[]{:S(2)}, u32[]{:S(2)}) async-start(f32[8,4,1152]{2,1,0:T(4,128)} %get-tuple-element.11), calls=%async_computation | async-start | bytes 294912 | tf_op jit(solution)/shard_map/all_to_all | solution.py:294
  10.1 0.0 collective-permute-start
  10.1 2.4 %shard_map.200 = (f32[160,216]{1,0:T(8,128)S(1)}, f32[32,128]{1,0:T(8,128)S(1)}, bf16[1280,216]{1,0:T(8,128)(2,1)S(1)}, bf16[1280,216]{1,0:T(8,128)(2,1)S(1)}) custom-call(s32[1,32]{1,0:T(1,128)} %bitcast.14, s32[1,32]{1,0:T(1,128)} %bitcast.15, f32[32,1715]{1,0:T(8,128)} %refs_2_.3, bf16[1920,216]{1,0:T(8,128)(2,1)} %constant.26.clone.refs_3_, ...), custom_call_target="tpu_custom_call" | custom-call | bytes 3139200 | tf_op jit(solution)/shard_map/pallas_call | solution.py:281
  12.5 1.3 %collective-permute-done.refs_1_ = f32[64,192]{1,0:T(8,128)S(1)} collective-permute-done((f32[64,192]{1,0:T(8,128)S(1)}, f32[64,192]{1,0:T(8,128)S(1)}, u32[]{:S(2)}, u32[]{:S(2)}) %collective-permute-start) | collective-permute-done | bytes 49184 | tf_op jit(solution)/shard_map/ppermute | solution.py:300
  13.8 4.0 %all-to-all-done.refs_0_ = f32[8,4,1152]{2,1,0:T(4,128)S(1)} async-done(((f32[8,4,1152]{2,1,0:T(4,128)}), f32[8,4,1152]{2,1,0:T(4,128)S(1)}, u32[]{:S(2)}, u32[]{:S(2)}) %all-to-all-start) | async-done | bytes 147488 | tf_op jit(solution)/shard_map/all_to_all | solution.py:294
  17.8 1.1 %shard_map.201 = f32[8,4,1152]{2,1,0:T(4,128)S(1)} custom-call(f32[8,4,1152]{2,1,0:T(4,128)S(1)} %all-to-all-done.refs_0_, f32[64,192]{1,0:T(8,128)S(1)} %collective-permute-done.refs_1_, f32[160,216]{1,0:T(8,128)S(1)} %get-tuple-element.13.refs_2_, f32[32,128]{1,0:T(8,128)S(1)} %get-tuple-element.14.refs_3_, ...), custom_call_target="tpu_custom_call" | custom-call | bytes 1604608 | tf_op jit(solution)/shard_map/pallas_call | solution.py:281
  18.8 10.0 %all_to_all.10.refs_0_ = f32[8,4,1152]{2,1,0:T(4,128)S(1)} all-to-all(f32[8,4,1152]{2,1,0:T(4,128)S(1)} %shard_map.201), channel_id=1, replica_groups={{0,4,8,12,28,24,20,16},{1,5,9,13,29,25,21,17},{2,6,10,14,30,26,22,18},{..., dimensions={0} | all-to-all | bytes 294912 | tf_op jit(solution)/shard_map/all_to_all | solution.py:294
  28.9 0.9 %shard_map.202 = f32[32,1080]{1,0:T(8,128)} custom-call(f32[8,4,1152]{2,1,0:T(4,128)S(1)} %all_to_all.10.refs_0_), custom_call_target="tpu_custom_call" | custom-call | bytes 285696 | tf_op jit(solution)/shard_map/pallas_call | solution.py:281
Async XLA Ops:
  2.8 14.9 %all-to-all-start = ((f32[8,4,1152]{2,1,0:T(4,128)}), f32[8,4,1152]{2,1,0:T(4,128)S(1)}, u32[]{:S(2)}, u32[]{:S(2)}) async-start(f32[8,4,1152]{2,1,0:T(4,128)} %get-tuple-element.11), calls=%async_computation | async-start | bytes 294912 | tf_op jit(solution)/shard_map/all_to_all | solution.py:294
  10.1 3.7 %collective-permute-start = (f32[64,192]{1,0:T(8,128)S(1)}, f32[64,192]{1,0:T(8,128)S(1)}, u32[]{:S(2)}, u32[]{:S(2)}) collective-permute-start(f32[64,192]{1,0:T(8,128)S(1)} %get-tuple-element.12), channel_id=1, source_target_pairs={{3,0},{0,1},{1,2},{2,3},{7,4},{4,5},{5,6},{6,7},{11,8},{8,9},{9,10... | collective-permute-start | bytes 147464 | tf_op jit(solution)/shard_map/ppermute | solution.py:300

commit v16 on v14

--- a/solution.py
+++ b/solution.py
@@ -17,7 +17,7 @@
 FACES = 6
 ORDERS = (2, 3, 4, 5, 6)
 TRACE = VARS * FACE
-TRACE_PAD = 256
+SUB_STEP = 64
 FLAT = 36
 SENT = VARS * FLAT
 STEP = 192
@@ -55,11 +55,10 @@
     top_nodes = grid_nodes(6)
     mortar = [lagrange_rows(6, (top_nodes - 1.0) / 2.0), lagrange_rows(6, (top_nodes + 1.0) / 2.0)]
     flat = lagrange_rows(5, top_nodes)
-    lift = np.zeros((5, TRACE_PAD, STEP))
+    lift = np.zeros((SUB_STEP, 6 * SUB_STEP))
     for sub in range(5):
         both = (mortar[sub // 2] @ flat, mortar[sub % 2] @ flat) if sub < 4 else (flat, flat)
-        for v in range(VARS):
-            lift[sub, v * FACE : (v + 1) * FACE, v * FLAT : (v + 1) * FLAT] = np.kron(*both)
+        lift[:FACE, sub * SUB_STEP : sub * SUB_STEP + FLAT] = np.kron(*both)
     cell = np.zeros((len(ORDERS), CELL_PAD, ROW))
     face = np.zeros((len(ORDERS), FACES_PAD, ROW))
     for index, p in enumerate(ORDERS):
@@ -74,8 +73,7 @@
                 first = (2 * axis + side) * FACE_PAD
                 face[index, first : first + FLAT] = np.einsum(spec, edge, lower, lower).reshape(FLAT, ROW)
     return (
-        split_table(lift[:2].reshape(-1, STEP)) + split_table(lift[2:4].reshape(-1, STEP)),
-        split_table(lift[4]),
+        np.concatenate(split_table(lift)),
         split_table(cell.reshape(-1, ROW)),
         split_table(face.reshape(-1, ROW)),
     )
@@ -136,6 +134,17 @@
 
 def pad_lanes(x, lanes):
     return jnp.concatenate([x, jnp.zeros((x.shape[0], lanes - x.shape[1]), x.dtype)], axis=1)
+
+
+def stacked(trace):
+    wide = pad_lanes(trace, TRACE - FACE + SUB_STEP)
+    return jnp.concatenate([wide[:, v * FACE : v * FACE + SUB_STEP] for v in range(VARS)], axis=0)
+
+
+def side_by_side(products):
+    count = products.shape[0] // VARS
+    parts = [products[v * count : (v + 1) * count, :FLAT] for v in range(VARS)]
+    return jnp.concatenate([*parts, jnp.zeros((count, STEP - SENT), jnp.float32)], axis=1)
 
 
 def pack_kernel(peers, cap, row_cap, elements, get, out, conf_out, message, sent):
@@ -150,14 +159,16 @@
     put = onehot_rows(place, groups * slots)
     eye = (iota((count, count), 0) == iota((count, count), 1)).astype(jnp.float32)
     sub_col = column(eye, sub.astype(jnp.float32))
-    high, low = halves(pad_lanes(get(2), TRACE_PAD))
-    masks = [(sub_col == float(s)).astype(jnp.bfloat16) for s in range(4)]
-    lifted = jnp.zeros((count, STEP), jnp.float32)
-    for first in (0, 2):
-        wide = [jnp.concatenate([half * mask for mask in masks[first : first + 2]], axis=1) for half in (high, low)]
-        lifted = lifted + dot3(*wide, get(3 + first), get(4 + first))
+    subs = jnp.concatenate([sub_col] * VARS, axis=0)
+    tables = get(3)
+    table_high, table_low = tables[:SUB_STEP], tables[SUB_STEP:]
+    split = 4 * SUB_STEP
+    lifts = dot3(*halves(stacked(get(2))), table_high[:, :split], table_low[:, :split])
+    lifts = jnp.where(subs < 2.0, lifts[:, : 2 * SUB_STEP], lifts[:, 2 * SUB_STEP :])
+    odd = (subs == 1.0) | (subs == 3.0)
+    lifted = side_by_side(jnp.where(odd, lifts[:, SUB_STEP:], lifts[:, :SUB_STEP]))
     lifted_high, lifted_low = halves(lifted)
-    code_col = column(put, (get(8) * elements + get(7) + 1).astype(jnp.float32))
+    code_col = column(put, (get(5) * elements + get(4) + 1).astype(jnp.float32))
     put = put.astype(jnp.bfloat16)
     packed = dot(put, lifted_high) + dot(put, lifted_low)
     packed = jnp.where(iota(packed.shape, 1) == TAG_FACE, code_col, packed)
@@ -172,11 +183,11 @@
         send = pltpu.make_async_copy(message.at[:, :, lanes], out.at[:, :, lanes], sent.at[half])
         send.start()
         sends.append(send)
-    cface, celem = get(9), get(10)
+    cface, celem = get(6), get(7)
     confs = cface.shape[1]
     eye = (iota((confs, confs), 0) == iota((confs, confs), 1)).astype(jnp.float32)
     conf_col = column(eye, (cface * elements + celem + 1).astype(jnp.float32))
-    conf = dot3(*halves(pad_lanes(get(11), TRACE_PAD)), get(12), get(13))
+    conf = side_by_side(dot3(*halves(stacked(get(8))), table_high[:, split:], table_low[:, split:]))
     conf_out[...] = jnp.where(iota(conf.shape, 1) == TAG_FACE, conf_col, conf)
     for send in sends:
         send.wait()
@@ -318,7 +329,7 @@
     slots = peers * row_cap
     groups = -(-cap // row_cap)
     lanes = groups * STEP
-    lift, conf_lift, cell, face = [tuple(jnp.asarray(t) for t in pair) for pair in basis_tables()]
+    lift, cell, face = jax.tree.map(jnp.asarray, basis_tables())
     f32 = jnp.float32
     line = lambda a: a.reshape(1, -1)
     order, coarse_row = line(order), line(coarse_row)
@@ -330,13 +341,12 @@
             line(mortar_dest),
             line(mortar_sub),
             mortar_trace,
-            *lift,
+            lift,
             line(mortar_elem),
             line(mortar_face),
             line(conf_face),
             line(conf_elem),
             conf_trace,
-            *conf_lift,
         ),
         scratch=[pltpu.VMEM(message, f32), pltpu.SemaphoreType.DMA((2,))],
     )

time: 29.7 us -> 29.6 us (level)
  no operation moved by 1% of the time
where the time goes in v16:
time: 29.6 us; the launch traced here: 29.3 us
  blocking collectives  9.85 us (33%)
  starting transfers between devices  7.3 us (25%)
  Pallas kernels  7.05 us (24%)
  waiting for transfers between devices  5.05 us (17%)
    all_to_all x1, blocking collectives, exchange(): lax.all_to_all(block, ('gy', 'gx'), split_axis=0, concat_axis=0, tiled=True)  9.85 us
    all_to_all x1, starting transfers between devices, exchange(): lax.all_to_all(block, ('gy', 'gx'), split_axis=0, concat_axis=0, tiled=True)  7.29 us
    pallas_call x4, Pallas kernels, call(): pl.pallas_call(functools.partial(fetched, kernel, len(far), len(hand_on),...  7.05 us
    all_to_all x1, waiting for transfers between devices, exchange(): lax.all_to_all(block, ('gy', 'gx'), split_axis=0, concat_axis=0, tiled=True)  3.76 us
    ppermute x1, waiting for transfers between devices, from_behind(): return lax.ppermute(block, axis, route)  1.29 us
  transfers between devices with their start and end apart: 2, of which 2 were waited for; matrix products, arithmetic and copies ran while one was open for 0% of the time, Pallas kernels for 8%

profile of v16, /device:TPU:0, one launch (start us, length us, event | category | flops | bytes accessed | tf_op | source)
XLA Modules:
  0.0 29.3 jit_solution(8511224290302901044)
XLA Ops:
  0.0 2.7 %shard_map.154 = (f32[8,4,1152]{2,1,0:T(4,128)}, f32[64,192]{1,0:T(8,128)S(1)}) custom-call(s32[1,96]{1,0:T(1,128)} %bitcast.8, s32[1,96]{1,0:T(1,128)} %bitcast.9, f32[96,245]{1,0:T(8,128)} %refs_2_.2, bf16[128,384]{1,0:T(8,128)(2,1)} %constant.10.clone.refs_3_, s32[1,96]{1,0:T(1,128)} %bitcast.10, s32[1,96]{1,0:T(1,128)} %bitcast.11, s32[1,64]{1,0:T(1,128)} %bitcast.12, ...), custom_call_target="tpu_custom_call" | custom-call | bytes 453760 | tf_op jit(solution)/shard_map/pallas_call | solution.py:289
  2.7 7.3 %all-to-all-start = ((f32[8,4,1152]{2,1,0:T(4,128)}), f32[8,4,1152]{2,1,0:T(4,128)S(1)}, u32[]{:S(2)}, u32[]{:S(2)}) async-start(f32[8,4,1152]{2,1,0:T(4,128)} %get-tuple-element.11), calls=%async_computation | async-start | bytes 294912 | tf_op jit(solution)/shard_map/all_to_all | solution.py:301
  10.0 0.0 collective-permute-start
  10.0 2.4 %shard_map.155 = (f32[160,216]{1,0:T(8,128)S(1)}, f32[32,128]{1,0:T(8,128)S(1)}, bf16[1280,216]{1,0:T(8,128)(2,1)S(1)}, bf16[1280,216]{1,0:T(8,128)(2,1)S(1)}) custom-call(s32[1,32]{1,0:T(1,128)} %bitcast.14, s32[1,32]{1,0:T(1,128)} %bitcast.15, f32[32,1715]{1,0:T(8,128)} %refs_2_.3, bf16[1920,216]{1,0:T(8,128)(2,1)} %constant.11.clone.refs_3_, ...), custom_call_target="tpu_custom_call" | custom-call | bytes 3139200 | tf_op jit(solution)/shard_map/pallas_call | solution.py:289
  12.4 1.3 %collective-permute-done.refs_1_ = f32[64,192]{1,0:T(8,128)S(1)} collective-permute-done((f32[64,192]{1,0:T(8,128)S(1)}, f32[64,192]{1,0:T(8,128)S(1)}, u32[]{:S(2)}, u32[]{:S(2)}) %collective-permute-start) | collective-permute-done | bytes 49184 | tf_op jit(solution)/shard_map/ppermute | solution.py:307
  13.7 3.8 %all-to-all-done.refs_0_ = f32[8,4,1152]{2,1,0:T(4,128)S(1)} async-done(((f32[8,4,1152]{2,1,0:T(4,128)}), f32[8,4,1152]{2,1,0:T(4,128)S(1)}, u32[]{:S(2)}, u32[]{:S(2)}) %all-to-all-start) | async-done | bytes 147488 | tf_op jit(solution)/shard_map/all_to_all | solution.py:301
  17.4 1.1 %shard_map.156 = f32[8,4,1152]{2,1,0:T(4,128)S(1)} custom-call(f32[8,4,1152]{2,1,0:T(4,128)S(1)} %all-to-all-done.refs_0_, f32[64,192]{1,0:T(8,128)S(1)} %collective-permute-done.refs_1_, f32[160,216]{1,0:T(8,128)S(1)} %get-tuple-element.13.refs_2_, f32[32,128]{1,0:T(8,128)S(1)} %get-tuple-element.14.refs_3_, ...), custom_call_target="tpu_custom_call" | custom-call | bytes 1604608 | tf_op jit(solution)/shard_map/pallas_call | solution.py:289
  18.5 9.8 %all_to_all.10.refs_0_ = f32[8,4,1152]{2,1,0:T(4,128)S(1)} all-to-all(f32[8,4,1152]{2,1,0:T(4,128)S(1)} %shard_map.156), channel_id=1, replica_groups=mesh['gx'=2,'gy'=4,'gz'=4] {'gy','gx'}, dimensions={0} | all-to-all | bytes 294912 | tf_op jit(solution)/shard_map/all_to_all | solution.py:301
  28.4 0.9 %shard_map.157 = f32[32,1080]{1,0:T(8,128)} custom-call(f32[8,4,1152]{2,1,0:T(4,128)S(1)} %all_to_all.10.refs_0_), custom_call_target="tpu_custom_call" | custom-call | bytes 285696 | tf_op jit(solution)/shard_map/pallas_call | solution.py:289
Async XLA Ops:
  2.7 14.7 %all-to-all-start = ((f32[8,4,1152]{2,1,0:T(4,128)}), f32[8,4,1152]{2,1,0:T(4,128)S(1)}, u32[]{:S(2)}, u32[]{:S(2)}) async-start(f32[8,4,1152]{2,1,0:T(4,128)} %get-tuple-element.11), calls=%async_computation | async-start | bytes 294912 | tf_op jit(solution)/shard_map/all_to_all | solution.py:301
  10.0 3.7 %collective-permute-start = (f32[64,192]{1,0:T(8,128)S(1)}, f32[64,192]{1,0:T(8,128)S(1)}, u32[]{:S(2)}, u32[]{:S(2)}) collective-permute-start(f32[64,192]{1,0:T(8,128)S(1)} %get-tuple-element.12), channel_id=1, source_target_pairs={{3,0},{0,1},{1,2},{2,3},{7,4},{4,5},{5,6},{6,7},{11,8},{8,9},{9,10... | collective-permute-start | bytes 147464 | tf_op jit(solution)/shard_map/ppermute | solution.py:307

commit v17 on v16

--- a/solution.py
+++ b/solution.py
@@ -24,6 +24,7 @@
 TAG_FACE = SENT
 ROWS_PAD = 1152
 TAG_SLOT = VARS * ROW
+PLACE_SPLIT = 512
 CELL_PAD = 384
 FACE_PAD = 40
 FACES_PAD = 256
@@ -193,7 +194,7 @@
         send.wait()
 
 
-def cell_kernel(peers, row_cap, get, y_out, col_out, spread):
+def cell_kernel(peers, row_cap, get, conf, y_out, col_out, conf_out, spread):
     order, crow = get(0), get(1)
     elements = order.shape[1]
     slots = peers * row_cap
@@ -214,6 +215,7 @@
     high, low = spread[0], spread[1]
     wide_high = jnp.concatenate([jnp.where(order_rows == float(p), high, 0.0).astype(jnp.bfloat16) for p in ORDERS], axis=1)
     wide_low = jnp.concatenate([jnp.where(order_rows == float(p), low, 0.0).astype(jnp.bfloat16) for p in ORDERS], axis=1)
+    conf_out[...] = conf[...]
     y_out[...] = dot3(wide_high, wide_low, get(3), get(4))
 
 
@@ -245,15 +247,23 @@
     out[:, :, TAG_SLOT : TAG_SLOT + 1] = cols[:, 2:3].reshape(peers, row_cap, 1)
 
 
-def place_kernel(peers, row_cap, get, arrived, out):
+def place_kernel(peers, row_cap, get, arrived, out, placed, sent):
     elements = out.shape[0]
     rows = peers * row_cap
     message = arrived[...].reshape(rows, arrived.shape[2])
-    x, slot_col = message[:, :TAG_SLOT], message[:, TAG_SLOT : TAG_SLOT + 1]
+    slot_col = message[:, TAG_SLOT : TAG_SLOT + 1]
     slot_row = jnp.sum(jnp.where(iota((rows, rows), 0) == iota((rows, rows), 1), slot_col, 0.0), axis=0, keepdims=True)
     put = (iota((elements, rows), 0).astype(jnp.float32) + 1.0 == slot_row).astype(jnp.bfloat16)
-    high, low = halves(x)
-    out[...] = dot(put, high) + dot(put, low)
+    sends = []
+    for half, (first, last) in enumerate(((0, PLACE_SPLIT), (PLACE_SPLIT, TAG_SLOT))):
+        high, low = halves(message[:, first:last])
+        placed[:, first:last] = dot(put, high) + dot(put, low)
+        lanes = pl.ds(first, last - first)
+        send = pltpu.make_async_copy(placed.at[:, lanes], out.at[:, lanes], sent.at[half])
+        send.start()
+        sends.append(send)
+    for send in sends:
+        send.wait()
 
 
 def fetched(kernel, n_far, n_pass, n_near, n_out, *refs):
@@ -351,14 +361,19 @@
         scratch=[pltpu.VMEM(message, f32), pltpu.SemaphoreType.DMA((2,))],
     )
     incoming = exchange(outgoing)
-    conf = from_behind(conf, "gz", 1)
-    y, cols, *face = call(
+    y, cols, conf, *face = call(
         functools.partial(cell_kernel, peers, row_cap),
-        [jax.ShapeDtypeStruct((VARS * slots, ROW), f32), jax.ShapeDtypeStruct((slots, 128), f32)],
+        [
+            jax.ShapeDtypeStruct((VARS * slots, ROW), f32),
+            jax.ShapeDtypeStruct((slots, 128), f32),
+            jax.ShapeDtypeStruct(conf.shape, f32),
+        ],
         (order, coarse_row, adjoint, *cell),
+        (conf,),
         scratch=[pltpu.VMEM((2, VARS * slots, CELL_PAD), f32)],
         hand_on=face,
     )
+    conf = from_behind(conf, "gz", 1)
     (rows,) = call(
         functools.partial(face_kernel, peers, row_cap, elements, groups),
         [jax.ShapeDtypeStruct((peers, row_cap, ROWS_PAD), f32)],
@@ -368,9 +383,10 @@
     )
     (out,) = call(
         functools.partial(place_kernel, peers, row_cap),
-        [jax.ShapeDtypeStruct((elements, VARS * ROW), f32)],
+        [pltpu.HBM((elements, VARS * ROW), f32)],
         (),
         (exchange(rows),),
+        scratch=[pltpu.VMEM((elements, VARS * ROW), f32), pltpu.SemaphoreType.DMA((2,))],
     )
     return out
 

time: 29.6 us -> 31.6 us (1.068)
  blocking collectives: 9.85 us -> 11.9 us
    all_to_all x1, waiting for transfers between devices: 3.76 us -> 1.33 us  [exchange(): lax.all_to_all(block, ('gy', 'gx'), split_axis=0, concat_axis=0, tiled=True)]
    ppermute x1, waiting for transfers between devices: 1.29 us -> 3.68 us  [from_behind(): return lax.ppermute(block, axis, route)]
    all_to_all x1, blocking collectives: 9.85 us -> 11.9 us  [exchange(): lax.all_to_all(block, ('gy', 'gx'), split_axis=0, concat_axis=0, tiled=True)]
where the time goes in v17:
time: 31.6 us; the launch traced here: 31.4 us
  blocking collectives  11.9 us (38%)
  starting transfers between devices  7.35 us (23%)
  Pallas kernels  7.04 us (22%)
  waiting for transfers between devices  5 us (16%)
    all_to_all x1, blocking collectives, exchange(): lax.all_to_all(block, ('gy', 'gx'), split_axis=0, concat_axis=0, tiled=True)  11.9 us
    all_to_all x1, starting transfers between devices, exchange(): lax.all_to_all(block, ('gy', 'gx'), split_axis=0, concat_axis=0, tiled=True)  7.29 us
    pallas_call x4, Pallas kernels, call(): pl.pallas_call(functools.partial(fetched, kernel, len(far), len(hand_on),...  7.04 us
    ppermute x1, waiting for transfers between devices, from_behind(): return lax.ppermute(block, axis, route)  3.68 us
    all_to_all x1, waiting for transfers between devices, exchange(): lax.all_to_all(block, ('gy', 'gx'), split_axis=0, concat_axis=0, tiled=True)  1.33 us
  transfers between devices with their start and end apart: 2, of which 2 were waited for; matrix products, arithmetic and copies ran while one was open for 0% of the time, Pallas kernels for 8%

profile of v17, /device:TPU:0, one launch (start us, length us, event | category | flops | bytes accessed | tf_op | source)
XLA Modules:
  0.0 31.4 jit_solution(2310655704097942742)
XLA Ops:
  0.0 2.7 %shard_map.154 = (f32[8,4,1152]{2,1,0:T(4,128)}, f32[64,192]{1,0:T(8,128)S(1)}) custom-call(s32[1,96]{1,0:T(1,128)} %bitcast.8, s32[1,96]{1,0:T(1,128)} %bitcast.9, f32[96,245]{1,0:T(8,128)} %refs_2_.2, bf16[128,384]{1,0:T(8,128)(2,1)} %constant.10.clone.refs_3_, s32[1,96]{1,0:T(1,128)} %bitcast.10, s32[1,96]{1,0:T(1,128)} %bitcast.11, s32[1,64]{1,0:T(1,128)} %bitcast.12, ...), custom_call_target="tpu_custom_call" | custom-call | bytes 453760 | tf_op jit(solution)/shard_map/pallas_call | solution.py:299
  2.7 7.3 %all-to-all-start = ((f32[8,4,1152]{2,1,0:T(4,128)}), f32[8,4,1152]{2,1,0:T(4,128)S(1)}, u32[]{:S(2)}, u32[]{:S(2)}) async-start(f32[8,4,1152]{2,1,0:T(4,128)} %get-tuple-element.12), calls=%async_computation | async-start | bytes 294912 | tf_op jit(solution)/shard_map/all_to_all | solution.py:311
  10.0 2.4 %shard_map.155 = (f32[160,216]{1,0:T(8,128)S(1)}, f32[32,128]{1,0:T(8,128)S(1)}, f32[64,192]{1,0:T(8,128)S(1)}, bf16[1280,216]{1,0:T(8,128)(2,1)S(1)}, bf16[1280,216]{1,0:T(8,128)(2,1)S(1)}) custom-call(s32[1,32]{1,0:T(1,128)} %bitcast.14, s32[1,32]{1,0:T(1,128)} %bitcast.15, f32[32,1715]{1,0:T(8,128)} %refs_2_.3, bf16[1920,216]{1,0:T(8,128)(2,1)} %constant.11.clone.refs_3_, ...), custom_call_target="tpu_custom_call" | custom-call | bytes 3237504 | tf_op jit(solution)/shard_map/pallas_call | solution.py:299
  12.4 0.1 collective-permute-start
  12.4 3.7 %collective-permute-done.refs_1_ = f32[64,192]{1,0:T(8,128)S(1)} collective-permute-done((f32[64,192]{1,0:T(8,128)S(1)}, f32[64,192]{1,0:T(8,128)S(1)}, u32[]{:S(2)}, u32[]{:S(2)}) %collective-permute-start) | collective-permute-done | bytes 49184 | tf_op jit(solution)/shard_map/ppermute | solution.py:317
  16.1 1.3 %all-to-all-done.refs_0_ = f32[8,4,1152]{2,1,0:T(4,128)S(1)} async-done(((f32[8,4,1152]{2,1,0:T(4,128)}), f32[8,4,1152]{2,1,0:T(4,128)S(1)}, u32[]{:S(2)}, u32[]{:S(2)}) %all-to-all-start) | async-done | bytes 147488 | tf_op jit(solution)/shard_map/all_to_all | solution.py:311
  17.4 1.1 %shard_map.156 = f32[8,4,1152]{2,1,0:T(4,128)S(1)} custom-call(f32[8,4,1152]{2,1,0:T(4,128)S(1)} %all-to-all-done.refs_0_, f32[64,192]{1,0:T(8,128)S(1)} %collective-permute-done.refs_1_, f32[160,216]{1,0:T(8,128)S(1)} %get-tuple-element.15.refs_2_, f32[32,128]{1,0:T(8,128)S(1)} %get-tuple-element.16.refs_3_, ...), custom_call_target="tpu_custom_call" | custom-call | bytes 1604608 | tf_op jit(solution)/shard_map/pallas_call | solution.py:299
  18.5 11.9 %all_to_all.10.refs_0_ = f32[8,4,1152]{2,1,0:T(4,128)S(1)} all-to-all(f32[8,4,1152]{2,1,0:T(4,128)S(1)} %shard_map.156), channel_id=1, replica_groups=mesh['gx'=2,'gy'=4,'gz'=4] {'gy','gx'}, dimensions={0} | all-to-all | bytes 294912 | tf_op jit(solution)/shard_map/all_to_all | solution.py:311
  30.4 0.9 %shard_map.157 = f32[32,1080]{1,0:T(8,128)} custom-call(f32[8,4,1152]{2,1,0:T(4,128)S(1)} %all_to_all.10.refs_0_), custom_call_target="tpu_custom_call" | custom-call | bytes 285696 | tf_op jit(solution)/shard_map/pallas_call | solution.py:299
Async XLA Ops:
  2.7 14.7 %all-to-all-start = ((f32[8,4,1152]{2,1,0:T(4,128)}), f32[8,4,1152]{2,1,0:T(4,128)S(1)}, u32[]{:S(2)}, u32[]{:S(2)}) async-start(f32[8,4,1152]{2,1,0:T(4,128)} %get-tuple-element.12), calls=%async_computation | async-start | bytes 294912 | tf_op jit(solution)/shard_map/all_to_all | solution.py:311
  12.4 3.7 %collective-permute-start = (f32[64,192]{1,0:T(8,128)S(1)}, f32[64,192]{1,0:T(8,128)S(1)}, u32[]{:S(2)}, u32[]{:S(2)}) collective-permute-start(f32[64,192]{1,0:T(8,128)S(1)} %get-tuple-element.14), channel_id=1, source_target_pairs={{3,0},{0,1},{1,2},{2,3},{7,4},{4,5},{5,6},{6,7},{11,8},{8,9},{9,10... | collective-permute-start | bytes 147464 | tf_op jit(solution)/shard_map/ppermute | solution.py:317

commit v18 on v16

--- a/solution.py
+++ b/solution.py
@@ -147,7 +147,23 @@
     return jnp.concatenate([*parts, jnp.zeros((count, STEP - SENT), jnp.float32)], axis=1)
 
 
-def pack_kernel(peers, cap, row_cap, elements, get, out, conf_out, message, sent):
+def restrict_cells(take, order_col, adjoint, table_high, table_low, spread):
+    slots = take.shape[0]
+    take = take.astype(jnp.bfloat16)
+    spread[...] = jnp.zeros_like(spread)
+    for half, part in enumerate(halves(adjoint)):
+        moved = dot(take, part)
+        for v in range(VARS):
+            spread[half, v * slots : (v + 1) * slots, :CELL] = moved[:, v * CELL : (v + 1) * CELL]
+    order_rows = jnp.concatenate([order_col] * VARS, axis=0)
+    wide = [
+        jnp.concatenate([jnp.where(order_rows == float(p), spread[half], 0.0).astype(jnp.bfloat16) for p in ORDERS], axis=1)
+        for half in range(2)
+    ]
+    return dot3(*wide, table_high, table_low)
+
+
+def pack_kernel(peers, cap, row_cap, elements, get, out, conf_out, y_out, message, sent, spread):
     dest, sub = get(0), get(1)
     count = dest.shape[1]
     groups, slots = -(-cap // row_cap), peers * row_cap
@@ -189,11 +205,19 @@
     conf_col = column(eye, (cface * elements + celem + 1).astype(jnp.float32))
     conf = side_by_side(dot3(*halves(stacked(get(8))), table_high[:, split:], table_low[:, split:]))
     conf_out[...] = jnp.where(iota(conf.shape, 1) == TAG_FACE, conf_col, conf)
+    order, crow, adjoint, table_high, table_low = [get(i) for i in range(9, 14)]
+
+    @pl.when(lax.axis_index("gz") % 2 == 0)
+    def _():
+        take = onehot_rows(row_places(crow, peers, elements, row_cap)[0], slots)
+        order_col = column(take, order.astype(jnp.float32))
+        y_out[...] = restrict_cells(take, order_col, adjoint, table_high, table_low, spread)
+
     for send in sends:
         send.wait()
 
 
-def cell_kernel(peers, row_cap, get, y_out, col_out, spread):
+def cell_kernel(peers, row_cap, get, y_early, y_out, col_out, spread):
     order, crow = get(0), get(1)
     elements = order.shape[1]
     slots = peers * row_cap
@@ -204,17 +228,16 @@
     lane = iota((slots, 128), 1)
     slot_col = column(take, slot + 1.0)
     col_out[...] = jnp.where(lane == 0, order_col, jnp.where(lane == 1, elem_col, slot_col))
-    take = take.astype(jnp.bfloat16)
-    spread[...] = jnp.zeros_like(spread)
-    for half, part in enumerate(halves(get(2))):
-        moved = dot(take, part)
-        for v in range(VARS):
-            spread[half, v * slots : (v + 1) * slots, :CELL] = moved[:, v * CELL : (v + 1) * CELL]
-    order_rows = jnp.concatenate([order_col] * VARS, axis=0)
-    high, low = spread[0], spread[1]
-    wide_high = jnp.concatenate([jnp.where(order_rows == float(p), high, 0.0).astype(jnp.bfloat16) for p in ORDERS], axis=1)
-    wide_low = jnp.concatenate([jnp.where(order_rows == float(p), low, 0.0).astype(jnp.bfloat16) for p in ORDERS], axis=1)
-    y_out[...] = dot3(wide_high, wide_low, get(3), get(4))
+    adjoint, table_high, table_low = get(2), get(3), get(4)
+    early = lax.axis_index("gz") % 2 == 0
+
+    @pl.when(early)
+    def _():
+        y_out[...] = y_early[...]
+
+    @pl.when(jnp.logical_not(early))
+    def _():
+        y_out[...] = restrict_cells(take, order_col, adjoint, table_high, table_low, spread)
 
 
 def face_kernel(peers, row_cap, elements, groups, get, incoming, conf, y, cols, table_high, table_low, out, spread):
@@ -334,9 +357,13 @@
     line = lambda a: a.reshape(1, -1)
     order, coarse_row = line(order), line(coarse_row)
     message = (peers, row_cap, lanes)
-    outgoing, conf = call(
+    outgoing, conf, y = call(
         functools.partial(pack_kernel, peers, cap, row_cap, elements),
-        [pltpu.HBM(message, f32), jax.ShapeDtypeStruct((confs, STEP), f32)],
+        [
+            pltpu.HBM(message, f32),
+            jax.ShapeDtypeStruct((confs, STEP), f32),
+            jax.ShapeDtypeStruct((VARS * slots, ROW), f32),
+        ],
         (
             line(mortar_dest),
             line(mortar_sub),
@@ -347,8 +374,16 @@
             line(conf_face),
             line(conf_elem),
             conf_trace,
+            order,
+            coarse_row,
+            adjoint,
+            *cell,
         ),
-        scratch=[pltpu.VMEM(message, f32), pltpu.SemaphoreType.DMA((2,))],
+        scratch=[
+            pltpu.VMEM(message, f32),
+            pltpu.SemaphoreType.DMA((2,)),
+            pltpu.VMEM((2, VARS * slots, CELL_PAD), f32),
+        ],
     )
     incoming = exchange(outgoing)
     conf = from_behind(conf, "gz", 1)
@@ -356,6 +391,7 @@
         functools.partial(cell_kernel, peers, row_cap),
         [jax.ShapeDtypeStruct((VARS * slots, ROW), f32), jax.ShapeDtypeStruct((slots, 128), f32)],
         (order, coarse_row, adjoint, *cell),
+        (y,),
         scratch=[pltpu.VMEM((2, VARS * slots, CELL_PAD), f32)],
         hand_on=face,
     )

time: 29.6 us -> 30.8 us (1.041)
  Pallas kernels: 7.05 us -> 7.81 us
    pallas_call x4, Pallas kernels: 7.05 us -> 7.81 us  [call(): pl.pallas_call(functools.partial(fetched, kernel, len(far), len(hand_on),...]
  transfers between devices with their start and end apart: 2 -> 2, of which waited for: 2 -> 2; matrix products, arithmetic and copies ran while one was open for 0% -> 0% of each run, Pallas kernels for 8% -> 7%
where the time goes in v18:
time: 30.8 us; the launch traced here: 30.6 us
  blocking collectives  10.1 us (33%)
  Pallas kernels  7.81 us (25%)
  starting transfers between devices  7.3 us (24%)
  waiting for transfers between devices  5.34 us (17%)
    all_to_all x1, blocking collectives, exchange(): lax.all_to_all(block, ('gy', 'gx'), split_axis=0, concat_axis=0, tiled=True)  10.1 us
    pallas_call x4, Pallas kernels, call(): pl.pallas_call(functools.partial(fetched, kernel, len(far), len(hand_on),...  7.81 us
    all_to_all x1, starting transfers between devices, exchange(): lax.all_to_all(block, ('gy', 'gx'), split_axis=0, concat_axis=0, tiled=True)  7.29 us
    all_to_all x1, waiting for transfers between devices, exchange(): lax.all_to_all(block, ('gy', 'gx'), split_axis=0, concat_axis=0, tiled=True)  3.76 us
    ppermute x1, waiting for transfers between devices, from_behind(): return lax.ppermute(block, axis, route)  1.58 us
  transfers between devices with their start and end apart: 2, of which 2 were waited for; matrix products, arithmetic and copies ran while one was open for 0% of the time, Pallas kernels for 7%

profile of v18, /device:TPU:0, one launch (start us, length us, event | category | flops | bytes accessed | tf_op | source)
XLA Modules:
  0.0 30.6 jit_solution(10149021956543771945)
XLA Ops:
  0.0 3.7 %shard_map.154 = (f32[8,4,1152]{2,1,0:T(4,128)}, f32[64,192]{1,0:T(8,128)S(1)}, f32[160,216]{1,0:T(8,128)S(1)}) custom-call(s32[1,96]{1,0:T(1,128)} %bitcast.12, s32[1,96]{1,0:T(1,128)} %bitcast.13, f32[96,245]{1,0:T(8,128)} %refs_2_.2, bf16[128,384]{1,0:T(8,128)(2,1)} %constant.10.clone.refs_3_, s32[1,96]{1,0:T(1,128)} %bitcast.14, s32[1,96]{1,0:T(1,128)} %bitcast.15, ...), custom_call_target="tpu_custom_call" | custom-call | bytes 2470656 | tf_op jit(solution)/shard_map/pallas_call | solution.py:312
  3.7 7.3 %all-to-all-start = ((f32[8,4,1152]{2,1,0:T(4,128)}), f32[8,4,1152]{2,1,0:T(4,128)S(1)}, u32[]{:S(2)}, u32[]{:S(2)}) async-start(f32[8,4,1152]{2,1,0:T(4,128)} %get-tuple-element.12), calls=%async_computation | async-start | bytes 294912 | tf_op jit(solution)/shard_map/all_to_all | solution.py:324
  11.0 0.0 collective-permute-start
  11.0 2.1 %shard_map.155 = (f32[160,216]{1,0:T(8,128)S(1)}, f32[32,128]{1,0:T(8,128)S(1)}, bf16[1280,216]{1,0:T(8,128)(2,1)S(1)}, bf16[1280,216]{1,0:T(8,128)(2,1)S(1)}) custom-call(s32[1,32]{1,0:T(1,128)} %bitcast.9, s32[1,32]{1,0:T(1,128)} %bitcast.11, f32[32,1715]{1,0:T(8,128)} %refs_2_.3, bf16[1920,216]{1,0:T(8,128)(2,1)} %constant.11.clone.refs_12_.refs_3_, ...), custom_call_target="tpu_custom_call" | custom-call | bytes 3277440 | tf_op jit(solution)/shard_map/pallas_call | solution.py:312
  13.1 1.6 %collective-permute-done.refs_1_ = f32[64,192]{1,0:T(8,128)S(1)} collective-permute-done((f32[64,192]{1,0:T(8,128)S(1)}, f32[64,192]{1,0:T(8,128)S(1)}, u32[]{:S(2)}, u32[]{:S(2)}) %collective-permute-start) | collective-permute-done | bytes 49184 | tf_op jit(solution)/shard_map/ppermute | solution.py:330
  14.7 3.8 %all-to-all-done.refs_0_ = f32[8,4,1152]{2,1,0:T(4,128)S(1)} async-done(((f32[8,4,1152]{2,1,0:T(4,128)}), f32[8,4,1152]{2,1,0:T(4,128)S(1)}, u32[]{:S(2)}, u32[]{:S(2)}) %all-to-all-start) | async-done | bytes 147488 | tf_op jit(solution)/shard_map/all_to_all | solution.py:324
  18.5 1.1 %shard_map.156 = f32[8,4,1152]{2,1,0:T(4,128)S(1)} custom-call(f32[8,4,1152]{2,1,0:T(4,128)S(1)} %all-to-all-done.refs_0_, f32[64,192]{1,0:T(8,128)S(1)} %collective-permute-done.refs_1_, f32[160,216]{1,0:T(8,128)S(1)} %get-tuple-element.15.refs_2_, f32[32,128]{1,0:T(8,128)S(1)} %get-tuple-element.16.refs_3_, ...), custom_call_target="tpu_custom_call" | custom-call | bytes 1604608 | tf_op jit(solution)/shard_map/pallas_call | solution.py:312
  19.6 10.1 %all_to_all.10.refs_0_ = f32[8,4,1152]{2,1,0:T(4,128)S(1)} all-to-all(f32[8,4,1152]{2,1,0:T(4,128)S(1)} %shard_map.156), channel_id=1, replica_groups=mesh['gx'=2,'gy'=4,'gz'=4] {'gy','gx'}, dimensions={0} | all-to-all | bytes 294912 | tf_op jit(solution)/shard_map/all_to_all | solution.py:324
  29.6 0.9 %shard_map.157 = f32[32,1080]{1,0:T(8,128)} custom-call(f32[8,4,1152]{2,1,0:T(4,128)S(1)} %all_to_all.10.refs_0_), custom_call_target="tpu_custom_call" | custom-call | bytes 285696 | tf_op jit(solution)/shard_map/pallas_call | solution.py:312
Async XLA Ops:
  3.7 14.7 %all-to-all-start = ((f32[8,4,1152]{2,1,0:T(4,128)}), f32[8,4,1152]{2,1,0:T(4,128)S(1)}, u32[]{:S(2)}, u32[]{:S(2)}) async-start(f32[8,4,1152]{2,1,0:T(4,128)} %get-tuple-element.12), calls=%async_computation | async-start | bytes 294912 | tf_op jit(solution)/shard_map/all_to_all | solution.py:324
  11.0 3.7 %collective-permute-start = (f32[64,192]{1,0:T(8,128)S(1)}, f32[64,192]{1,0:T(8,128)S(1)}, u32[]{:S(2)}, u32[]{:S(2)}) collective-permute-start(f32[64,192]{1,0:T(8,128)S(1)} %get-tuple-element.13), channel_id=1, source_target_pairs={{3,0},{0,1},{1,2},{2,3},{7,4},{4,5},{5,6},{6,7},{11,8},{8,9},{9,10... | collective-permute-start | bytes 147464 | tf_op jit(solution)/shard_map/ppermute | solution.py:330
